TPU v7x, 128 devices: a whole 4x4x4 slice. The times are simulated.
128 devices in a mesh: tr: 8 (over z, core), tc: 16 (over x, y).
Axes of the slice: x: 4, y: 4, z: 4, core: 2. Of those that a mesh axis runs over, the one named last changes fastest.
Arguments:
- embeddings: bfloat16 [98304, 1024], P(('tr', 'tc')), may hold values from -100 to 100
- labels: int32 [98304], P(('tr', 'tc')), may hold values from 0 to 31, as said below
Outputs:
- best_sim: float32 [98304], P(('tr', 'tc'))
- weighted: float32 [98304], P(('tr', 'tc'))
- flag: float32 [98304], P(('tr', 'tc'))
Inputs may be any that keep to these rules, and one draw needn't show every extreme that they name: In each aligned block of 768 files (one corpus shard), at most 288 files have labels // 4 equal to any one value g, and every shard has exactly 288 for some g; for every g and every c below 16, the shards c, c + 16, c + 32, ... together hold exactly 768 files with labels // 4 = g; every label is held by two or more files.
All inputs are finite; a program needn't handle non-finite values.
Results may differ from a plain program's by a relative error of at most 0.0013.
Values may be sent and summed in bfloat16 or wider, within the bound.
No kernel may reach another device: no remote copies, remote signals or barrier semaphores. Data moves between devices by JAX's collectives and lax.ppermute only.
A program may use at most 128 MiB of HBM per device.

v0:
```python
import jax
import jax.numpy as jnp
from jax import lax
from jax.sharding import PartitionSpec as P

GROUP_CLUSTERS = 4


SCALE = 256.0
NEGATIVE = -1e30
EPSILON = 1e-06
THRESHOLD = 0.3
SHARPNESS = 50.0


def fresh_stats(count):
    return (
        jnp.full((count,), NEGATIVE, jnp.float32),
        jnp.zeros((count,), jnp.float32),
        jnp.zeros((count,), jnp.float32),
    )


def tile_update(stats, sims, mask):
    best, total, weight = stats
    scores = SCALE * sims
    block_top = jnp.max(jnp.where(mask, scores, NEGATIVE), axis=1)
    new_best = jnp.maximum(best, block_top)
    factor = jnp.exp(best - new_best)
    terms = jnp.where(mask, jnp.exp(scores - new_best[:, None]), 0.0)
    return (
        new_best,
        total * factor + jnp.sum(terms, axis=1),
        weight * factor + jnp.sum(terms * sims, axis=1),
    )


def pair_products(left, right):
    return lax.dot_general(
        left, right, (((1,), (1,)), ((), ())), preferred_element_type=jnp.float32
    )


def per_device(embeddings, labels):
    shard_rows, feature_dim = embeddings.shape
    tile_rows = lax.axis_size("tr")
    capacity = 3 * shard_rows // tile_rows
    values = embeddings.astype(jnp.float32)
    unit = (values * lax.rsqrt(jnp.sum(values * values, axis=1, keepdims=True) + EPSILON)).astype(
        jnp.bfloat16
    )
    owner = labels // GROUP_CLUSTERS
    onehot = (owner[:, None] == jnp.arange(tile_rows, dtype=jnp.int32)[None, :]).astype(jnp.int32)
    ranks = jnp.sum((jnp.cumsum(onehot, axis=0) - 1) * onehot, axis=1)
    slots = owner * capacity + ranks
    send_rows = jnp.zeros((tile_rows * capacity, feature_dim), jnp.bfloat16).at[slots].set(unit)
    send_labels = jnp.full((tile_rows * capacity,), -1, jnp.int32).at[slots].set(labels)
    got_rows, got_labels = (
        lax.all_to_all(
            send_rows.reshape(tile_rows, capacity, feature_dim),
            "tr",
            split_axis=0,
            concat_axis=0,
            tiled=True,
        ),
        lax.all_to_all(
            send_labels.reshape(tile_rows, capacity), "tr", split_axis=0, concat_axis=0, tiled=True
        ),
    )
    flat_rows = got_rows.reshape(tile_rows * capacity, feature_dim)
    flat_labels = got_labels.reshape(tile_rows * capacity)
    filled = flat_labels >= 0
    position = jnp.cumsum(filled.astype(jnp.int32)) - 1
    target = jnp.where(filled, position, shard_rows)
    queries = (
        jnp.zeros((shard_rows, feature_dim), jnp.bfloat16).at[target].set(flat_rows, mode="drop")
    )
    query_labels = jnp.zeros((shard_rows,), jnp.int32).at[target].set(flat_labels, mode="drop")
    local_range = jnp.arange(shard_rows, dtype=jnp.int32)
    query_index = lax.axis_index("tc") * shard_rows + local_range
    stats = fresh_stats(shard_rows)
    key_rows = lax.all_gather(queries, "tc", axis=0, tiled=True)
    key_labels = lax.all_gather(query_labels, "tc", axis=0, tiled=True)
    count = key_rows.shape[0] // shard_rows
    offsets = jnp.arange(count, dtype=jnp.int32) * shard_rows

    def step(inner, item):
        block_rows, block_labels, offset = item
        sims = pair_products(queries, block_rows)
        mask = (query_labels[:, None] == block_labels[None, :]) & (
            query_index[:, None] != offset + local_range[None, :]
        )
        return (tile_update(inner, sims, mask), None)

    stats, unused = lax.scan(
        step,
        stats,
        (
            key_rows.reshape(count, shard_rows, feature_dim),
            key_labels.reshape(count, shard_rows),
            offsets,
        ),
    )
    best_sim = stats[0] / SCALE
    weighted = stats[2] / stats[1]
    flag = jax.nn.sigmoid(SHARPNESS * (best_sim - THRESHOLD))
    results = jnp.stack([best_sim, weighted, flag])
    spread = jnp.where(filled[None, :], results[:, jnp.where(filled, position, 0)], 0.0)
    back = lax.all_to_all(
        spread.reshape(3, tile_rows, capacity), "tr", split_axis=1, concat_axis=1, tiled=True
    )
    mine = back.reshape(3, tile_rows * capacity)[:, slots]
    return (mine[0], mine[1], mine[2])


def solution(mesh):
    placed = (P(("tr", "tc"), None), P(("tr", "tc")))
    return jax.shard_map(
        per_device,
        mesh=mesh,
        in_specs=placed,
        out_specs=(P(("tr", "tc")), P(("tr", "tc")), P(("tr", "tc"))),
        check_vma=False,
    )
```

profile of v0, /device:TPU:2, one launch (start us, length us, event | category | flops | bytes accessed | tf_op | source)
XLA Modules:
  0.0 381.7 jit_solution(9128932523774820840)
XLA Ops:
  7.2 0.8 add_select_fusion
  8.0 1.7 reduce-window.15
  10.3 0.7 compare_select_fusion.2
  11.0 3.5 scatter_custom_fusion
  14.5 0.7 all_to_all.12
  15.2 5.3 %all-to-all-start = ((s32[8,1,288]{2,1,0:T(1,128)}), s32[8,1,288]{2,1,0:T(1,128)S(1)}, u32[]{:S(2)}, u32[]{:S(2)}) async-start(s32[8,1,288]{2,1,0:T(1,128)} %all_to_all.12), calls=%async_computation | async-start | bytes 24576 | tf_op jit(solution)/shard_map/all_to_all | solution.py:66
  20.5 1.8 fusion.12
  22.3 9.3 %scatter_custom_fusion.2 = bf16[2304,1024]{1,0:T(8,128)(2,1)} fusion(s32[768]{0:T(1024)S(1)} %compare_select_fusion.2, bf16[]{:T(256)} %constant.72.clone.1, bf16[768,1024]{1,0:T(8,128)(2,1)S(1)} %copy-done, f32[768]{0:T(1024)S(1)} %add_rsqrt_fusion), kind=kCustom, calls=%fused_computation.32 | custom fusion | flops 2359296 | bytes 6295554 | tf_op jit(solution)/shard_map/scatter | solution.py:56
  31.6 4.8 %all-to-all-start.1 = ((bf16[8,288,1024]{2,1,0:T(8,128)(2,1)}), bf16[8,288,1024]{2,1,0:T(8,128)(2,1)}, u32[]{:S(2)}, u32[]{:S(2)}) async-start(bf16[8,288,1024]{2,1,0:T(8,128)(2,1)} %bitcast.71), calls=%async_computation.1 | async-start | bytes 9437184 | tf_op jit(solution)/shard_map/all_to_all | solution.py:59
  37.3 54.5 %all-to-all-done.1 = bf16[8,288,1024]{2,1,0:T(8,128)(2,1)} async-done(((bf16[8,288,1024]{2,1,0:T(8,128)(2,1)}), bf16[8,288,1024]{2,1,0:T(8,128)(2,1)}, u32[]{:S(2)}, u32[]{:S(2)}) %all-to-all-start.1) | async-done | bytes 4718624 | tf_op jit(solution)/shard_map/all_to_all | solution.py:59
  91.8 15.1 %scatter_custom_fusion.3 = bf16[768,1024]{1,0:T(8,128)(2,1)} fusion(s32[2304]{0:T(1024)S(1)} %get-tuple-element.109, bf16[2304,1024]{1,0:T(8,128)(2,1)} %bitcast.6, bf16[]{:T(256)} %constant.72.clone.1), kind=kCustom, calls=%fused_computation.35 | custom fusion | bytes 1573376 | tf_op jit(solution)/shard_map/scatter | solution.py:76
  107.1 9.0 %scatter_custom_fusion.1 = s32[768]{0:T(1024)S(1)} fusion(s32[2304]{0:T(1024)S(1)} %get-tuple-element.109, s32[2304]{0:T(1024)S(1)} %reshape.203, s32[]{:T(128)} %constant.33.clone.1), kind=kCustom, calls=%fused_computation.72 | custom fusion | bytes 3076 | tf_op jit(solution)/shard_map/scatter | solution.py:78
  116.1 23.7 %all-gather = s32[16,1,768]{2,1,0:T(1,128)S(1)} all-gather(s32[1,1,768]{2,1,0:T(1,128)S(1)} %reshape.226), channel_id=1, replica_groups=mesh['tr'=8,'tc'=16] {'tc'}, dimensions={0}, use_global_device_ids=true | all-gather | bytes 52224 | tf_op jit(solution)/shard_map/all_gather | solution.py:83
  139.8 120.8 %all-gather.3.cloned.1.call-done = bf16[12288,1024]{1,0:T(8,128)(2,1)} async-done(((bf16[768,1024]{1,0:T(8,128)(2,1)}), bf16[12288,1024]{1,0:T(8,128)(2,1)}) %all-gather.3.cloned.1.call-update) | async-done | bytes 25165840 | tf_op jit(solution)/shard_map/all_gather | solution.py:82
  260.7 95.7 %while.15 = (s32[]{:T(128)}, f32[768]{0:T(1024)S(1)}, f32[768]{0:T(1024)S(1)}, f32[768]{0:T(1024)S(1)}, s32[768]{0:T(1024)S(1)}, /*index=5*/s32[16,768]{1,0:T(8,...) while((s32[]{:T(128)}, f32[768]{0:T(1024)S(1)}, ...), condition=%wide.region_14.15_spmd.clone, body=%wide.region_10.14_spmd.clone.sunk | while | flops 1216813824 | bytes 7953572 | solution.py:95
  261.3 0.7 iota_add_fusion.3
  261.9 3.5 select_reduce_fusion.2
  265.4 1.1 fusion.37
  267.2 0.7 iota_add_fusion.3
  267.9 3.5 select_reduce_fusion.2
  271.4 1.1 fusion.37
  273.2 0.7 iota_add_fusion.3
  273.9 3.5 select_reduce_fusion.2
  277.4 1.1 fusion.37
  279.2 0.7 iota_add_fusion.3
  279.9 3.5 select_reduce_fusion.2
  283.4 1.1 fusion.37
  285.2 0.7 iota_add_fusion.3
  285.9 3.5 select_reduce_fusion.2
  289.4 1.1 fusion.37
  291.2 0.7 iota_add_fusion.3
  291.8 3.5 select_reduce_fusion.2
  295.4 1.1 fusion.37
  297.2 0.7 iota_add_fusion.3
  297.8 3.5 select_reduce_fusion.2
  301.3 1.1 fusion.37
  303.1 0.7 iota_add_fusion.3
  303.8 3.5 select_reduce_fusion.2
  307.3 1.1 fusion.37
  309.1 0.7 iota_add_fusion.3
  309.8 3.5 select_reduce_fusion.2
  313.3 1.1 fusion.37
  315.1 0.7 iota_add_fusion.3
  315.8 3.5 select_reduce_fusion.2
  319.3 1.1 fusion.37
  321.1 0.7 iota_add_fusion.3
  321.7 3.5 select_reduce_fusion.2
  325.3 1.1 fusion.37
  327.1 0.7 iota_add_fusion.3
  327.7 3.5 select_reduce_fusion.2
  331.2 1.1 fusion.37
  333.7 3.5 select_reduce_fusion.2
  337.2 1.1 fusion.37
  339.7 3.5 select_reduce_fusion.2
  343.2 1.1 fusion.37
  345.7 3.5 select_reduce_fusion.2
  349.2 1.1 fusion.37
  351.7 3.5 select_reduce_fusion.2
  355.2 1.1 fusion.37
  356.6 3.9 %gather_fusion = f32[2304,3]{1,0:T(8,128)S(1)} fusion(f32[3,768]{0,1:T(8,128)S(1)} %copy.20, s32[3072]{0:T(1024)S(1)} %pad_clamp_fusion), kind=kCustom, calls=%fused_computation | custom fusion | bytes 64512 | tf_op jit(solution)/shard_map/gather | solution.py:108
  361.7 4.4 %all-to-all-start.2 = ((f32[3,8,288]{2,0,1:T(4,128)}), f32[3,8,288]{2,0,1:T(4,128)S(1)}, u32[]{:S(2)}, u32[]{:S(2)}) async-start(f32[3,8,288]{2,0,1:T(4,128)} %broadcast_select_fusion), calls=%async_computation.2 | async-start | bytes 98304 | tf_op jit(solution)/shard_map/all_to_all | solution.py:109
  366.1 5.5 %all-to-all-done.2 = f32[3,8,288]{2,0,1:T(4,128)S(1)} async-done(((f32[3,8,288]{2,0,1:T(4,128)}), f32[3,8,288]{2,0,1:T(4,128)S(1)}, u32[]{:S(2)}, u32[]{:S(2)}) %all-to-all-start.2) | async-done | bytes 27680 | tf_op jit(solution)/shard_map/all_to_all | solution.py:109
  372.1 1.6 gather_fusion.1
  373.6 1.2 slice_reduce_fusion
  (125 shorter events, 16.0 us)
Async XLA Ops:
  7.2 15.1 %copy-start = (bf16[768,1024]{1,0:T(8,128)(2,1)S(1)}, bf16[768,1024]{1,0:T(8,128)(2,1)}, u32[]{:S(2)}) copy-start(bf16[768,1024]{1,0:T(8,128)(2,1)} %param.4) | copy-start | bytes 4718596
  15.2 16.4 %all-to-all-start = ((s32[8,1,288]{2,1,0:T(1,128)}), s32[8,1,288]{2,1,0:T(1,128)S(1)}, u32[]{:S(2)}, u32[]{:S(2)}) async-start(s32[8,1,288]{2,1,0:T(1,128)} %all_to_all.12), calls=%async_computation | async-start | bytes 24576 | tf_op jit(solution)/shard_map/all_to_all | solution.py:66
  31.6 60.2 %all-to-all-start.1 = ((bf16[8,288,1024]{2,1,0:T(8,128)(2,1)}), bf16[8,288,1024]{2,1,0:T(8,128)(2,1)}, u32[]{:S(2)}, u32[]{:S(2)}) async-start(bf16[8,288,1024]{2,1,0:T(8,128)(2,1)} %bitcast.71), calls=%async_computation.1 | async-start | bytes 9437184 | tf_op jit(solution)/shard_map/all_to_all | solution.py:59
  36.4 224.3 %all-gather.3.cloned.1.call-start = ((), (), s32[]{:S(2)}) async-start(), calls=%async_computation.3 | async-start | bytes 26738688 | tf_op jit(solution)/shard_map/all_gather | solution.py:82
  361.7 10.0 %all-to-all-start.2 = ((f32[3,8,288]{2,0,1:T(4,128)}), f32[3,8,288]{2,0,1:T(4,128)S(1)}, u32[]{:S(2)}, u32[]{:S(2)}) async-start(f32[3,8,288]{2,0,1:T(4,128)} %broadcast_select_fusion), calls=%async_computation.2 | async-start | bytes 98304 | tf_op jit(solution)/shard_map/all_to_all | solution.py:109
Sparse Core Ops, SparseCore 0:
  107.1 153.5 all-gather.2
where the time goes:
time: 383 us; the launch traced here: 382 us
  waiting for transfers between devices  181 us (47%)
  matrix products  56 us (15%)
  local copies, waits for them, and re-layouts  46.5 us (12%)
  other arithmetic  44.7 us (12%)
  blocking collectives  23.7 us (6%)
  starting transfers between devices  14.6 us (4%)
  between operations  14.3 us (4%)
    all_gather x1, waiting for transfers between devices, per_device(): key_rows = lax.all_gather(queries, 'tc', axis=0, tiled=True)  121 us
    dot_general x16, matrix products, pair_products(): lax.dot_general(left, right, (((1,), (1,)), ((), ())), preferred_element_...  56 us
    all_to_all x1, waiting for transfers between devices, per_device(): lax.all_to_all(send_rows.reshape(tile_rows, capacity, feature_dim), 'tr',...  54.5 us
    all_gather x1, blocking collectives, per_device(): key_labels = lax.all_gather(query_labels, 'tc', axis=0, tiled=True)  23.7 us
    reduce_sum x16, other arithmetic, tile_update(): jnp.sum(terms * sims, axis=1)  18.3 us
    scatter x1, local copies, waits for them, and re-layouts, per_device(): jnp.zeros((shard_rows, feature_dim), jnp.bfloat16).at[target]  15.1 us
    add x16, other arithmetic, step(): offset + local_range[None, :]  10.4 us
    dynamic_slice x32, local copies, waits for them, and re-layouts, per_device(): lax.scan(step, stats, (key_rows.reshape(count, shard_rows, feature_dim),...  9.7 us
  transfers between devices with their start and end apart: 4, of which 3 were waited for; matrix products, arithmetic and copies ran while one was open for 6% of the time, Pallas kernels for 0%

commit v1 on v0

v1 whole, which is shorter than its diff:
```python
import functools

import jax
import jax.numpy as jnp
from jax import lax
from jax.experimental import pallas as pl
from jax.experimental.pallas import tpu as pltpu
from jax.sharding import PartitionSpec as P

GROUP_SHIFT = 2
TILE_ROWS = 8
SIDE = 4
ROWS = 768
WIDTH = 1024
CAP = 288
PAIR = 304
LANES = 384
BLOCK = ROWS + 16
SPAN = 1152
EPSILON = 1e-06
THRESHOLD = 0.3
SHARPNESS = 50.0
SCALE2 = 256.0 * 1.4426950408889634
NEGATIVE = -1e30
FLOOR = -5e29
CHUNK = 256
VMEM = 56 * 1024 * 1024
BF = jnp.bfloat16
F32 = jnp.float32


def iota(shape, axis):
    return lax.broadcasted_iota(jnp.int32, shape, axis)


def dot(a, b):
    return lax.dot_general(a, b, (((1,), (0,)), ((), ())), preferred_element_type=F32)


def dot_nt(a, b):
    return lax.dot_general(a, b, (((1,), (1,)), ((), ())), preferred_element_type=F32)


def params(**more):
    return pltpu.CompilerParams(vmem_limit_bytes=VMEM, **more)


def whole(shape):
    return pl.BlockSpec(shape, lambda *_: (0,) * len(shape))


def pack_kernel(emb_ref, lab_ref, out_ref, rank_ref, unit):
    g = pl.program_id(0)
    lab = lab_ref[...]
    owner = lax.shift_right_logical(lab, GROUP_SHIFT)

    @pl.when(g == 0)
    def _():
        values = emb_ref[...].astype(F32)
        total = jnp.sum(values * values, axis=1, keepdims=True)
        unit[...] = (values * lax.rsqrt(total + EPSILON)).astype(BF)
        onehot = (iota((TILE_ROWS, ROWS), 0) == owner).astype(F32)
        before = (iota((ROWS, ROWS), 0) < iota((ROWS, ROWS), 1)).astype(F32).astype(BF)
        seen = dot(onehot.astype(BF), before)
        rank_ref[...] = jnp.sum(onehot * seen, axis=0, keepdims=True).astype(jnp.int32)

    slot = jnp.where(owner == g, rank_ref[...], -1)
    pick = (iota((LANES, ROWS), 0) == slot).astype(F32).astype(BF)
    out_ref[0] = dot(pick[:PAIR], unit[...]).astype(BF)
    marks = jnp.broadcast_to(lab.astype(F32) + 1.0, (16, ROWS)).astype(BF)
    out_ref[0, CAP:, :LANES] = (dot_nt(marks, pick) - 1.0).astype(BF)
    out_ref[0, CAP:, LANES:] = jnp.zeros((16, WIDTH - LANES), BF)


def pack(embeddings, labels):
    return pl.pallas_call(
        pack_kernel,
        grid=(TILE_ROWS,),
        in_specs=[whole((ROWS, WIDTH)), whole((1, ROWS))],
        out_specs=[pl.BlockSpec((1, PAIR, WIDTH), lambda g: (g, 0, 0)), whole((1, ROWS))],
        out_shape=[
            jax.ShapeDtypeStruct((TILE_ROWS, PAIR, WIDTH), BF),
            jax.ShapeDtypeStruct((1, ROWS), jnp.int32),
        ],
        scratch_shapes=[pltpu.VMEM((ROWS, WIDTH), BF)],
        compiler_params=params(),
        name="pack",
    )(embeddings, labels)


def compact_kernel(got_ref, out_ref, offset_ref, rows, names, place):
    r = pl.program_id(0)

    @pl.when(r == 0)
    def _():
        place[0] = 0
        rows[:16] = jnp.zeros((16, WIDTH), BF)
        names[...] = jnp.zeros((8, SPAN), F32)

    offset = place[0]
    offset_ref[r] = offset
    lab = got_ref[0, CAP:, :LANES].astype(F32)[:8]
    count = jnp.sum((lab[:1] >= 0.0).astype(F32)).astype(jnp.int32)
    place[0] = offset + count
    base = pl.multiple_of(lax.div(offset, 16) * 16, 16)
    column = iota((PAIR, PAIR), 1)
    move = (iota((PAIR, PAIR), 0) == column + (offset - base)) & (column < count)
    moved = dot(move.astype(F32).astype(BF), got_ref[0]).astype(BF)
    rows[pl.ds(base, 16)] = rows[pl.ds(base, 16)] + moved[:16]
    rows[pl.ds(base + 16, PAIR - 16)] = moved[16:]
    held = jnp.concatenate([jnp.maximum(lab, 0.0), jnp.zeros((8, SPAN - LANES), F32)], axis=1)
    names[...] += pltpu.roll(held, offset, 1)

    @pl.when(r == TILE_ROWS - 1)
    def _():
        out_ref[:ROWS] = rows[:ROWS]
        out_ref[ROWS:, :ROWS] = jnp.broadcast_to(names[:1, :ROWS], (16, ROWS)).astype(BF)
        out_ref[ROWS:, ROWS:] = jnp.zeros((16, WIDTH - ROWS), BF)


def compact(got):
    return pl.pallas_call(
        compact_kernel,
        grid=(TILE_ROWS,),
        in_specs=[pl.BlockSpec((1, PAIR, WIDTH), lambda r: (r, 0, 0))],
        out_specs=[whole((BLOCK, WIDTH)), pl.BlockSpec(memory_space=pltpu.SMEM)],
        out_shape=[
            jax.ShapeDtypeStruct((BLOCK, WIDTH), BF),
            jax.ShapeDtypeStruct((TILE_ROWS,), jnp.int32),
        ],
        scratch_shapes=[
            pltpu.VMEM((ROWS + PAIR, WIDTH), BF),
            pltpu.VMEM((8, SPAN), F32),
            pltpu.SMEM((1,), jnp.int32),
        ],
        compiler_params=params(),
        name="compact",
    )(got)


def fold(tile):
    return tile.reshape(tile.shape[0] // 8, 8, tile.shape[1])


def column_stats(query, keys, scores):
    names = query[ROWS:, :ROWS].astype(F32)[:1]
    top = jnp.full((8, ROWS), NEGATIVE, F32)
    for k, (block, marks, same) in enumerate(keys):

        def score(i, top, k=k, block=block, marks=marks, same=same):
            start = pl.multiple_of(i * CHUNK, CHUNK)
            sims = dot_nt(block[pl.ds(start, CHUNK)], query[:ROWS]) * SCALE2
            mark = marks[pl.ds(start, CHUNK)]
            mask = jnp.concatenate([mark] * (ROWS // 128), axis=1) == names
            if same:
                mask = mask & (iota((CHUNK, ROWS), 0) + start != iota((CHUNK, ROWS), 1))
            sims = jnp.where(mask, sims, NEGATIVE)
            scores[pl.ds(pl.multiple_of(k * ROWS + start, CHUNK), CHUNK)] = sims
            return jnp.maximum(top, jnp.max(fold(sims), axis=0))

        top = lax.fori_loop(0, ROWS // CHUNK, score, top)
    top = jnp.maximum(jnp.max(top, axis=0, keepdims=True), FLOOR)

    def add(i, sums):
        sims = scores[pl.ds(pl.multiple_of(i * CHUNK, CHUNK), CHUNK)]
        terms = jnp.exp2(sims - top)
        return (
            sums[0] + jnp.sum(fold(terms), axis=0),
            sums[1] + jnp.sum(fold(terms * sims), axis=0),
        )

    zero = jnp.zeros((8, ROWS), F32)
    total, weight = lax.fori_loop(0, len(keys) * ROWS // CHUNK, add, (zero, zero))
    return top, jnp.sum(total, axis=0, keepdims=True), jnp.sum(weight, axis=0, keepdims=True)


def merge(parts):
    top = functools.reduce(jnp.maximum, [p[0] for p in parts])
    factors = [jnp.exp2(p[0] - top) for p in parts]
    total = sum(p[1] * f for p, f in zip(parts, factors))
    weight = sum(p[2] * f for p, f in zip(parts, factors))
    return top, total, weight


def put_stats(ref, stats):
    for k, value in enumerate(stats):
        ref[k : k + 1] = value


def get_stats(ref):
    return tuple(ref[k : k + 1] for k in range(3))


def pair_kernel(plan, blocks, old, *refs):
    n_old = len(old)
    ins, olds = refs[: len(blocks)], refs[len(blocks) : len(blocks) + n_old]
    outs = refs[len(blocks) + n_old : -2]
    marks, scores = refs[-2:]
    where = {b: i for i, b in enumerate(blocks)}
    used = sorted({k for _, keys in plan for k in keys})
    for b in used:
        names = ins[where[b]][ROWS:, :ROWS].astype(F32)
        marks[where[b]] = jnp.transpose(jnp.broadcast_to(names[:1], (128, ROWS)))
    before = {b: olds[i] for i, b in enumerate(old)}
    for out, (q, keys) in zip(outs, plan):
        stats = column_stats(
            ins[where[q]], [(ins[where[k]], marks.at[where[k]], k == q) for k in keys], scores
        )
        if q in before:
            stats = merge([stats, get_stats(before[q])])
        put_stats(out, stats)


def pairs(plan, blocks, old):
    names, n = list(blocks), len(plan)
    most = max(len(keys) for _, keys in plan)
    units = sum(len(keys) for _, keys in plan)
    return pl.pallas_call(
        functools.partial(pair_kernel, plan, names, list(old)),
        out_shape=[jax.ShapeDtypeStruct((8, ROWS), F32)] * n,
        in_specs=[pl.BlockSpec(memory_space=pltpu.VMEM)] * (len(blocks) + len(old)),
        out_specs=[pl.BlockSpec(memory_space=pltpu.VMEM)] * n,
        scratch_shapes=[
            pltpu.VMEM((len(blocks), ROWS, 128), F32),
            pltpu.VMEM((most * ROWS, ROWS), F32),
        ],
        compiler_params=params(),
        cost_estimate=pl.CostEstimate(
            flops=2 * units * ROWS * ROWS * WIDTH,
            bytes_accessed=2 * len(blocks) * BLOCK * WIDTH,
            transcendentals=units * ROWS * ROWS,
        ),
        name="pairs",
    )(*blocks.values(), *old.values())


def spread_kernel(offset_ref, *refs):
    out_ref = refs[-1]
    top, total, weight = merge([get_stats(r) for r in refs[:-1]])
    best = top / SCALE2
    mean = weight / total / SCALE2
    row = iota((8, ROWS), 0)
    values = jnp.where(row == 0, best, jnp.where(row == 1, mean, 0.0))
    values = jnp.concatenate([values, jnp.zeros((8, SPAN - ROWS), F32)], axis=1)
    for r in range(TILE_ROWS):
        offset = offset_ref[r]
        out_ref[r] = pltpu.roll(values, lax.rem(SPAN - offset, SPAN), 1)[:, :LANES]


def spread(offsets, stats):
    return pl.pallas_call(
        spread_kernel,
        out_shape=jax.ShapeDtypeStruct((TILE_ROWS, 8, LANES), F32),
        in_specs=[pl.BlockSpec(memory_space=pltpu.SMEM)]
        + [pl.BlockSpec(memory_space=pltpu.VMEM)] * len(stats),
        out_specs=pl.BlockSpec(memory_space=pltpu.VMEM),
        compiler_params=params(),
        name="spread",
    )(offsets, *stats)


def unpack_kernel(back_ref, lab_ref, rank_ref, best_ref, mean_ref, flag_ref):
    owner = lax.shift_right_logical(lab_ref[...], GROUP_SHIFT)
    found = jnp.zeros((24, ROWS), F32)
    for g in range(TILE_ROWS):
        slot = jnp.where(owner == g, rank_ref[...], -1)
        pick = (iota((LANES, ROWS), 0) == slot).astype(F32).astype(BF)
        values = back_ref[g]
        high = values.astype(BF).astype(F32)
        mid = (values - high).astype(BF).astype(F32)
        low = values - high - mid
        found += dot(jnp.concatenate([high, mid, low], axis=0).astype(BF), pick)
    found = found[:8] + (found[8:16] + found[16:])
    best = found[:1]
    best_ref[...] = best
    mean_ref[...] = found[1:2]
    flag_ref[...] = 1.0 / (1.0 + jnp.exp(-SHARPNESS * (best - THRESHOLD)))


def unpack(back, labels, rank):
    return pl.pallas_call(
        unpack_kernel,
        out_shape=[jax.ShapeDtypeStruct((1, ROWS), F32)] * 3,
        in_specs=[pl.BlockSpec(memory_space=pltpu.VMEM)] * 3,
        out_specs=[pl.BlockSpec(memory_space=pltpu.VMEM)] * 3,
        compiler_params=params(),
        name="unpack",
    )(back, labels, rank)


def shift(array, dx, dy):
    moves = []
    for tr in range(TILE_ROWS):
        sign = 1 - 2 * (tr % 2)
        for x in range(SIDE):
            for y in range(SIDE):
                to = ((x + sign * dx) % SIDE) * SIDE + (y + sign * dy) % SIDE
                base = tr * SIDE * SIDE
                moves.append((base + x * SIDE + y, base + to))
    return lax.ppermute(array, ("tr", "tc"), moves)


PLACES = {"O": (0, 0), "A": (1, 0), "B": (2, 0), "C": (0, 1), "D": (0, -1), "E": (0, 2)}
NEAR = [("O", "OAC"), ("A", "OCD"), ("C", "OA"), ("D", "AC")]
FAR = [("O", "B"), ("A", "E"), ("B", "CE"), ("C", "B"), ("E", "A")]


def per_device(embeddings, labels):
    lab = labels.reshape(1, ROWS)
    packed, rank = pack(embeddings, lab)
    got = lax.all_to_all(packed, "tr", split_axis=0, concat_axis=0, tiled=True)
    mine, offsets = compact(got)
    a = shift(mine, -1, 0)
    c = shift(mine, 0, -1)
    d = shift(mine, 0, 1)
    b = shift(a, -1, 0)
    e = shift(d, 0, 1)
    near = pairs(NEAR, {"O": mine, "A": a, "C": c, "D": d}, {})
    stats = dict(zip([q for q, _ in NEAR], near))
    far = pairs(
        FAR,
        {"O": mine, "A": a, "B": b, "C": c, "E": e},
        {q: stats[q] for q in "OAC"},
    )
    stats.update(zip([q for q, _ in FAR], far))
    parts = [stats["O"]] + [shift(stats[q], *PLACES[q]) for q in "ABCDE"]
    sent = spread(offsets, parts)
    back = lax.all_to_all(sent, "tr", split_axis=0, concat_axis=0, tiled=True)
    outs = unpack(back, lab, rank)
    return tuple(o.reshape(ROWS) for o in outs)


def solution(mesh):
    files = P(("tr", "tc"))
    return jax.shard_map(
        per_device,
        mesh=mesh,
        in_specs=(P(("tr", "tc"), None), files),
        out_specs=(files, files, files),
        check_vma=False,
    )
```

time: 383 us -> 206 us (0.54)
  waiting for transfers between devices: 181 us -> 36.4 us
  Pallas kernels: 0 us -> 68.8 us
  matrix products: 56 us -> 0 us
  blocking collectives: 23.7 us -> 74.1 us
  local copies, waits for them, and re-layouts: 46.5 us -> 5.35 us
  other arithmetic: 44.7 us -> 3.84 us
  between operations: 14.3 us -> 0.7 us
    all_gather x1 -> x0, waiting for transfers between devices: 121 us -> none  [per_device(): key_rows = lax.all_gather(queries, 'tc', axis=0, tiled=True)]
    all_to_all x0 -> x2, blocking collectives: none -> 74.1 us  [the longest x1 64.3 us: per_device(): got = lax.all_to_all(packed, 'tr', split_axis=0, concat_axis=0, tiled=True)]
    pallas_call x0 -> x6, Pallas kernels: none -> 68.8 us  [the longest x2 46.8 us: pairs(): pl.pallas_call(functools.partial(pair_kernel, plan, names, list(old)), ou...]
    all_to_all x3 -> x0, waiting for transfers between devices: 60 us -> none  [the longest x1 54.5 us: per_device(): lax.all_to_all(send_rows.reshape(tile_rows, capacity, feature_dim), 'tr',...]
    dot_general x16 -> x0, matrix products: 56 us -> none  [pair_products(): lax.dot_general(left, right, (((1,), (1,)), ((), ())), preferred_element_...]
    ppermute x0 -> x10, waiting for transfers between devices: none -> 36.4 us  [shift(): return lax.ppermute(array, ('tr', 'tc'), moves)]
    scatter x3 -> x0, local copies, waits for them, and re-layouts: 27.7 us -> none  [the longest x1 15.1 us: per_device(): jnp.zeros((shard_rows, feature_dim), jnp.bfloat16).at[target]]
    all_gather x1 -> x0, blocking collectives: 23.7 us -> none  [per_device(): key_labels = lax.all_gather(query_labels, 'tc', axis=0, tiled=True)]
  transfers between devices with their start and end apart: 4 -> 10, of which waited for: 3 -> 4; matrix products, arithmetic and copies ran while one was open for 6% -> 0% of each run, Pallas kernels for 0% -> 23%
where the time goes in v1:
time: 206 us; the launch traced here: 205 us
  blocking collectives  74.1 us (36%)
  Pallas kernels  68.8 us (33%)
  waiting for transfers between devices  36.4 us (18%)
  starting transfers between devices  15.5 us (8%)
  local copies, waits for them, and re-layouts  5.35 us (3%)
  other arithmetic  3.84 us (2%)
    all_to_all x1, blocking collectives, per_device(): got = lax.all_to_all(packed, 'tr', split_axis=0, concat_axis=0, tiled=True)  64.3 us
    pallas_call x2, Pallas kernels, pairs(): pl.pallas_call(functools.partial(pair_kernel, plan, names, list(old)), ou...  46.8 us
    ppermute x10, waiting for transfers between devices, shift(): return lax.ppermute(array, ('tr', 'tc'), moves)  36.4 us
    ppermute x10, starting transfers between devices, shift(): return lax.ppermute(array, ('tr', 'tc'), moves)  15.5 us
    all_to_all x1, blocking collectives, per_device(): back = lax.all_to_all(sent, 'tr', split_axis=0, concat_axis=0, tiled=True)  9.76 us
    pallas_call x1, Pallas kernels, pack(): pl.pallas_call(pack_kernel, grid=(TILE_ROWS,), in_specs=[whole((ROWS, WID...  9.22 us
    pallas_call x1, Pallas kernels, compact(): pl.pallas_call(compact_kernel, grid=(TILE_ROWS,), in_specs=[pl.BlockSpec(...  8.76 us
  transfers between devices with their start and end apart: 10, of which 4 were waited for; matrix products, arithmetic and copies ran while one was open for 0% of the time, Pallas kernels for 23%

profile of v1, /device:TPU:2, one launch (start us, length us, event | category | flops | bytes accessed | tf_op | source)
XLA Modules:
  0.0 204.7 jit_solution(2619801153679031989)
XLA Ops:
  0.6 1.3 reshape.18.lab_ref
  1.9 9.2 %pack.1 = (bf16[8,304,1024]{2,1,0:T(8,128)(2,1)}, s32[1,768]{1,0:T(1,128)}) custom-call(bf16[768,1024]{1,0:T(8,128)(2,1)} %emb_ref.1, s32[1,768]{1,0:T(1,128)} %reshape.18.lab_ref), custom_call_target="tpu_custom_call" | custom-call | tf_op jit(solution)/shard_map/pack/pallas_call | solution.py:76
  11.1 64.3 %all_to_all.10.got_ref = bf16[8,304,1024]{2,1,0:T(8,128)(2,1)} all-to-all(bf16[8,304,1024]{2,1,0:T(8,128)(2,1)} %get-tuple-element.19), channel_id=1, replica_groups=mesh['tr'=8,'tc'=16] {'tr'}, dimensions={0} | all-to-all | bytes 9961472 | tf_op jit(solution)/shard_map/all_to_all | solution.py:311
  75.4 8.8 %compact.1 = (bf16[784,1024]{1,0:T(8,128)(2,1)}, s32[8]{0:T(128)}) custom-call(bf16[8,304,1024]{2,1,0:T(8,128)(2,1)} %all_to_all.10.got_ref), custom_call_target="tpu_custom_call" | custom-call | tf_op jit(solution)/shard_map/compact/pallas_call | solution.py:122
  84.2 1.6 collective-permute-start.3
  85.8 0.5 collective-permute-start
  86.4 1.7 collective-permute-start.2
  88.0 33.1 %collective-permute-done.3.refs_3_ = bf16[784,1024]{1,0:T(8,128)(2,1)S(1)} collective-permute-done((bf16[784,1024]{1,0:T(8,128)(2,1)}, bf16[784,1024]{1,0:T(8,128)(2,1)S(1)}, u32[]{:S(2)}, u32[]{:S(2)}) %collective-permute-start.3) | collective-permute-done | bytes 1605664 | tf_op jit(solution)/shard_map/ppermute | solution.py:300
  121.2 0.0 copy-start.8
  121.2 1.9 collective-permute-start.4
  123.1 0.0 collective-permute-done.refs_1_
  123.1 0.0 copy-start.5
  123.1 0.5 collective-permute-start.1
  123.6 0.0 collective-permute-done.2.refs_2_.refs_3_
  123.6 0.0 copy-done.8
  123.6 0.6 copy-done.5
  124.3 0.0 copy-start.6
  124.3 1.1 copy-done.6
  125.4 27.9 %pairs.2 = (f32[8,768]{1,0:T(8,128)}, f32[8,768]{1,0:T(8,128)}, f32[8,768]{1,0:T(8,128)}, f32[8,768]{1,0:T(8,128)}) custom-call(bf16[784,1024]{1,0:T(8,128)(2,1)} %get-tuple-element.21.refs_0_, bf16[784,1024]{1,0:T(8,128)(2,1)} %copy-done.5, bf16[784,1024]{1,0:T(8,128)(2,1)} %copy-done.6, bf16[784,1024]{1,0:T(8,128)(2,1)} %copy-done.8), custom_call_target="tpu_custom_call" | custom-call | flops 12079595520 | bytes 6422528 | tf_op jit(solution)/shard_map/pairs/pallas_call | solution.py:218
  153.4 2.7 %collective-permute-start.8 = (f32[8,768]{1,0:T(8,128)}, f32[8,768]{1,0:T(8,128)S(1)}, u32[]{:S(2)}, u32[]{:S(2)}) collective-permute-start(f32[8,768]{1,0:T(8,128)} %get-tuple-element.29), channel_id=1, source_target_pairs={{0,3},{1,0},{2,1},{3,2},{4,7},{5,4},{6,5},{7,6},{8,11},{9,8},{10,9... | collective-permute-start | bytes 73736 | tf_op jit(solution)/shard_map/ppermute | solution.py:300
  156.0 0.0 collective-permute-done.4.refs_4_
  156.1 0.0 copy-start.7
  156.1 0.0 collective-permute-done.1.refs_2_
  156.1 0.0 copy-start.9
  156.1 1.1 copy-done.7
  157.2 0.5 copy-done.9
  157.7 18.8 %pairs.3 = (f32[8,768]{1,0:T(8,128)}, f32[8,768]{1,0:T(8,128)}, f32[8,768]{1,0:T(8,128)}, f32[8,768]{1,0:T(8,128)}, f32[8,768]{1,0:T(8,128)}) custom-call(bf16[784,1024]{1,0:T(8,128)(2,1)} %get-tuple-element.21.refs_0_, bf16[784,1024]{1,0:T(8,128)(2,1)} %copy-done.5, bf16[784,1024]{1,0:T(8,128)(2,1)} %copy-done.9, bf16[784,1024]{1,0:T(8,128)(2,1)} %copy-done.6, ...), custom_call_target="tpu_custom_call" | custom-call | flops 7247757312 | bytes 8028160 | tf_op jit(solution)/shard_map/pairs/pallas_call | solution.py:218
  176.6 1.6 collective-permute-start.5
  178.1 2.3 %collective-permute-start.6 = (f32[8,768]{1,0:T(8,128)}, f32[8,768]{1,0:T(8,128)S(1)}, u32[]{:S(2)}, u32[]{:S(2)}) collective-permute-start(f32[8,768]{1,0:T(8,128)} %get-tuple-element.27), channel_id=1, source_target_pairs={{0,8},{1,9},{2,10},{3,11},{4,12},{5,13},{6,14},{7,15},{8,0},{9,1},... | collective-permute-start | bytes 73736 | tf_op jit(solution)/shard_map/ppermute | solution.py:300
  180.4 0.5 collective-permute-start.7
  180.9 2.2 %collective-permute-start.9 = (f32[8,768]{1,0:T(8,128)}, f32[8,768]{1,0:T(8,128)S(1)}, u32[]{:S(2)}, u32[]{:S(2)}) collective-permute-start(f32[8,768]{1,0:T(8,128)} %get-tuple-element.30), channel_id=1, source_target_pairs={{0,2},{1,3},{2,0},{3,1},{4,6},{5,7},{6,4},{7,5},{8,10},{9,11},{10,... | collective-permute-start | bytes 73736 | tf_op jit(solution)/shard_map/ppermute | solution.py:300
  183.1 0.0 collective-permute-done.8.refs_4_
  183.1 0.0 copy-start
  183.1 0.0 collective-permute-done.5.refs_1_
  183.2 0.0 copy-start.1
  183.2 0.5 collective-permute-done.6.refs_2_
  183.7 0.0 copy-start.2
  183.7 2.0 collective-permute-done.7.refs_3_
  185.7 0.0 copy-start.3
  185.7 0.8 collective-permute-done.9.refs_5_
  186.5 0.0 copy-start.4
  186.5 0.0 copy-done
  186.5 0.0 copy-done.1
  186.5 0.0 copy-done.2
  186.5 0.0 copy-done.3
  186.5 0.6 copy-done.4
  187.1 1.6 spread.1
  188.7 9.8 %all_to_all.11.back_ref = f32[8,8,384]{2,1,0:T(8,128)} all-to-all(f32[8,8,384]{2,1,0:T(8,128)} %spread.1), channel_id=1, replica_groups=mesh['tr'=8,'tc'=16] {'tr'}, dimensions={0} | all-to-all | bytes 196608 | tf_op jit(solution)/shard_map/all_to_all | solution.py:328
  198.5 2.4 %unpack.1 = (f32[1,768]{1,0:T(1,128)}, f32[1,768]{1,0:T(1,128)}, f32[1,768]{1,0:T(1,128)}) custom-call(f32[8,8,384]{2,1,0:T(8,128)} %all_to_all.11.back_ref, s32[1,768]{1,0:T(1,128)} %reshape.18.lab_ref, s32[1,768]{1,0:T(1,128)} %get-tuple-element.31.rank_ref), custom_call_target="tpu_custom_call" | custom-call | tf_op jit(solution)/shard_map/unpack/pallas_call | solution.py:281
  200.9 1.3 reduce
  202.1 1.3 reduce.1
  203.4 1.3 reduce.2
Async XLA Ops:
  84.2 36.9 %collective-permute-start.3 = (bf16[784,1024]{1,0:T(8,128)(2,1)}, bf16[784,1024]{1,0:T(8,128)(2,1)S(1)}, u32[]{:S(2)}, u32[]{:S(2)}) collective-permute-start(bf16[784,1024]{1,0:T(8,128)(2,1)} %get-tuple-element.21.refs_0_), channel_id=1, source_target_pairs={{0,1},{1,2},{2,3},{3,0},{4,5},{5,6},{6,7},{7,4},{8,9},{9,10},{10,1... | collective-permute-start | bytes 4816904 | tf_op jit(solution)/shard_map/ppermute | solution.py:300
  85.8 37.3 %collective-permute-start = (bf16[784,1024]{1,0:T(8,128)(2,1)}, bf16[784,1024]{1,0:T(8,128)(2,1)S(1)}, u32[]{:S(2)}, u32[]{:S(2)}) collective-permute-start(bf16[784,1024]{1,0:T(8,128)(2,1)} %get-tuple-element.21.refs_0_), channel_id=1, source_target_pairs={{0,12},{1,13},{2,14},{3,15},{4,0},{5,1},{6,2},{7,3},{8,4},{9,5},{1... | collective-permute-start | bytes 4816904 | tf_op jit(solution)/shard_map/ppermute | solution.py:300
  86.4 37.3 %collective-permute-start.2 = (bf16[784,1024]{1,0:T(8,128)(2,1)}, bf16[784,1024]{1,0:T(8,128)(2,1)S(1)}, u32[]{:S(2)}, u32[]{:S(2)}) collective-permute-start(bf16[784,1024]{1,0:T(8,128)(2,1)} %get-tuple-element.21.refs_0_), channel_id=1, source_target_pairs={{0,3},{1,0},{2,1},{3,2},{4,7},{5,4},{6,5},{7,6},{8,11},{9,8},{10,9... | collective-permute-start | bytes 4816904 | tf_op jit(solution)/shard_map/ppermute | solution.py:300
  121.2 2.5 %copy-start.8 = (bf16[784,1024]{1,0:T(8,128)(2,1)}, bf16[784,1024]{1,0:T(8,128)(2,1)S(1)}, u32[]{:S(2)}) copy-start(bf16[784,1024]{1,0:T(8,128)(2,1)S(1)} %collective-permute-done.3.refs_3_) | copy-start | bytes 4816900
  121.2 34.9 %collective-permute-start.4 = (bf16[784,1024]{1,0:T(8,128)(2,1)S(1)}, bf16[784,1024]{1,0:T(8,128)(2,1)S(1)}, u32[]{:S(2)}, u32[]{:S(2)}) collective-permute-start(bf16[784,1024]{1,0:T(8,128)(2,1)S(1)} %collective-permute-done.3.refs_3_), channel_id=1, source_target_pairs={{0,1},{1,2},{2,3},{3,0},{4,5},{5,6},{6,7},{7,4},{8,9},{9,10},{10,1... | collective-permute-start | bytes 4816904 | tf_op jit(solution)/shard_map/ppermute | solution.py:300
  123.1 1.2 copy-start.5
  123.1 32.9 %collective-permute-start.1 = (bf16[784,1024]{1,0:T(8,128)(2,1)S(1)}, bf16[784,1024]{1,0:T(8,128)(2,1)S(1)}, u32[]{:S(2)}, u32[]{:S(2)}) collective-permute-start(bf16[784,1024]{1,0:T(8,128)(2,1)S(1)} %collective-permute-done.refs_1_), channel_id=1, source_target_pairs={{0,12},{1,13},{2,14},{3,15},{4,0},{5,1},{6,2},{7,3},{8,4},{9,5},{1... | collective-permute-start | bytes 4816904 | tf_op jit(solution)/shard_map/ppermute | solution.py:300
  124.3 1.1 copy-start.6
  153.4 29.8 %collective-permute-start.8 = (f32[8,768]{1,0:T(8,128)}, f32[8,768]{1,0:T(8,128)S(1)}, u32[]{:S(2)}, u32[]{:S(2)}) collective-permute-start(f32[8,768]{1,0:T(8,128)} %get-tuple-element.29), channel_id=1, source_target_pairs={{0,3},{1,0},{2,1},{3,2},{4,7},{5,4},{6,5},{7,6},{8,11},{9,8},{10,9... | collective-permute-start | bytes 73736 | tf_op jit(solution)/shard_map/ppermute | solution.py:300
  156.1 1.2 copy-start.7
  156.1 1.7 copy-start.9
  176.6 6.6 %collective-permute-start.5 = (f32[8,768]{1,0:T(8,128)}, f32[8,768]{1,0:T(8,128)S(1)}, u32[]{:S(2)}, u32[]{:S(2)}) collective-permute-start(f32[8,768]{1,0:T(8,128)} %get-tuple-element.26), channel_id=1, source_target_pairs={{0,4},{1,5},{2,6},{3,7},{4,8},{5,9},{6,10},{7,11},{8,12},{9,13},{1... | collective-permute-start | bytes 73736 | tf_op jit(solution)/shard_map/ppermute | solution.py:300
  178.1 5.5 %collective-permute-start.6 = (f32[8,768]{1,0:T(8,128)}, f32[8,768]{1,0:T(8,128)S(1)}, u32[]{:S(2)}, u32[]{:S(2)}) collective-permute-start(f32[8,768]{1,0:T(8,128)} %get-tuple-element.27), channel_id=1, source_target_pairs={{0,8},{1,9},{2,10},{3,11},{4,12},{5,13},{6,14},{7,15},{8,0},{9,1},... | collective-permute-start | bytes 73736 | tf_op jit(solution)/shard_map/ppermute | solution.py:300
  180.4 5.2 %collective-permute-start.7 = (f32[8,768]{1,0:T(8,128)}, f32[8,768]{1,0:T(8,128)S(1)}, u32[]{:S(2)}, u32[]{:S(2)}) collective-permute-start(f32[8,768]{1,0:T(8,128)} %get-tuple-element.28), channel_id=1, source_target_pairs={{0,1},{1,2},{2,3},{3,0},{4,5},{5,6},{6,7},{7,4},{8,9},{9,10},{10,1... | collective-permute-start | bytes 73736 | tf_op jit(solution)/shard_map/ppermute | solution.py:300
  180.9 5.5 %collective-permute-start.9 = (f32[8,768]{1,0:T(8,128)}, f32[8,768]{1,0:T(8,128)S(1)}, u32[]{:S(2)}, u32[]{:S(2)}) collective-permute-start(f32[8,768]{1,0:T(8,128)} %get-tuple-element.30), channel_id=1, source_target_pairs={{0,2},{1,3},{2,0},{3,1},{4,6},{5,7},{6,4},{7,5},{8,10},{9,11},{10,... | collective-permute-start | bytes 73736 | tf_op jit(solution)/shard_map/ppermute | solution.py:300
  183.1 3.3 %copy-start = (f32[8,768]{1,0:T(8,128)}, f32[8,768]{1,0:T(8,128)S(1)}, u32[]{:S(2)}) copy-start(f32[8,768]{1,0:T(8,128)S(1)} %collective-permute-done.8.refs_4_) | copy-start | bytes 73732
  183.2 3.3 %copy-start.1 = (f32[8,768]{1,0:T(8,128)}, f32[8,768]{1,0:T(8,128)S(1)}, u32[]{:S(2)}) copy-start(f32[8,768]{1,0:T(8,128)S(1)} %collective-permute-done.5.refs_1_) | copy-start | bytes 73732
  183.7 2.8 %copy-start.2 = (f32[8,768]{1,0:T(8,128)}, f32[8,768]{1,0:T(8,128)S(1)}, u32[]{:S(2)}) copy-start(f32[8,768]{1,0:T(8,128)S(1)} %collective-permute-done.6.refs_2_) | copy-start | bytes 73732
  185.7 0.8 copy-start.3
  186.5 0.6 copy-start.4

commit v2 on v1

--- a/solution.py
+++ b/solution.py
@@ -24,6 +24,8 @@
 NEGATIVE = -1e30
 FLOOR = -5e29
 CHUNK = 256
+HALF = 384
+STRIP = 32
 VMEM = 56 * 1024 * 1024
 BF = jnp.bfloat16
 F32 = jnp.float32
@@ -142,38 +144,6 @@
     return tile.reshape(tile.shape[0] // 8, 8, tile.shape[1])
 
 
-def column_stats(query, keys, scores):
-    names = query[ROWS:, :ROWS].astype(F32)[:1]
-    top = jnp.full((8, ROWS), NEGATIVE, F32)
-    for k, (block, marks, same) in enumerate(keys):
-
-        def score(i, top, k=k, block=block, marks=marks, same=same):
-            start = pl.multiple_of(i * CHUNK, CHUNK)
-            sims = dot_nt(block[pl.ds(start, CHUNK)], query[:ROWS]) * SCALE2
-            mark = marks[pl.ds(start, CHUNK)]
-            mask = jnp.concatenate([mark] * (ROWS // 128), axis=1) == names
-            if same:
-                mask = mask & (iota((CHUNK, ROWS), 0) + start != iota((CHUNK, ROWS), 1))
-            sims = jnp.where(mask, sims, NEGATIVE)
-            scores[pl.ds(pl.multiple_of(k * ROWS + start, CHUNK), CHUNK)] = sims
-            return jnp.maximum(top, jnp.max(fold(sims), axis=0))
-
-        top = lax.fori_loop(0, ROWS // CHUNK, score, top)
-    top = jnp.maximum(jnp.max(top, axis=0, keepdims=True), FLOOR)
-
-    def add(i, sums):
-        sims = scores[pl.ds(pl.multiple_of(i * CHUNK, CHUNK), CHUNK)]
-        terms = jnp.exp2(sims - top)
-        return (
-            sums[0] + jnp.sum(fold(terms), axis=0),
-            sums[1] + jnp.sum(fold(terms * sims), axis=0),
-        )
-
-    zero = jnp.zeros((8, ROWS), F32)
-    total, weight = lax.fori_loop(0, len(keys) * ROWS // CHUNK, add, (zero, zero))
-    return top, jnp.sum(total, axis=0, keepdims=True), jnp.sum(weight, axis=0, keepdims=True)
-
-
 def merge(parts):
     top = functools.reduce(jnp.maximum, [p[0] for p in parts])
     factors = [jnp.exp2(p[0] - top) for p in parts]
@@ -191,47 +161,189 @@
     return tuple(ref[k : k + 1] for k in range(3))
 
 
-def pair_kernel(plan, blocks, old, *refs):
-    n_old = len(old)
-    ins, olds = refs[: len(blocks)], refs[len(blocks) : len(blocks) + n_old]
-    outs = refs[len(blocks) + n_old : -2]
-    marks, scores = refs[-2:]
-    where = {b: i for i, b in enumerate(blocks)}
-    used = sorted({k for _, keys in plan for k in keys})
-    for b in used:
-        names = ins[where[b]][ROWS:, :ROWS].astype(F32)
-        marks[where[b]] = jnp.transpose(jnp.broadcast_to(names[:1], (128, ROWS)))
-    before = {b: olds[i] for i, b in enumerate(old)}
-    for out, (q, keys) in zip(outs, plan):
-        stats = column_stats(
-            ins[where[q]], [(ins[where[k]], marks.at[where[k]], k == q) for k in keys], scores
+def spread_names(block):
+    names = block[ROWS:, :ROWS].astype(F32)[:1]
+    return names, jnp.transpose(jnp.broadcast_to(names, (128, ROWS)))
+
+
+def across(mark):
+    return jnp.concatenate([mark] * (ROWS // 128), axis=1)
+
+
+def gather_columns(top, total, weight):
+    best = jnp.max(top, axis=0, keepdims=True)
+    factor = jnp.exp2(top - best)
+    return (
+        best,
+        jnp.sum(total * factor, axis=0, keepdims=True),
+        jnp.sum(weight * factor, axis=0, keepdims=True),
+    )
+
+
+def own_kernel(block, out, scores):
+    names, marks = spread_names(block)
+    top = jnp.full((8, ROWS), FLOOR, F32)
+    for start in range(0, ROWS, CHUNK):
+        sims = dot_nt(block[start : start + CHUNK], block[:ROWS]) * SCALE2
+        mask = (across(marks[start : start + CHUNK]) == names) & (
+            iota((CHUNK, ROWS), 0) + start != iota((CHUNK, ROWS), 1)
         )
-        if q in before:
-            stats = merge([stats, get_stats(before[q])])
-        put_stats(out, stats)
-
-
-def pairs(plan, blocks, old):
-    names, n = list(blocks), len(plan)
-    most = max(len(keys) for _, keys in plan)
-    units = sum(len(keys) for _, keys in plan)
+        sims = jnp.where(mask, sims, NEGATIVE)
+        scores[start : start + CHUNK] = sims
+        top = jnp.maximum(top, jnp.max(fold(sims), axis=0))
+    total = jnp.zeros((8, ROWS), F32)
+    weight = jnp.zeros((8, ROWS), F32)
+    for start in range(0, ROWS, STRIP):
+        sims = scores[start : start + STRIP]
+        terms = jnp.exp2(fold(sims) - top)
+        total += jnp.sum(terms, axis=0)
+        weight += jnp.sum(terms * fold(sims), axis=0)
+    put_stats(out, gather_columns(top, total, weight))
+
+
+def own_pairs(block):
+    return pl.pallas_call(
+        own_kernel,
+        out_shape=jax.ShapeDtypeStruct((8, ROWS), F32),
+        in_specs=[pl.BlockSpec(memory_space=pltpu.VMEM)],
+        out_specs=pl.BlockSpec(memory_space=pltpu.VMEM),
+        scratch_shapes=[pltpu.VMEM((ROWS, ROWS), F32)],
+        compiler_params=params(),
+        cost_estimate=pl.CostEstimate(
+            flops=2 * ROWS * ROWS * WIDTH,
+            bytes_accessed=2 * BLOCK * WIDTH,
+            transcendentals=ROWS * ROWS,
+        ),
+        name="own",
+    )(block)
+
+
+def pair_kernel(plan, blocks, old, half_ref, *refs):
+    n, n_old = len(blocks), len(old)
+    ins, olds = refs[:n], refs[n : n + n_old]
+    outs = refs[n + n_old : n + n_old + n]
+    held, marks, names, rows, tops, totals, weights, scores0, scores1, sems = refs[n + n_old + n :]
+    scores = (scores0, scores1)
+    place = {b: i for i, b in enumerate(blocks)}
+    copies = [pltpu.make_async_copy(ins[i], held.at[i], sems.at[i]) for i in range(n)]
+    for copy in copies:
+        copy.start()
+    lane = iota((1, 128), 1)
+    empty = jnp.where(lane % 4 == 0, NEGATIVE, 0.0)
+    for i in range(n):
+        rows[i] = jnp.broadcast_to(empty, (ROWS, 128))
+    tops[...] = jnp.full((n, 8, ROWS), FLOOR, F32)
+    totals[...] = jnp.zeros((n, 8, ROWS), F32)
+    weights[...] = jnp.zeros((n, 8, ROWS), F32)
+    ready = set()
+
+    def need(i):
+        if i not in ready:
+            ready.add(i)
+            copies[i].wait()
+            one, many = spread_names(held.at[i])
+            names[i] = jnp.broadcast_to(one, (8, ROWS))
+            marks[i] = many
+
+    steps = []
+    for k, (left, right, axis) in enumerate(plan):
+        left, right = place[left], place[right]
+        if axis is None:
+            steps += [(k, left, right, 0, (left, right)), (k, left, right, HALF, (left, right))]
+        else:
+            half = half_ref[axis]
+            first = jnp.where(half == 0, left, right)
+            second = jnp.where(half == 0, right, left)
+            start = pl.multiple_of(half * HALF, HALF)
+            steps.append((k, first, second, start, (left, right)))
+
+    def product(step, out):
+        _, left, right, start, both = step
+        for i in both:
+            need(i)
+        out[...] = dot_nt(held[left, pl.ds(start, HALF)], held[right, :ROWS])
+
+    def reduce(step, data):
+        k, left, right, start, _ = step
+        name = names[right][:1]
+        top = tops[right]
+        peak = top
+        for at in range(0, HALF, STRIP):
+            here = pl.ds(start + at, STRIP)
+            mask = across(marks[left, here]) == name
+            sims = jnp.where(mask, data[at : at + STRIP] * SCALE2, NEGATIVE)
+            data[at : at + STRIP] = sims
+            peak = jnp.maximum(peak, jnp.max(fold(sims), axis=0))
+            best = jnp.maximum(jnp.max(sims, axis=1, keepdims=True), FLOOR)
+            terms = jnp.exp2(sims - best)
+            total = jnp.sum(terms, axis=1, keepdims=True)
+            weight = jnp.sum(terms * sims, axis=1, keepdims=True)
+            rows[left, here] = jnp.where(
+                lane == 4 * k,
+                best,
+                jnp.where(
+                    lane == 4 * k + 1, total, jnp.where(lane == 4 * k + 2, weight, rows[left, here])
+                ),
+            )
+        factor = jnp.exp2(top - peak)
+        total = totals[right] * factor
+        weight = weights[right] * factor
+        for at in range(0, HALF, STRIP):
+            sims = fold(data[at : at + STRIP])
+            terms = jnp.exp2(sims - peak)
+            total += jnp.sum(terms, axis=0)
+            weight += jnp.sum(terms * sims, axis=0)
+        tops[right] = peak
+        totals[right] = total
+        weights[right] = weight
+
+    product(steps[0], scores[0])
+    for t, step in enumerate(steps):
+        if t + 1 < len(steps):
+            product(steps[t + 1], scores[(t + 1) % 2])
+        reduce(step, scores[t % 2])
+
+    for i, b in enumerate(blocks):
+        parts = [gather_columns(tops[i], totals[i], weights[i])]
+        mine = [k for k, (left, right, axis) in enumerate(plan) if left == b or (axis is not None and right == b)]
+        if mine:
+            turned = jnp.transpose(rows[i])
+            parts += [tuple(turned[4 * k + j : 4 * k + j + 1] for j in range(3)) for k in mine]
+        if b in old:
+            parts.append(get_stats(olds[old.index(b)]))
+        put_stats(outs[i], merge(parts))
+
+
+def pairs(plan, blocks, old, halves):
+    names, n = list(blocks), len(blocks)
+    steps = sum(2 if axis is None else 1 for _, _, axis in plan)
+    anywhere = pl.BlockSpec(memory_space=pl.ANY)
+    vmem = pl.BlockSpec(memory_space=pltpu.VMEM)
     return pl.pallas_call(
         functools.partial(pair_kernel, plan, names, list(old)),
         out_shape=[jax.ShapeDtypeStruct((8, ROWS), F32)] * n,
-        in_specs=[pl.BlockSpec(memory_space=pltpu.VMEM)] * (len(blocks) + len(old)),
-        out_specs=[pl.BlockSpec(memory_space=pltpu.VMEM)] * n,
+        in_specs=[pl.BlockSpec(memory_space=pltpu.SMEM)] + [anywhere] * n + [vmem] * len(old),
+        out_specs=[vmem] * n,
         scratch_shapes=[
-            pltpu.VMEM((len(blocks), ROWS, 128), F32),
-            pltpu.VMEM((most * ROWS, ROWS), F32),
+            pltpu.VMEM((n, BLOCK, WIDTH), BF),
+            pltpu.VMEM((n, ROWS, 128), F32),
+            pltpu.VMEM((n, 8, ROWS), F32),
+            pltpu.VMEM((n, ROWS, 128), F32),
+            pltpu.VMEM((n, 8, ROWS), F32),
+            pltpu.VMEM((n, 8, ROWS), F32),
+            pltpu.VMEM((n, 8, ROWS), F32),
+            pltpu.VMEM((HALF, ROWS), F32),
+            pltpu.VMEM((HALF, ROWS), F32),
+            pltpu.SemaphoreType.DMA((n,)),
         ],
         compiler_params=params(),
         cost_estimate=pl.CostEstimate(
-            flops=2 * units * ROWS * ROWS * WIDTH,
-            bytes_accessed=2 * len(blocks) * BLOCK * WIDTH,
-            transcendentals=units * ROWS * ROWS,
+            flops=2 * steps * HALF * ROWS * WIDTH,
+            bytes_accessed=2 * n * BLOCK * WIDTH,
+            transcendentals=2 * steps * HALF * ROWS,
         ),
         name="pairs",
-    )(*blocks.values(), *old.values())
+    )(halves, *blocks.values(), *old.values())
 
 
 def spread_kernel(offset_ref, *refs):
@@ -272,15 +384,15 @@
         found += dot(jnp.concatenate([high, mid, low], axis=0).astype(BF), pick)
     found = found[:8] + (found[8:16] + found[16:])
     best = found[:1]
-    best_ref[...] = best
-    mean_ref[...] = found[1:2]
-    flag_ref[...] = 1.0 / (1.0 + jnp.exp(-SHARPNESS * (best - THRESHOLD)))
+    best_ref[...] = best.reshape(ROWS)
+    mean_ref[...] = found[1:2].reshape(ROWS)
+    flag_ref[...] = (1.0 / (1.0 + jnp.exp(-SHARPNESS * (best - THRESHOLD)))).reshape(ROWS)
 
 
 def unpack(back, labels, rank):
     return pl.pallas_call(
         unpack_kernel,
-        out_shape=[jax.ShapeDtypeStruct((1, ROWS), F32)] * 3,
+        out_shape=[jax.ShapeDtypeStruct((ROWS,), F32)] * 3,
         in_specs=[pl.BlockSpec(memory_space=pltpu.VMEM)] * 3,
         out_specs=[pl.BlockSpec(memory_space=pltpu.VMEM)] * 3,
         compiler_params=params(),
@@ -301,33 +413,32 @@
 
 
 PLACES = {"O": (0, 0), "A": (1, 0), "B": (2, 0), "C": (0, 1), "D": (0, -1), "E": (0, 2)}
-NEAR = [("O", "OAC"), ("A", "OCD"), ("C", "OA"), ("D", "AC")]
-FAR = [("O", "B"), ("A", "E"), ("B", "CE"), ("C", "B"), ("E", "A")]
+NEAR = [("O", "A", None), ("O", "C", None), ("A", "C", None), ("D", "A", None), ("C", "D", 1)]
+FAR = [("B", "O", 0), ("B", "C", None), ("E", "A", None), ("E", "B", 0)]
 
 
 def per_device(embeddings, labels):
     lab = labels.reshape(1, ROWS)
+    tc = lax.axis_index("tc")
+    halves = jnp.stack([tc // (2 * SIDE), (tc % SIDE) // 2]).astype(jnp.int32)
     packed, rank = pack(embeddings, lab)
     got = lax.all_to_all(packed, "tr", split_axis=0, concat_axis=0, tiled=True)
     mine, offsets = compact(got)
     a = shift(mine, -1, 0)
     c = shift(mine, 0, -1)
     d = shift(mine, 0, 1)
+    own = own_pairs(mine)
     b = shift(a, -1, 0)
     e = shift(d, 0, 1)
-    near = pairs(NEAR, {"O": mine, "A": a, "C": c, "D": d}, {})
-    stats = dict(zip([q for q, _ in NEAR], near))
-    far = pairs(
-        FAR,
-        {"O": mine, "A": a, "B": b, "C": c, "E": e},
-        {q: stats[q] for q in "OAC"},
-    )
-    stats.update(zip([q for q, _ in FAR], far))
+    blocks = {"O": mine, "A": a, "C": c, "D": d}
+    stats = dict(zip(blocks, pairs(NEAR, blocks, {"O": own}, halves)))
+    blocks = {"O": mine, "B": b, "C": c, "E": e, "A": a}
+    far = pairs(FAR, blocks, {q: stats[q] for q in "OAC"}, halves)
+    stats.update(zip(blocks, far))
     parts = [stats["O"]] + [shift(stats[q], *PLACES[q]) for q in "ABCDE"]
     sent = spread(offsets, parts)
     back = lax.all_to_all(sent, "tr", split_axis=0, concat_axis=0, tiled=True)
-    outs = unpack(back, lab, rank)
-    return tuple(o.reshape(ROWS) for o in outs)
+    return unpack(back, lab, rank)
 
 
 def solution(mesh):

time: 206 us -> 184 us (0.89)
  Pallas kernels: 68.8 us -> 50.7 us
  other arithmetic: 3.84 us -> 0.61 us
  local copies, waits for them, and re-layouts: 5.35 us -> 3.06 us
    pallas_call x2, Pallas kernels: 46.8 us -> 24.8 us  [pairs(): pl.pallas_call(functools.partial(pair_kernel, plan, names, list(old)), ou...]
    pallas_call x1 -> x2, Pallas kernels: 2.39 us -> 6.33 us  [the longest x1 3.96 us: own_pairs(): pl.pallas_call(own_kernel, out_shape=jax.ShapeDtypeStruct((8, ROWS), F32)...]
    pallas_call x3 -> x0, other arithmetic: 3.84 us -> none  [unpack(): pl.pallas_call(unpack_kernel, out_shape=[jax.ShapeDtypeStruct((1, ROWS),...]
    unnamed x20 -> x14, local copies, waits for them, and re-layouts: 4.08 us -> 1.78 us
  transfers between devices with their start and end apart: 10 -> 10, of which waited for: 4 -> 5; matrix products, arithmetic and copies ran while one was open for 0% -> 0% of each run, Pallas kernels for 23% -> 16%
where the time goes in v2:
time: 184 us; the launch traced here: 183 us
  blocking collectives  74.1 us (40%)
  Pallas kernels  50.7 us (28%)
  waiting for transfers between devices  37.4 us (20%)
  starting transfers between devices  16.3 us (9%)
  local copies, waits for them, and re-layouts  3.06 us (2%)
    all_to_all x1, blocking collectives, per_device(): got = lax.all_to_all(packed, 'tr', split_axis=0, concat_axis=0, tiled=True)  64.3 us
    ppermute x10, waiting for transfers between devices, shift(): return lax.ppermute(array, ('tr', 'tc'), moves)  37.4 us
    pallas_call x2, Pallas kernels, pairs(): pl.pallas_call(functools.partial(pair_kernel, plan, names, list(old)), ou...  24.8 us
    ppermute x10, starting transfers between devices, shift(): return lax.ppermute(array, ('tr', 'tc'), moves)  16.3 us
    all_to_all x1, blocking collectives, per_device(): back = lax.all_to_all(sent, 'tr', split_axis=0, concat_axis=0, tiled=True)  9.76 us
    pallas_call x1, Pallas kernels, pack(): pl.pallas_call(pack_kernel, grid=(TILE_ROWS,), in_specs=[whole((ROWS, WID...  9.19 us
    pallas_call x1, Pallas kernels, compact(): pl.pallas_call(compact_kernel, grid=(TILE_ROWS,), in_specs=[pl.BlockSpec(...  8.72 us
    pallas_call x1, Pallas kernels, own_pairs(): pl.pallas_call(own_kernel, out_shape=jax.ShapeDtypeStruct((8, ROWS), F32)...  3.96 us
  transfers between devices with their start and end apart: 10, of which 5 were waited for; matrix products, arithmetic and copies ran while one was open for 0% of the time, Pallas kernels for 16%

profile of v2, /device:TPU:2, one launch (start us, length us, event | category | flops | bytes accessed | tf_op | source)
XLA Modules:
  0.0 182.8 jit_solution(3231129181506660533)
XLA Ops:
  0.6 1.3 reshape.9.lab_ref
  1.9 9.2 %pack.1 = (bf16[8,304,1024]{2,1,0:T(8,128)(2,1)}, s32[1,768]{1,0:T(1,128)}) custom-call(bf16[768,1024]{1,0:T(8,128)(2,1)} %emb_ref.1, s32[1,768]{1,0:T(1,128)} %reshape.9.lab_ref), custom_call_target="tpu_custom_call" | custom-call | tf_op jit(solution)/shard_map/pack/pallas_call | solution.py:78
  11.1 64.3 %all_to_all.10.got_ref = bf16[8,304,1024]{2,1,0:T(8,128)(2,1)} all-to-all(bf16[8,304,1024]{2,1,0:T(8,128)(2,1)} %get-tuple-element.16), channel_id=1, replica_groups=mesh['tr'=8,'tc'=16] {'tr'}, dimensions={0} | all-to-all | bytes 9961472 | tf_op jit(solution)/shard_map/all_to_all | solution.py:425
  75.4 8.7 %compact.1 = (bf16[784,1024]{1,0:T(8,128)(2,1)}, s32[8]{0:T(128)}) custom-call(bf16[8,304,1024]{2,1,0:T(8,128)(2,1)} %all_to_all.10.got_ref), custom_call_target="tpu_custom_call" | custom-call | tf_op jit(solution)/shard_map/compact/pallas_call | solution.py:124
  84.1 0.6 collective-permute-start
  84.7 1.6 collective-permute-start.3
  86.3 1.7 collective-permute-start.2
  88.0 17.2 %collective-permute-done.refs_1_.refs_4_ = bf16[784,1024]{1,0:T(8,128)(2,1)S(1)} collective-permute-done((bf16[784,1024]{1,0:T(8,128)(2,1)}, bf16[784,1024]{1,0:T(8,128)(2,1)S(1)}, u32[]{:S(2)}, u32[]{:S(2)}) %collective-permute-start) | collective-permute-done | bytes 1605664 | tf_op jit(solution)/shard_map/ppermute | solution.py:412
  105.2 0.0 copy-start.5
  105.2 0.9 collective-permute-start.1
  106.1 16.1 %collective-permute-done.3.refs_3_ = bf16[784,1024]{1,0:T(8,128)(2,1)} collective-permute-done((bf16[784,1024]{1,0:T(8,128)(2,1)}, bf16[784,1024]{1,0:T(8,128)(2,1)}, u32[]{:S(2)}, u32[]{:S(2)}) %collective-permute-start.3) | collective-permute-done | bytes 1605664 | tf_op jit(solution)/shard_map/ppermute | solution.py:412
  122.3 1.7 collective-permute-start.4
  124.0 0.6 pad_add_fusion.half_ref
  124.6 4.0 %own.1.refs_4_ = f32[8,768]{1,0:T(8,128)} custom-call(bf16[784,1024]{1,0:T(8,128)(2,1)} %get-tuple-element.18.block.refs_0_), custom_call_target="tpu_custom_call" | custom-call | flops 1207959552 | bytes 1605632 | tf_op jit(solution)/shard_map/own/pallas_call | solution.py:205
  128.6 0.0 copy-done.5
  128.6 0.0 collective-permute-done.2.refs_2_
  128.6 0.0 copy-start.6
  128.6 1.2 copy-done.6
  129.7 13.8 %pairs.2 = (f32[8,768]{1,0:T(8,128)}, f32[8,768]{1,0:T(8,128)}, f32[8,768]{1,0:T(8,128)}, f32[8,768]{1,0:T(8,128)}) custom-call(s32[2]{0:T(128)} %pad_add_fusion.half_ref, bf16[784,1024]{1,0:T(8,128)(2,1)} %get-tuple-element.18.block.refs_0_, bf16[784,1024]{1,0:T(8,128)(2,1)} %copy-done.5, bf16[784,1024]{1,0:T(8,128)(2,1)} %copy-done.6, ...), custom_call_target="tpu_custom_call" | custom-call | flops 5435817984 | bytes 6422528 | tf_op jit(solution)/shard_map/pairs/pallas_call | solution.py:322
  143.5 2.0 %collective-permute-start.8 = (f32[8,768]{1,0:T(8,128)}, f32[8,768]{1,0:T(8,128)S(1)}, u32[]{:S(2)}, u32[]{:S(2)}) collective-permute-start(f32[8,768]{1,0:T(8,128)} %get-tuple-element.26), channel_id=1, source_target_pairs={{0,3},{1,0},{2,1},{3,2},{4,7},{5,4},{6,5},{7,6},{8,11},{9,8},{10,9... | collective-permute-start | bytes 73736 | tf_op jit(solution)/shard_map/ppermute | solution.py:412
  145.5 0.0 collective-permute-done.1.refs_1_
  145.5 0.0 collective-permute-done.4.refs_3_
  145.5 11.0 %pairs.3 = (f32[8,768]{1,0:T(8,128)}, f32[8,768]{1,0:T(8,128)}, f32[8,768]{1,0:T(8,128)}, f32[8,768]{1,0:T(8,128)}, f32[8,768]{1,0:T(8,128)}) custom-call(s32[2]{0:T(128)} %pad_add_fusion.half_ref, bf16[784,1024]{1,0:T(8,128)(2,1)} %get-tuple-element.18.block.refs_0_, bf16[784,1024]{1,0:T(8,128)(2,1)} %collective-permute-done.1.refs_1_, ...), custom_call_target="tpu_custom_call" | custom-call | flops 3623878656 | bytes 8028160 | tf_op jit(solution)/shard_map/pairs/pallas_call | solution.py:322
  156.5 1.7 collective-permute-start.5
  158.2 4.7 %collective-permute-start.6 = (f32[8,768]{1,0:T(8,128)}, f32[8,768]{1,0:T(8,128)S(1)}, u32[]{:S(2)}, u32[]{:S(2)}) collective-permute-start(f32[8,768]{1,0:T(8,128)} %get-tuple-element.24), channel_id=1, source_target_pairs={{0,8},{1,9},{2,10},{3,11},{4,12},{5,13},{6,14},{7,15},{8,0},{9,1},... | collective-permute-start | bytes 73736 | tf_op jit(solution)/shard_map/ppermute | solution.py:412
  162.9 0.0 collective-permute-start.7
  162.9 1.5 collective-permute-start.9
  164.4 0.0 collective-permute-done.8.refs_4_
  164.4 0.0 copy-start
  164.4 0.0 collective-permute-done.5.refs_1_
  164.4 0.0 copy-start.1
  164.4 0.5 collective-permute-done.6.refs_2_
  164.9 0.0 copy-start.2
  164.9 3.2 %collective-permute-done.7.refs_3_ = f32[8,768]{1,0:T(8,128)S(1)} collective-permute-done((f32[8,768]{1,0:T(8,128)}, f32[8,768]{1,0:T(8,128)S(1)}, u32[]{:S(2)}, u32[]{:S(2)}) %collective-permute-start.7) | collective-permute-done | bytes 24608 | tf_op jit(solution)/shard_map/ppermute | solution.py:412
  168.2 0.0 copy-start.3
  168.2 0.3 collective-permute-done.9.refs_5_
  168.5 0.0 copy-start.4
  168.5 0.0 copy-done
  168.5 0.0 copy-done.1
  168.5 0.0 copy-done.2
  168.5 0.3 copy-done.3
  168.8 0.3 copy-done.4
  169.1 1.6 spread.1
  170.7 9.8 %all_to_all.11.back_ref = f32[8,8,384]{2,1,0:T(8,128)} all-to-all(f32[8,8,384]{2,1,0:T(8,128)} %spread.1), channel_id=1, replica_groups=mesh['tr'=8,'tc'=16] {'tr'}, dimensions={0} | all-to-all | bytes 196608 | tf_op jit(solution)/shard_map/all_to_all | solution.py:440
  180.5 2.4 %unpack.1 = (f32[768]{0:T(1024)}, f32[768]{0:T(1024)}, f32[768]{0:T(1024)}) custom-call(f32[8,8,384]{2,1,0:T(8,128)} %all_to_all.11.back_ref, s32[1,768]{1,0:T(1,128)} %reshape.9.lab_ref, s32[1,768]{1,0:T(1,128)} %get-tuple-element.28.rank_ref), custom_call_target="tpu_custom_call" | custom-call | tf_op jit(solution)/shard_map/unpack/pallas_call | solution.py:393
Async XLA Ops:
  84.1 21.0 %collective-permute-start = (bf16[784,1024]{1,0:T(8,128)(2,1)}, bf16[784,1024]{1,0:T(8,128)(2,1)S(1)}, u32[]{:S(2)}, u32[]{:S(2)}) collective-permute-start(bf16[784,1024]{1,0:T(8,128)(2,1)} %get-tuple-element.18.block.refs_0_), channel_id=1, source_target_pairs={{0,12},{1,13},{2,14},{3,15},{4,0},{5,1},{6,2},{7,3},{8,4},{9,5},{1... | collective-permute-start | bytes 4816904 | tf_op jit(solution)/shard_map/ppermute | solution.py:412
  84.7 37.5 %collective-permute-start.3 = (bf16[784,1024]{1,0:T(8,128)(2,1)}, bf16[784,1024]{1,0:T(8,128)(2,1)}, u32[]{:S(2)}, u32[]{:S(2)}) collective-permute-start(bf16[784,1024]{1,0:T(8,128)(2,1)} %get-tuple-element.18.block.refs_0_), channel_id=1, source_target_pairs={{0,1},{1,2},{2,3},{3,0},{4,5},{5,6},{6,7},{7,4},{8,9},{9,10},{10,1... | collective-permute-start | bytes 4816904 | tf_op jit(solution)/shard_map/ppermute | solution.py:412
  86.3 42.3 %collective-permute-start.2 = (bf16[784,1024]{1,0:T(8,128)(2,1)}, bf16[784,1024]{1,0:T(8,128)(2,1)S(1)}, u32[]{:S(2)}, u32[]{:S(2)}) collective-permute-start(bf16[784,1024]{1,0:T(8,128)(2,1)} %get-tuple-element.18.block.refs_0_), channel_id=1, source_target_pairs={{0,3},{1,0},{2,1},{3,2},{4,7},{5,4},{6,5},{7,6},{8,11},{9,8},{10,9... | collective-permute-start | bytes 4816904 | tf_op jit(solution)/shard_map/ppermute | solution.py:412
  105.2 23.4 %copy-start.5 = (bf16[784,1024]{1,0:T(8,128)(2,1)}, bf16[784,1024]{1,0:T(8,128)(2,1)S(1)}, u32[]{:S(2)}) copy-start(bf16[784,1024]{1,0:T(8,128)(2,1)S(1)} %collective-permute-done.refs_1_.refs_4_) | copy-start | bytes 4816900
  105.2 40.3 %collective-permute-start.1 = (bf16[784,1024]{1,0:T(8,128)(2,1)S(1)}, bf16[784,1024]{1,0:T(8,128)(2,1)}, u32[]{:S(2)}, u32[]{:S(2)}) collective-permute-start(bf16[784,1024]{1,0:T(8,128)(2,1)S(1)} %collective-permute-done.refs_1_.refs_4_), channel_id=1, source_target_pairs={{0,12},{1,13},{2,14},{3,15},{4,0},{5,1},{6,2},{7,3},{8,4},{9,5},{1... | collective-permute-start | bytes 4816904 | tf_op jit(solution)/shard_map/ppermute | solution.py:412
  122.3 23.2 %collective-permute-start.4 = (bf16[784,1024]{1,0:T(8,128)(2,1)}, bf16[784,1024]{1,0:T(8,128)(2,1)}, u32[]{:S(2)}, u32[]{:S(2)}) collective-permute-start(bf16[784,1024]{1,0:T(8,128)(2,1)} %collective-permute-done.3.refs_3_), channel_id=1, source_target_pairs={{0,1},{1,2},{2,3},{3,0},{4,5},{5,6},{6,7},{7,4},{8,9},{9,10},{10,1... | collective-permute-start | bytes 4816904 | tf_op jit(solution)/shard_map/ppermute | solution.py:412
  128.6 1.2 copy-start.6
  143.5 20.9 %collective-permute-start.8 = (f32[8,768]{1,0:T(8,128)}, f32[8,768]{1,0:T(8,128)S(1)}, u32[]{:S(2)}, u32[]{:S(2)}) collective-permute-start(f32[8,768]{1,0:T(8,128)} %get-tuple-element.26), channel_id=1, source_target_pairs={{0,3},{1,0},{2,1},{3,2},{4,7},{5,4},{6,5},{7,6},{8,11},{9,8},{10,9... | collective-permute-start | bytes 73736 | tf_op jit(solution)/shard_map/ppermute | solution.py:412
  156.5 7.9 %collective-permute-start.5 = (f32[8,768]{1,0:T(8,128)}, f32[8,768]{1,0:T(8,128)S(1)}, u32[]{:S(2)}, u32[]{:S(2)}) collective-permute-start(f32[8,768]{1,0:T(8,128)} %get-tuple-element.23), channel_id=1, source_target_pairs={{0,4},{1,5},{2,6},{3,7},{4,8},{5,9},{6,10},{7,11},{8,12},{9,13},{1... | collective-permute-start | bytes 73736 | tf_op jit(solution)/shard_map/ppermute | solution.py:412
  158.2 6.7 %collective-permute-start.6 = (f32[8,768]{1,0:T(8,128)}, f32[8,768]{1,0:T(8,128)S(1)}, u32[]{:S(2)}, u32[]{:S(2)}) collective-permute-start(f32[8,768]{1,0:T(8,128)} %get-tuple-element.24), channel_id=1, source_target_pairs={{0,8},{1,9},{2,10},{3,11},{4,12},{5,13},{6,14},{7,15},{8,0},{9,1},... | collective-permute-start | bytes 73736 | tf_op jit(solution)/shard_map/ppermute | solution.py:412
  162.9 5.2 %collective-permute-start.7 = (f32[8,768]{1,0:T(8,128)}, f32[8,768]{1,0:T(8,128)S(1)}, u32[]{:S(2)}, u32[]{:S(2)}) collective-permute-start(f32[8,768]{1,0:T(8,128)} %get-tuple-element.25), channel_id=1, source_target_pairs={{0,1},{1,2},{2,3},{3,0},{4,5},{5,6},{6,7},{7,4},{8,9},{9,10},{10,1... | collective-permute-start | bytes 73736 | tf_op jit(solution)/shard_map/ppermute | solution.py:412
  162.9 5.5 %collective-permute-start.9 = (f32[8,768]{1,0:T(8,128)}, f32[8,768]{1,0:T(8,128)S(1)}, u32[]{:S(2)}, u32[]{:S(2)}) collective-permute-start(f32[8,768]{1,0:T(8,128)} %get-tuple-element.27), channel_id=1, source_target_pairs={{0,2},{1,3},{2,0},{3,1},{4,6},{5,7},{6,4},{7,5},{8,10},{9,11},{10,... | collective-permute-start | bytes 73736 | tf_op jit(solution)/shard_map/ppermute | solution.py:412
  164.4 4.0 %copy-start = (f32[8,768]{1,0:T(8,128)}, f32[8,768]{1,0:T(8,128)S(1)}, u32[]{:S(2)}) copy-start(f32[8,768]{1,0:T(8,128)S(1)} %collective-permute-done.8.refs_4_) | copy-start | bytes 73732
  164.4 4.0 %copy-start.1 = (f32[8,768]{1,0:T(8,128)}, f32[8,768]{1,0:T(8,128)S(1)}, u32[]{:S(2)}) copy-start(f32[8,768]{1,0:T(8,128)S(1)} %collective-permute-done.5.refs_1_) | copy-start | bytes 73732
  164.9 3.5 %copy-start.2 = (f32[8,768]{1,0:T(8,128)}, f32[8,768]{1,0:T(8,128)S(1)}, u32[]{:S(2)}) copy-start(f32[8,768]{1,0:T(8,128)S(1)} %collective-permute-done.6.refs_2_) | copy-start | bytes 73732
  168.2 0.6 copy-start.3
  168.5 0.6 copy-start.4

commit v3 on v2

--- a/solution.py
+++ b/solution.py
@@ -12,10 +12,12 @@
 SIDE = 4
 ROWS = 768
 WIDTH = 1024
+PIECE = 512
 CAP = 288
-PAIR = 304
+TAIL = 16
+PAIR = CAP + TAIL
 LANES = 384
-BLOCK = ROWS + 16
+BLOCK = ROWS + TAIL
 SPAN = 1152
 EPSILON = 1e-06
 THRESHOLD = 0.3
@@ -51,93 +53,157 @@
     return pl.BlockSpec(shape, lambda *_: (0,) * len(shape))
 
 
-def pack_kernel(emb_ref, lab_ref, out_ref, rank_ref, unit):
+def vmem():
+    return pl.BlockSpec(memory_space=pltpu.VMEM)
+
+
+def smem():
+    return pl.BlockSpec(memory_space=pltpu.SMEM)
+
+
+def pick(lab_ref, rank_ref, g, slots):
+    owner = lax.shift_right_logical(lab_ref[...].reshape(1, ROWS), GROUP_SHIFT)
+    slot = jnp.where(owner == g, rank_ref[...], -1)
+    return (iota((slots, ROWS), 0) == slot).astype(F32).astype(BF)
+
+
+def pack_first_kernel(emb_ref, lab_ref, out_ref, rank_ref, rest_ref, unit):
     g = pl.program_id(0)
-    lab = lab_ref[...]
-    owner = lax.shift_right_logical(lab, GROUP_SHIFT)
+    lab = lab_ref[...].reshape(1, ROWS)
 
     @pl.when(g == 0)
     def _():
         values = emb_ref[...].astype(F32)
         total = jnp.sum(values * values, axis=1, keepdims=True)
-        unit[...] = (values * lax.rsqrt(total + EPSILON)).astype(BF)
+        rows = (values * lax.rsqrt(total + EPSILON)).astype(BF)
+        unit[...] = rows[:, :PIECE]
+        rest_ref[...] = rows[:, PIECE:]
+        owner = lax.shift_right_logical(lab, GROUP_SHIFT)
         onehot = (iota((TILE_ROWS, ROWS), 0) == owner).astype(F32)
         before = (iota((ROWS, ROWS), 0) < iota((ROWS, ROWS), 1)).astype(F32).astype(BF)
         seen = dot(onehot.astype(BF), before)
         rank_ref[...] = jnp.sum(onehot * seen, axis=0, keepdims=True).astype(jnp.int32)
 
-    slot = jnp.where(owner == g, rank_ref[...], -1)
-    pick = (iota((LANES, ROWS), 0) == slot).astype(F32).astype(BF)
-    out_ref[0] = dot(pick[:PAIR], unit[...]).astype(BF)
-    marks = jnp.broadcast_to(lab.astype(F32) + 1.0, (16, ROWS)).astype(BF)
-    out_ref[0, CAP:, :LANES] = (dot_nt(marks, pick) - 1.0).astype(BF)
-    out_ref[0, CAP:, LANES:] = jnp.zeros((16, WIDTH - LANES), BF)
-
-
-def pack(embeddings, labels):
-    return pl.pallas_call(
-        pack_kernel,
+    chosen = pick(lab_ref, rank_ref, g, LANES)
+    out_ref[0] = dot(chosen[:PAIR], unit[...]).astype(BF)
+    marks = jnp.broadcast_to(lab.astype(F32) + 1.0, (TAIL, ROWS)).astype(BF)
+    out_ref[0, CAP:, :LANES] = (dot_nt(marks, chosen) - 1.0).astype(BF)
+    out_ref[0, CAP:, LANES:] = jnp.zeros((TAIL, PIECE - LANES), BF)
+
+
+def pack_first(embeddings, labels):
+    return pl.pallas_call(
+        pack_first_kernel,
         grid=(TILE_ROWS,),
-        in_specs=[whole((ROWS, WIDTH)), whole((1, ROWS))],
-        out_specs=[pl.BlockSpec((1, PAIR, WIDTH), lambda g: (g, 0, 0)), whole((1, ROWS))],
+        in_specs=[whole((ROWS, WIDTH)), whole((ROWS,))],
+        out_specs=[
+            pl.BlockSpec((1, PAIR, PIECE), lambda g: (g, 0, 0)),
+            whole((1, ROWS)),
+            whole((ROWS, WIDTH - PIECE)),
+        ],
         out_shape=[
-            jax.ShapeDtypeStruct((TILE_ROWS, PAIR, WIDTH), BF),
+            jax.ShapeDtypeStruct((TILE_ROWS, PAIR, PIECE), BF),
             jax.ShapeDtypeStruct((1, ROWS), jnp.int32),
+            jax.ShapeDtypeStruct((ROWS, WIDTH - PIECE), BF),
         ],
-        scratch_shapes=[pltpu.VMEM((ROWS, WIDTH), BF)],
-        compiler_params=params(),
-        name="pack",
+        scratch_shapes=[pltpu.VMEM((ROWS, PIECE), BF)],
+        compiler_params=params(),
+        name="pack_first",
     )(embeddings, labels)
 
 
-def compact_kernel(got_ref, out_ref, offset_ref, rows, names, place):
-    r = pl.program_id(0)
-
-    @pl.when(r == 0)
-    def _():
-        place[0] = 0
-        rows[:16] = jnp.zeros((16, WIDTH), BF)
-        names[...] = jnp.zeros((8, SPAN), F32)
-
-    offset = place[0]
-    offset_ref[r] = offset
-    lab = got_ref[0, CAP:, :LANES].astype(F32)[:8]
-    count = jnp.sum((lab[:1] >= 0.0).astype(F32)).astype(jnp.int32)
-    place[0] = offset + count
-    base = pl.multiple_of(lax.div(offset, 16) * 16, 16)
-    column = iota((PAIR, PAIR), 1)
-    move = (iota((PAIR, PAIR), 0) == column + (offset - base)) & (column < count)
-    moved = dot(move.astype(F32).astype(BF), got_ref[0]).astype(BF)
-    rows[pl.ds(base, 16)] = rows[pl.ds(base, 16)] + moved[:16]
-    rows[pl.ds(base + 16, PAIR - 16)] = moved[16:]
-    held = jnp.concatenate([jnp.maximum(lab, 0.0), jnp.zeros((8, SPAN - LANES), F32)], axis=1)
-    names[...] += pltpu.roll(held, offset, 1)
-
-    @pl.when(r == TILE_ROWS - 1)
-    def _():
-        out_ref[:ROWS] = rows[:ROWS]
-        out_ref[ROWS:, :ROWS] = jnp.broadcast_to(names[:1, :ROWS], (16, ROWS)).astype(BF)
-        out_ref[ROWS:, ROWS:] = jnp.zeros((16, WIDTH - ROWS), BF)
-
-
-def compact(got):
-    return pl.pallas_call(
-        compact_kernel,
+def pack_rest_kernel(unit_ref, lab_ref, rank_ref, out_ref):
+    chosen = pick(lab_ref, rank_ref, pl.program_id(0), CAP)
+    out_ref[0] = dot(chosen, unit_ref[...]).astype(BF)
+
+
+def pack_rest(unit, labels, rank):
+    width = unit.shape[1]
+    return pl.pallas_call(
+        pack_rest_kernel,
         grid=(TILE_ROWS,),
-        in_specs=[pl.BlockSpec((1, PAIR, WIDTH), lambda r: (r, 0, 0))],
-        out_specs=[whole((BLOCK, WIDTH)), pl.BlockSpec(memory_space=pltpu.SMEM)],
+        in_specs=[whole((ROWS, width)), whole((ROWS,)), whole((1, ROWS))],
+        out_specs=pl.BlockSpec((1, CAP, width), lambda g: (g, 0, 0)),
+        out_shape=jax.ShapeDtypeStruct((TILE_ROWS, CAP, width), BF),
+        compiler_params=params(),
+        cost_estimate=pl.CostEstimate(
+            flops=2 * TILE_ROWS * CAP * ROWS * width,
+            bytes_accessed=2 * TILE_ROWS * CAP * width,
+            transcendentals=0,
+        ),
+        name="pack_rest",
+    )(unit, labels, rank)
+
+
+def close_gaps(got_ref, rows, offsets, counts):
+    sent = got_ref.shape[1]
+    rows[:16] = jnp.zeros((16, rows.shape[1]), BF)
+    column = iota((PAIR, sent), 1)
+    apart = iota((PAIR, sent), 0) - column
+    for r in range(TILE_ROWS):
+        base = pl.multiple_of(lax.shift_right_logical(offsets[r], 4) * 16, 16)
+        move = (apart == offsets[r] - base) & (column < counts[r])
+        moved = dot(move.astype(F32).astype(BF), got_ref[r]).astype(BF)
+        rows[pl.ds(base, 16)] = rows[pl.ds(base, 16)] + moved[:16]
+        rows[pl.ds(base + 16, PAIR - 16)] = moved[16:]
+
+
+def compact_first_kernel(got_ref, out_ref, place_ref, rows):
+    names = jnp.zeros((8, SPAN), F32)
+    offset = jnp.int32(0)
+    offsets, counts = [], []
+    for r in range(TILE_ROWS):
+        lab = got_ref[r, CAP:, :LANES].astype(F32)[:8]
+        count = jnp.sum((lab[:1] >= 0.0).astype(F32)).astype(jnp.int32)
+        held = jnp.concatenate(
+            [jnp.maximum(lab, 0.0), jnp.zeros((8, SPAN - LANES), F32)], axis=1
+        )
+        names += pltpu.roll(held, offset, 1)
+        place_ref[r] = offset
+        place_ref[TILE_ROWS + r] = count
+        offsets.append(offset)
+        counts.append(count)
+        offset = offset + count
+    close_gaps(got_ref, rows, offsets, counts)
+    out_ref[:ROWS] = rows[:ROWS]
+    second = jnp.concatenate(
+        [names[:, PIECE:ROWS], jnp.zeros((8, 2 * PIECE - ROWS), F32)], axis=1
+    )
+    out_ref[ROWS:] = jnp.concatenate([names[:, :PIECE], second], axis=0).astype(BF)
+
+
+def compact_first(got):
+    return pl.pallas_call(
+        compact_first_kernel,
+        in_specs=[vmem()],
+        out_specs=[vmem(), smem()],
         out_shape=[
-            jax.ShapeDtypeStruct((BLOCK, WIDTH), BF),
-            jax.ShapeDtypeStruct((TILE_ROWS,), jnp.int32),
+            jax.ShapeDtypeStruct((BLOCK, PIECE), BF),
+            jax.ShapeDtypeStruct((2 * TILE_ROWS,), jnp.int32),
         ],
-        scratch_shapes=[
-            pltpu.VMEM((ROWS + PAIR, WIDTH), BF),
-            pltpu.VMEM((8, SPAN), F32),
-            pltpu.SMEM((1,), jnp.int32),
-        ],
-        compiler_params=params(),
-        name="compact",
+        scratch_shapes=[pltpu.VMEM((ROWS + PAIR, PIECE), BF)],
+        compiler_params=params(),
+        name="compact_first",
     )(got)
+
+
+def compact_rest_kernel(place_ref, got_ref, out_ref, rows):
+    places = [place_ref[i] for i in range(2 * TILE_ROWS)]
+    close_gaps(got_ref, rows, places[:TILE_ROWS], places[TILE_ROWS:])
+    out_ref[...] = rows[:ROWS]
+
+
+def compact_rest(place, got):
+    width = got.shape[2]
+    return pl.pallas_call(
+        compact_rest_kernel,
+        in_specs=[smem(), vmem()],
+        out_specs=vmem(),
+        out_shape=jax.ShapeDtypeStruct((ROWS, width), BF),
+        scratch_shapes=[pltpu.VMEM((ROWS + PAIR, width), BF)],
+        compiler_params=params(),
+        name="compact_rest",
+    )(place, got)
 
 
 def fold(tile):
@@ -162,7 +228,8 @@
 
 
 def spread_names(block):
-    names = block[ROWS:, :ROWS].astype(F32)[:1]
+    tail = block[ROWS:].astype(F32)
+    names = jnp.concatenate([tail[:1], tail[8:9, : ROWS - PIECE]], axis=1)
     return names, jnp.transpose(jnp.broadcast_to(names, (128, ROWS)))
 
 
@@ -180,11 +247,12 @@
     )
 
 
-def own_kernel(block, out, scores):
+def own_kernel(block, rest, out, scores):
     names, marks = spread_names(block)
     top = jnp.full((8, ROWS), FLOOR, F32)
     for start in range(0, ROWS, CHUNK):
-        sims = dot_nt(block[start : start + CHUNK], block[:ROWS]) * SCALE2
+        sims = dot_nt(block[start : start + CHUNK], block[:ROWS])
+        sims = (sims + dot_nt(rest[start : start + CHUNK], rest[...])) * SCALE2
         mask = (across(marks[start : start + CHUNK]) == names) & (
             iota((CHUNK, ROWS), 0) + start != iota((CHUNK, ROWS), 1)
         )
@@ -201,12 +269,12 @@
     put_stats(out, gather_columns(top, total, weight))
 
 
-def own_pairs(block):
+def own_pairs(block, rest):
     return pl.pallas_call(
         own_kernel,
         out_shape=jax.ShapeDtypeStruct((8, ROWS), F32),
-        in_specs=[pl.BlockSpec(memory_space=pltpu.VMEM)],
-        out_specs=pl.BlockSpec(memory_space=pltpu.VMEM),
+        in_specs=[vmem(), vmem()],
+        out_specs=vmem(),
         scratch_shapes=[pltpu.VMEM((ROWS, ROWS), F32)],
         compiler_params=params(),
         cost_estimate=pl.CostEstimate(
@@ -215,19 +283,28 @@
             transcendentals=ROWS * ROWS,
         ),
         name="own",
-    )(block)
+    )(block, rest)
 
 
 def pair_kernel(plan, blocks, old, half_ref, *refs):
     n, n_old = len(blocks), len(old)
-    ins, olds = refs[:n], refs[n : n + n_old]
-    outs = refs[n + n_old : n + n_old + n]
-    held, marks, names, rows, tops, totals, weights, scores0, scores1, sems = refs[n + n_old + n :]
+    ins, rests, olds = refs[:n], refs[n : 2 * n], refs[2 * n : 2 * n + n_old]
+    outs = refs[2 * n + n_old : 3 * n + n_old]
+    held, held2, marks, names, rows, tops, totals, weights, scores0, scores1, sems = refs[
+        3 * n + n_old :
+    ]
     scores = (scores0, scores1)
     place = {b: i for i, b in enumerate(blocks)}
-    copies = [pltpu.make_async_copy(ins[i], held.at[i], sems.at[i]) for i in range(n)]
-    for copy in copies:
-        copy.start()
+    copies = [
+        (
+            pltpu.make_async_copy(ins[i], held.at[i], sems.at[2 * i]),
+            pltpu.make_async_copy(rests[i], held2.at[i], sems.at[2 * i + 1]),
+        )
+        for i in range(n)
+    ]
+    for first, second in copies:
+        first.start()
+        second.start()
     lane = iota((1, 128), 1)
     empty = jnp.where(lane % 4 == 0, NEGATIVE, 0.0)
     for i in range(n):
@@ -240,7 +317,8 @@
     def need(i):
         if i not in ready:
             ready.add(i)
-            copies[i].wait()
+            copies[i][0].wait()
+            copies[i][1].wait()
             one, many = spread_names(held.at[i])
             names[i] = jnp.broadcast_to(one, (8, ROWS))
             marks[i] = many
@@ -261,7 +339,10 @@
         _, left, right, start, both = step
         for i in both:
             need(i)
-        out[...] = dot_nt(held[left, pl.ds(start, HALF)], held[right, :ROWS])
+        here = pl.ds(start, HALF)
+        out[...] = dot_nt(held[left, here], held[right, :ROWS]) + dot_nt(
+            held2[left, here], held2[right]
+        )
 
     def reduce(step, data):
         k, left, right, start, _ = step
@@ -318,14 +399,14 @@
     names, n = list(blocks), len(blocks)
     steps = sum(2 if axis is None else 1 for _, _, axis in plan)
     anywhere = pl.BlockSpec(memory_space=pl.ANY)
-    vmem = pl.BlockSpec(memory_space=pltpu.VMEM)
     return pl.pallas_call(
         functools.partial(pair_kernel, plan, names, list(old)),
         out_shape=[jax.ShapeDtypeStruct((8, ROWS), F32)] * n,
-        in_specs=[pl.BlockSpec(memory_space=pltpu.SMEM)] + [anywhere] * n + [vmem] * len(old),
-        out_specs=[vmem] * n,
+        in_specs=[smem()] + [anywhere] * (2 * n) + [vmem()] * len(old),
+        out_specs=[vmem()] * n,
         scratch_shapes=[
-            pltpu.VMEM((n, BLOCK, WIDTH), BF),
+            pltpu.VMEM((n, BLOCK, PIECE), BF),
+            pltpu.VMEM((n, ROWS, WIDTH - PIECE), BF),
             pltpu.VMEM((n, ROWS, 128), F32),
             pltpu.VMEM((n, 8, ROWS), F32),
             pltpu.VMEM((n, ROWS, 128), F32),
@@ -334,7 +415,7 @@
             pltpu.VMEM((n, 8, ROWS), F32),
             pltpu.VMEM((HALF, ROWS), F32),
             pltpu.VMEM((HALF, ROWS), F32),
-            pltpu.SemaphoreType.DMA((n,)),
+            pltpu.SemaphoreType.DMA((2 * n,)),
         ],
         compiler_params=params(),
         cost_estimate=pl.CostEstimate(
@@ -343,7 +424,7 @@
             transcendentals=2 * steps * HALF * ROWS,
         ),
         name="pairs",
-    )(halves, *blocks.values(), *old.values())
+    )(halves, *[b[0] for b in blocks.values()], *[b[1] for b in blocks.values()], *old.values())
 
 
 def spread_kernel(offset_ref, *refs):
@@ -372,16 +453,14 @@
 
 
 def unpack_kernel(back_ref, lab_ref, rank_ref, best_ref, mean_ref, flag_ref):
-    owner = lax.shift_right_logical(lab_ref[...], GROUP_SHIFT)
     found = jnp.zeros((24, ROWS), F32)
     for g in range(TILE_ROWS):
-        slot = jnp.where(owner == g, rank_ref[...], -1)
-        pick = (iota((LANES, ROWS), 0) == slot).astype(F32).astype(BF)
+        chosen = pick(lab_ref, rank_ref, g, LANES)
         values = back_ref[g]
         high = values.astype(BF).astype(F32)
         mid = (values - high).astype(BF).astype(F32)
         low = values - high - mid
-        found += dot(jnp.concatenate([high, mid, low], axis=0).astype(BF), pick)
+        found += dot(jnp.concatenate([high, mid, low], axis=0).astype(BF), chosen)
     found = found[:8] + (found[8:16] + found[16:])
     best = found[:1]
     best_ref[...] = best.reshape(ROWS)
@@ -413,32 +492,47 @@
 
 
 PLACES = {"O": (0, 0), "A": (1, 0), "B": (2, 0), "C": (0, 1), "D": (0, -1), "E": (0, 2)}
-NEAR = [("O", "A", None), ("O", "C", None), ("A", "C", None), ("D", "A", None), ("C", "D", 1)]
+FIRST = [("O", "A", None)]
+NEAR = [("O", "C", None), ("A", "C", None), ("D", "A", None), ("C", "D", 1)]
 FAR = [("B", "O", 0), ("B", "C", None), ("E", "A", None), ("E", "B", 0)]
 
 
 def per_device(embeddings, labels):
-    lab = labels.reshape(1, ROWS)
+    tie = lax.optimization_barrier
     tc = lax.axis_index("tc")
     halves = jnp.stack([tc // (2 * SIDE), (tc % SIDE) // 2]).astype(jnp.int32)
-    packed, rank = pack(embeddings, lab)
-    got = lax.all_to_all(packed, "tr", split_axis=0, concat_axis=0, tiled=True)
-    mine, offsets = compact(got)
-    a = shift(mine, -1, 0)
-    c = shift(mine, 0, -1)
-    d = shift(mine, 0, 1)
-    own = own_pairs(mine)
-    b = shift(a, -1, 0)
-    e = shift(d, 0, 1)
-    blocks = {"O": mine, "A": a, "C": c, "D": d}
-    stats = dict(zip(blocks, pairs(NEAR, blocks, {"O": own}, halves)))
-    blocks = {"O": mine, "B": b, "C": c, "E": e, "A": a}
+
+    def exchange(packed):
+        return lax.all_to_all(packed, "tr", split_axis=0, concat_axis=0, tiled=True)
+
+    packed, rank, unit = pack_first(embeddings, labels)
+    got = exchange(packed)
+    packed = pack_rest(unit, labels, rank)
+    packed, got = tie((packed, got))
+    got_rest = exchange(packed)
+    mine, place = compact_first(got)
+    a, c, d = shift(mine, -1, 0), shift(mine, 0, -1), shift(mine, 0, 1)
+    b, e = shift(a, -1, 0), shift(d, 0, 1)
+    got_rest, a, b, c, d, e = tie((got_rest, a, b, c, d, e))
+    mine2 = compact_rest(place, got_rest)
+    a2, c2, d2 = shift(mine2, -1, 0), shift(mine2, 0, -1), shift(mine2, 0, 1)
+    own = own_pairs(mine, mine2)
+    a2, own, halves = tie((a2, own, halves))
+    b2 = shift(a2, -1, 0)
+    blocks = {"O": (mine, mine2), "A": (a, a2)}
+    stats = dict(zip(blocks, pairs(FIRST, blocks, {"O": own}, halves)))
+    d2, stats["O"] = tie((d2, stats["O"]))
+    e2 = shift(d2, 0, 1)
+    blocks.update(C=(c, c2), D=(d, d2))
+    stats.update(zip(blocks, pairs(NEAR, blocks, stats, halves)))
+    blocks.update(B=(b, b2), E=(e, e2))
+    del blocks["D"]
     far = pairs(FAR, blocks, {q: stats[q] for q in "OAC"}, halves)
     stats.update(zip(blocks, far))
     parts = [stats["O"]] + [shift(stats[q], *PLACES[q]) for q in "ABCDE"]
-    sent = spread(offsets, parts)
-    back = lax.all_to_all(sent, "tr", split_axis=0, concat_axis=0, tiled=True)
-    return unpack(back, lab, rank)
+    sent = spread(place, parts)
+    back = exchange(sent)
+    return unpack(back, labels, rank)
 
 
 def solution(mesh):

time: 184 us -> 169 us (0.918)
  blocking collectives: 74.1 us -> 10.1 us
  waiting for transfers between devices: 37.4 us -> 63.4 us
  starting transfers between devices: 16.3 us -> 32.7 us
  Pallas kernels: 50.7 us -> 58.7 us
    all_to_all x2 -> x1, blocking collectives: 74.1 us -> 10.1 us  [exchange(): return lax.all_to_all(packed, 'tr', split_axis=0, concat_axis=0, tiled=True)]
    all_to_all x0 -> x2, waiting for transfers between devices: none -> 25.4 us  [exchange(): return lax.all_to_all(packed, 'tr', split_axis=0, concat_axis=0, tiled=True)]
    all_to_all x0 -> x2, starting transfers between devices: none -> 9.71 us  [exchange(): return lax.all_to_all(packed, 'tr', split_axis=0, concat_axis=0, tiled=True)]
    ppermute x10 -> x15, starting transfers between devices: 16.3 us -> 23 us  [shift(): return lax.ppermute(array, ('tr', 'tc'), moves)]
    pallas_call x2 -> x4, Pallas kernels: 17.9 us -> 22.4 us  [the longest x1 7.55 us: pack_first(): pl.pallas_call(pack_first_kernel, grid=(TILE_ROWS,), in_specs=[whole((ROW...]
    pallas_call x2 -> x3, Pallas kernels: 24.8 us -> 28.4 us  [pairs(): pl.pallas_call(functools.partial(pair_kernel, plan, names, list(old)), ou...]
    ppermute x10 -> x15, waiting for transfers between devices: 37.4 us -> 38 us  [shift(): return lax.ppermute(array, ('tr', 'tc'), moves)]
  transfers between devices with their start and end apart: 10 -> 17, of which waited for: 5 -> 9; matrix products, arithmetic and copies ran while one was open for 0% -> 0% of each run, Pallas kernels for 16% -> 25%
where the time goes in v3:
time: 169 us; the launch traced here: 168 us
  waiting for transfers between devices  63.4 us (38%)
  Pallas kernels  58.7 us (35%)
  starting transfers between devices  32.7 us (19%)
  blocking collectives  10.1 us (6%)
  local copies, waits for them, and re-layouts  1.81 us (1%)
    ppermute x15, waiting for transfers between devices, shift(): return lax.ppermute(array, ('tr', 'tc'), moves)  38 us
    pallas_call x3, Pallas kernels, pairs(): pl.pallas_call(functools.partial(pair_kernel, plan, names, list(old)), ou...  28.4 us
    all_to_all x2, waiting for transfers between devices, exchange(): return lax.all_to_all(packed, 'tr', split_axis=0, concat_axis=0, tiled=True)  25.4 us
    ppermute x15, starting transfers between devices, shift(): return lax.ppermute(array, ('tr', 'tc'), moves)  23 us
    all_to_all x1, blocking collectives, exchange(): return lax.all_to_all(packed, 'tr', split_axis=0, concat_axis=0, tiled=True)  10.1 us
    all_to_all x2, starting transfers between devices, exchange(): return lax.all_to_all(packed, 'tr', split_axis=0, concat_axis=0, tiled=True)  9.71 us
    pallas_call x1, Pallas kernels, pack_first(): pl.pallas_call(pack_first_kernel, grid=(TILE_ROWS,), in_specs=[whole((ROW...  7.55 us
    pallas_call x1, Pallas kernels, pack_rest(): pl.pallas_call(pack_rest_kernel, grid=(TILE_ROWS,), in_specs=[whole((ROWS...  6.05 us
  transfers between devices with their start and end apart: 17, of which 9 were waited for; matrix products, arithmetic and copies ran while one was open for 0% of the time, Pallas kernels for 25%

profile of v3, /device:TPU:2, one launch (start us, length us, event | category | flops | bytes accessed | tf_op | source)
XLA Modules:
  0.0 168.1 jit_solution(7020590018586439048)
XLA Ops:
  0.6 7.6 %pack_first.1 = (bf16[8,304,512]{2,1,0:T(8,128)(2,1)}, s32[1,768]{1,0:T(1,128)}, bf16[768,512]{1,0:T(8,128)(2,1)}) custom-call(bf16[768,1024]{1,0:T(8,128)(2,1)} %emb_ref.1, s32[768]{0:T(1024)} %lab_ref.5), custom_call_target="tpu_custom_call" | custom-call | tf_op jit(solution)/shard_map/pack_first/pallas_call | solution.py:95
  8.2 5.3 %all-to-all-start = ((bf16[8,304,512]{2,1,0:T(8,128)(2,1)}), bf16[8,304,512]{2,1,0:T(8,128)(2,1)S(1)}, u32[]{:S(2)}, u32[]{:S(2)}) async-start(bf16[8,304,512]{2,1,0:T(8,128)(2,1)} %get-tuple-element.34), calls=%async_computation | async-start | bytes 4980736 | tf_op jit(solution)/shard_map/all_to_all | solution.py:506
  13.5 6.0 %pack_rest.1 = bf16[8,288,512]{2,1,0:T(8,128)(2,1)} custom-call(bf16[768,512]{1,0:T(8,128)(2,1)} %get-tuple-element.32.unit_ref, s32[768]{0:T(1024)} %lab_ref.5, s32[1,768]{1,0:T(1,128)} %get-tuple-element.33.rank_ref), custom_call_target="tpu_custom_call" | custom-call | flops 1811939328 | bytes 2359296 | tf_op jit(solution)/shard_map/pack_rest/pallas_call | solution.py:122
  19.5 25.4 %all-to-all-done.got_ref = bf16[8,304,512]{2,1,0:T(8,128)(2,1)S(1)} async-done(((bf16[8,304,512]{2,1,0:T(8,128)(2,1)}), bf16[8,304,512]{2,1,0:T(8,128)(2,1)S(1)}, u32[]{:S(2)}, u32[]{:S(2)}) %all-to-all-start) | async-done | bytes 2490400 | tf_op jit(solution)/shard_map/all_to_all | solution.py:506
  44.9 0.0 copy-start
  44.9 4.4 %all-to-all-start.1 = ((bf16[8,288,512]{2,1,0:T(8,128)(2,1)}), bf16[8,288,512]{2,1,0:T(8,128)(2,1)}, u32[]{:S(2)}, u32[]{:S(2)}) async-start(bf16[8,288,512]{2,1,0:T(8,128)(2,1)} %pack_rest.1), calls=%async_computation.1 | async-start | bytes 4718592 | tf_op jit(solution)/shard_map/all_to_all | solution.py:506
  49.3 0.0 copy-done
  49.3 4.3 %compact_first.1 = (bf16[784,512]{1,0:T(8,128)(2,1)}, s32[16]{0:T(128)}) custom-call(bf16[8,304,512]{2,1,0:T(8,128)(2,1)} %copy-done), custom_call_target="tpu_custom_call" | custom-call | tf_op jit(solution)/shard_map/compact_first/pallas_call | solution.py:176
  53.6 1.6 collective-permute-start.3
  55.2 0.5 collective-permute-start
  55.8 1.7 collective-permute-start.2
  57.4 15.0 %collective-permute-done.3.refs_3_ = bf16[784,512]{1,0:T(8,128)(2,1)S(1)} collective-permute-done((bf16[784,512]{1,0:T(8,128)(2,1)}, bf16[784,512]{1,0:T(8,128)(2,1)S(1)}, u32[]{:S(2)}, u32[]{:S(2)}) %collective-permute-start.3) | collective-permute-done | bytes 802848 | tf_op jit(solution)/shard_map/ppermute | solution.py:491
  72.5 0.0 copy-start.10
  72.5 2.2 %collective-permute-start.4 = (bf16[784,512]{1,0:T(8,128)(2,1)S(1)}, bf16[784,512]{1,0:T(8,128)(2,1)S(1)}, u32[]{:S(2)}, u32[]{:S(2)}) collective-permute-start(bf16[784,512]{1,0:T(8,128)(2,1)S(1)} %collective-permute-done.3.refs_3_), channel_id=1, source_target_pairs={{0,1},{1,2},{2,3},{3,0},{4,5},{5,6},{6,7},{7,4},{8,9},{9,10},{10,1... | collective-permute-start | bytes 2408456 | tf_op jit(solution)/shard_map/ppermute | solution.py:491
  74.7 0.0 collective-permute-done.refs_1_
  74.7 0.0 copy-start.6
  74.7 0.5 collective-permute-start.1
  75.2 0.0 collective-permute-done.2.refs_2_
  75.2 11.5 %collective-permute-done.4.refs_4_ = bf16[784,512]{1,0:T(8,128)(2,1)S(1)} collective-permute-done((bf16[784,512]{1,0:T(8,128)(2,1)S(1)}, bf16[784,512]{1,0:T(8,128)(2,1)S(1)}, u32[]{:S(2)}, u32[]{:S(2)}) %collective-permute-start.4) | collective-permute-done | bytes 802848 | tf_op jit(solution)/shard_map/ppermute | solution.py:491
  86.7 0.0 copy-done.10
  86.7 0.1 collective-permute-done.1.refs_3_
  86.9 0.0 all-to-all-done.1.got_ref
  86.9 4.5 %compact_rest.1.rest.refs_2_.refs_4_.refs_5_ = bf16[768,512]{1,0:T(8,128)(2,1)} custom-call(s32[16]{0:T(128)} %get-tuple-element.36.place_ref.offset_ref, bf16[8,288,512]{2,1,0:T(8,128)(2,1)} %all-to-all-done.1.got_ref), custom_call_target="tpu_custom_call" | custom-call | tf_op jit(solution)/shard_map/compact_rest/pallas_call | solution.py:198
  91.4 1.2 collective-permute-start.5
  92.6 2.4 %collective-permute-start.8 = (bf16[768,512]{1,0:T(8,128)(2,1)}, bf16[768,512]{1,0:T(8,128)(2,1)}, u32[]{:S(2)}, u32[]{:S(2)}) collective-permute-start(bf16[768,512]{1,0:T(8,128)(2,1)} %compact_rest.1.rest.refs_2_.refs_4_.refs_5_), channel_id=1, source_target_pairs={{0,1},{1,2},{2,3},{3,0},{4,5},{5,6},{6,7},{7,4},{8,9},{9,10},{10,1... | collective-permute-start | bytes 2359304 | tf_op jit(solution)/shard_map/ppermute | solution.py:491
  94.9 0.9 collective-permute-start.6
  95.8 0.6 pad_add_fusion.half_ref
  96.4 3.9 %own.1.refs_4_ = f32[8,768]{1,0:T(8,128)} custom-call(bf16[784,512]{1,0:T(8,128)(2,1)} %get-tuple-element.38.block.refs_0_, bf16[768,512]{1,0:T(8,128)(2,1)} %compact_rest.1.rest.refs_2_.refs_4_.refs_5_), custom_call_target="tpu_custom_call" | custom-call | flops 1207959552 | bytes 1605632 | tf_op jit(solution)/shard_map/own/pallas_call | solution.py:273
  100.3 0.0 copy-done.6
  100.3 0.0 copy-done.7
  100.3 0.0 copy-done.8
  100.3 0.0 copy-done.9
  100.3 3.4 %collective-permute-done.5.refs_3_.refs_5_.refs_6_ = bf16[768,512]{1,0:T(8,128)(2,1)} collective-permute-done((bf16[768,512]{1,0:T(8,128)(2,1)}, bf16[768,512]{1,0:T(8,128)(2,1)}, u32[]{:S(2)}, u32[]{:S(2)}) %collective-permute-start.5) | collective-permute-done | bytes 786464 | tf_op jit(solution)/shard_map/ppermute | solution.py:491
  103.7 5.4 %pairs.3 = (f32[8,768]{1,0:T(8,128)}, f32[8,768]{1,0:T(8,128)}) custom-call(s32[2]{0:T(128)} %pad_add_fusion.half_ref, bf16[784,512]{1,0:T(8,128)(2,1)} %get-tuple-element.38.block.refs_0_, bf16[784,512]{1,0:T(8,128)(2,1)} %copy-done.6, bf16[768,512]{1,0:T(8,128)(2,1)} %compact_rest.1.rest.refs_2_.refs_4_.refs_5_, ...), custom_call_target="tpu_custom_call" | custom-call | flops 1207959552 | bytes 3211264 | tf_op jit(solution)/shard_map/pairs/pallas_call | solution.py:402
  109.1 4.0 %collective-permute-done.8.refs_7_ = bf16[768,512]{1,0:T(8,128)(2,1)} collective-permute-done((bf16[768,512]{1,0:T(8,128)(2,1)}, bf16[768,512]{1,0:T(8,128)(2,1)}, u32[]{:S(2)}, u32[]{:S(2)}) %collective-permute-start.8) | collective-permute-done | bytes 786464 | tf_op jit(solution)/shard_map/ppermute | solution.py:491
  113.0 1.9 %collective-permute-start.9 = (bf16[768,512]{1,0:T(8,128)(2,1)}, bf16[768,512]{1,0:T(8,128)(2,1)S(1)}, u32[]{:S(2)}, u32[]{:S(2)}) collective-permute-start(bf16[768,512]{1,0:T(8,128)(2,1)} %collective-permute-done.8.refs_7_), channel_id=1, source_target_pairs={{0,1},{1,2},{2,3},{3,0},{4,5},{5,6},{6,7},{7,4},{8,9},{9,10},{10,1... | collective-permute-start | bytes 2359304 | tf_op jit(solution)/shard_map/ppermute | solution.py:491
  115.0 1.4 collective-permute-start.7
  116.4 0.0 collective-permute-done.6.refs_6_.refs_7_
  116.4 11.8 %pairs.4 = (f32[8,768]{1,0:T(8,128)}, f32[8,768]{1,0:T(8,128)}, f32[8,768]{1,0:T(8,128)}, f32[8,768]{1,0:T(8,128)}) custom-call(s32[2]{0:T(128)} %pad_add_fusion.half_ref, bf16[784,512]{1,0:T(8,128)(2,1)} %get-tuple-element.38.block.refs_0_, bf16[784,512]{1,0:T(8,128)(2,1)} %copy-done.6, bf16[784,512]{1,0:T(8,128)(2,1)} %copy-done.7, ...), custom_call_target="tpu_custom_call" | custom-call | flops 4227858432 | bytes 6422528 | tf_op jit(solution)/shard_map/pairs/pallas_call | solution.py:402
  128.2 3.5 %collective-permute-start.13 = (f32[8,768]{1,0:T(8,128)}, f32[8,768]{1,0:T(8,128)S(1)}, u32[]{:S(2)}, u32[]{:S(2)}) collective-permute-start(f32[8,768]{1,0:T(8,128)} %get-tuple-element.59), channel_id=1, source_target_pairs={{0,3},{1,0},{2,1},{3,2},{4,7},{5,4},{6,5},{7,6},{8,11},{9,8},{10,9... | collective-permute-start | bytes 73736 | tf_op jit(solution)/shard_map/ppermute | solution.py:491
  131.7 0.0 collective-permute-done.9.refs_9_
  131.8 0.0 collective-permute-done.7.refs_8_
  131.8 0.0 copy-start.12
  131.8 0.9 copy-done.11
  132.6 0.3 copy-done.12
  133.0 11.2 %pairs.5 = (f32[8,768]{1,0:T(8,128)}, f32[8,768]{1,0:T(8,128)}, f32[8,768]{1,0:T(8,128)}, f32[8,768]{1,0:T(8,128)}, f32[8,768]{1,0:T(8,128)}) custom-call(s32[2]{0:T(128)} %pad_add_fusion.half_ref, bf16[784,512]{1,0:T(8,128)(2,1)} %get-tuple-element.38.block.refs_0_, bf16[784,512]{1,0:T(8,128)(2,1)} %copy-done.6, bf16[784,512]{1,0:T(8,128)(2,1)} %copy-done.7, ...), custom_call_target="tpu_custom_call" | custom-call | flops 3623878656 | bytes 8028160 | tf_op jit(solution)/shard_map/pairs/pallas_call | solution.py:402
  144.2 0.1 collective-permute-start.10
  144.3 3.6 %collective-permute-start.11 = (f32[8,768]{1,0:T(8,128)}, f32[8,768]{1,0:T(8,128)S(1)}, u32[]{:S(2)}, u32[]{:S(2)}) collective-permute-start(f32[8,768]{1,0:T(8,128)} %get-tuple-element.57), channel_id=1, source_target_pairs={{0,8},{1,9},{2,10},{3,11},{4,12},{5,13},{6,14},{7,15},{8,0},{9,1},... | collective-permute-start | bytes 73736 | tf_op jit(solution)/shard_map/ppermute | solution.py:491
  147.9 0.0 collective-permute-start.12
  147.9 1.5 collective-permute-start.14
  149.3 0.0 collective-permute-done.13.refs_4_
  149.4 0.0 collective-permute-done.10.refs_1_
  149.4 0.0 copy-start.2
  149.4 0.5 collective-permute-done.11.refs_2_
  149.9 3.2 %collective-permute-done.12.refs_3_ = f32[8,768]{1,0:T(8,128)S(1)} collective-permute-done((f32[8,768]{1,0:T(8,128)}, f32[8,768]{1,0:T(8,128)S(1)}, u32[]{:S(2)}, u32[]{:S(2)}) %collective-permute-start.12) | collective-permute-done | bytes 24608 | tf_op jit(solution)/shard_map/ppermute | solution.py:491
  153.1 0.3 collective-permute-done.14.refs_5_
  153.4 0.0 copy-done.1
  153.4 0.0 copy-done.2
  153.4 0.0 copy-done.3
  153.4 0.3 copy-done.4
  153.7 0.3 copy-done.5
  154.0 1.6 spread.1
  155.6 10.1 %all_to_all.15.back_ref = f32[8,8,384]{2,1,0:T(8,128)} all-to-all(f32[8,8,384]{2,1,0:T(8,128)} %spread.1), channel_id=1, replica_groups=mesh['tr'=8,'tc'=16] {'tr'}, dimensions={0} | all-to-all | bytes 196608 | tf_op jit(solution)/shard_map/all_to_all | solution.py:506
  165.7 2.4 %unpack.1 = (f32[768]{0:T(1024)}, f32[768]{0:T(1024)}, f32[768]{0:T(1024)}) custom-call(f32[8,8,384]{2,1,0:T(8,128)} %all_to_all.15.back_ref, s32[768]{0:T(1024)} %lab_ref.5, s32[1,768]{1,0:T(1,128)} %get-tuple-element.33.rank_ref), custom_call_target="tpu_custom_call" | custom-call | tf_op jit(solution)/shard_map/unpack/pallas_call | solution.py:472
  (8 shorter events, 0.0 us)
Async XLA Ops:
  8.2 36.7 %all-to-all-start = ((bf16[8,304,512]{2,1,0:T(8,128)(2,1)}), bf16[8,304,512]{2,1,0:T(8,128)(2,1)S(1)}, u32[]{:S(2)}, u32[]{:S(2)}) async-start(bf16[8,304,512]{2,1,0:T(8,128)(2,1)} %get-tuple-element.34), calls=%async_computation | async-start | bytes 4980736 | tf_op jit(solution)/shard_map/all_to_all | solution.py:506
  44.9 4.4 %copy-start = (bf16[8,304,512]{2,1,0:T(8,128)(2,1)}, bf16[8,304,512]{2,1,0:T(8,128)(2,1)S(1)}, u32[]{:S(2)}) copy-start(bf16[8,304,512]{2,1,0:T(8,128)(2,1)S(1)} %all-to-all-done.got_ref) | copy-start | bytes 7471108
  44.9 41.9 %all-to-all-start.1 = ((bf16[8,288,512]{2,1,0:T(8,128)(2,1)}), bf16[8,288,512]{2,1,0:T(8,128)(2,1)}, u32[]{:S(2)}, u32[]{:S(2)}) async-start(bf16[8,288,512]{2,1,0:T(8,128)(2,1)} %pack_rest.1), calls=%async_computation.1 | async-start | bytes 4718592 | tf_op jit(solution)/shard_map/all_to_all | solution.py:506
  53.6 18.8 %collective-permute-start.3 = (bf16[784,512]{1,0:T(8,128)(2,1)}, bf16[784,512]{1,0:T(8,128)(2,1)S(1)}, u32[]{:S(2)}, u32[]{:S(2)}) collective-permute-start(bf16[784,512]{1,0:T(8,128)(2,1)} %get-tuple-element.38.block.refs_0_), channel_id=1, source_target_pairs={{0,1},{1,2},{2,3},{3,0},{4,5},{5,6},{6,7},{7,4},{8,9},{9,10},{10,1... | collective-permute-start | bytes 2408456 | tf_op jit(solution)/shard_map/ppermute | solution.py:491
  55.2 19.4 %collective-permute-start = (bf16[784,512]{1,0:T(8,128)(2,1)}, bf16[784,512]{1,0:T(8,128)(2,1)S(1)}, u32[]{:S(2)}, u32[]{:S(2)}) collective-permute-start(bf16[784,512]{1,0:T(8,128)(2,1)} %get-tuple-element.38.block.refs_0_), channel_id=1, source_target_pairs={{0,12},{1,13},{2,14},{3,15},{4,0},{5,1},{6,2},{7,3},{8,4},{9,5},{1... | collective-permute-start | bytes 2408456 | tf_op jit(solution)/shard_map/ppermute | solution.py:491
  55.8 19.4 %collective-permute-start.2 = (bf16[784,512]{1,0:T(8,128)(2,1)}, bf16[784,512]{1,0:T(8,128)(2,1)S(1)}, u32[]{:S(2)}, u32[]{:S(2)}) collective-permute-start(bf16[784,512]{1,0:T(8,128)(2,1)} %get-tuple-element.38.block.refs_0_), channel_id=1, source_target_pairs={{0,3},{1,0},{2,1},{3,2},{4,7},{5,4},{6,5},{7,6},{8,11},{9,8},{10,9... | collective-permute-start | bytes 2408456 | tf_op jit(solution)/shard_map/ppermute | solution.py:491
  72.5 14.3 %copy-start.10 = (bf16[784,512]{1,0:T(8,128)(2,1)}, bf16[784,512]{1,0:T(8,128)(2,1)S(1)}, u32[]{:S(2)}) copy-start(bf16[784,512]{1,0:T(8,128)(2,1)S(1)} %collective-permute-done.3.refs_3_) | copy-start | bytes 2408452
  72.5 14.3 %collective-permute-start.4 = (bf16[784,512]{1,0:T(8,128)(2,1)S(1)}, bf16[784,512]{1,0:T(8,128)(2,1)S(1)}, u32[]{:S(2)}, u32[]{:S(2)}) collective-permute-start(bf16[784,512]{1,0:T(8,128)(2,1)S(1)} %collective-permute-done.3.refs_3_), channel_id=1, source_target_pairs={{0,1},{1,2},{2,3},{3,0},{4,5},{5,6},{6,7},{7,4},{8,9},{9,10},{10,1... | collective-permute-start | bytes 2408456 | tf_op jit(solution)/shard_map/ppermute | solution.py:491
  74.7 25.6 %copy-start.6 = (bf16[784,512]{1,0:T(8,128)(2,1)}, bf16[784,512]{1,0:T(8,128)(2,1)S(1)}, u32[]{:S(2)}) copy-start(bf16[784,512]{1,0:T(8,128)(2,1)S(1)} %collective-permute-done.refs_1_) | copy-start | bytes 2408452
  74.7 12.2 %collective-permute-start.1 = (bf16[784,512]{1,0:T(8,128)(2,1)S(1)}, bf16[784,512]{1,0:T(8,128)(2,1)S(1)}, u32[]{:S(2)}, u32[]{:S(2)}) collective-permute-start(bf16[784,512]{1,0:T(8,128)(2,1)S(1)} %collective-permute-done.refs_1_), channel_id=1, source_target_pairs={{0,12},{1,13},{2,14},{3,15},{4,0},{5,1},{6,2},{7,3},{8,4},{9,5},{1... | collective-permute-start | bytes 2408456 | tf_op jit(solution)/shard_map/ppermute | solution.py:491
  75.2 25.1 %copy-start.7 = (bf16[784,512]{1,0:T(8,128)(2,1)}, bf16[784,512]{1,0:T(8,128)(2,1)S(1)}, u32[]{:S(2)}) copy-start(bf16[784,512]{1,0:T(8,128)(2,1)S(1)} %collective-permute-done.2.refs_2_) | copy-start | bytes 2408452
  86.7 13.6 %copy-start.8 = (bf16[784,512]{1,0:T(8,128)(2,1)}, bf16[784,512]{1,0:T(8,128)(2,1)S(1)}, u32[]{:S(2)}) copy-start(bf16[784,512]{1,0:T(8,128)(2,1)S(1)} %collective-permute-done.4.refs_4_) | copy-start | bytes 2408452
  86.8 13.4 %copy-start.9 = (bf16[784,512]{1,0:T(8,128)(2,1)}, bf16[784,512]{1,0:T(8,128)(2,1)S(1)}, u32[]{:S(2)}) copy-start(bf16[784,512]{1,0:T(8,128)(2,1)S(1)} %collective-permute-done.1.refs_3_) | copy-start | bytes 2408452
  91.4 12.3 %collective-permute-start.5 = (bf16[768,512]{1,0:T(8,128)(2,1)}, bf16[768,512]{1,0:T(8,128)(2,1)}, u32[]{:S(2)}, u32[]{:S(2)}) collective-permute-start(bf16[768,512]{1,0:T(8,128)(2,1)} %compact_rest.1.rest.refs_2_.refs_4_.refs_5_), channel_id=1, source_target_pairs={{0,12},{1,13},{2,14},{3,15},{4,0},{5,1},{6,2},{7,3},{8,4},{9,5},{1... | collective-permute-start | bytes 2359304 | tf_op jit(solution)/shard_map/ppermute | solution.py:491
  92.6 20.5 %collective-permute-start.8 = (bf16[768,512]{1,0:T(8,128)(2,1)}, bf16[768,512]{1,0:T(8,128)(2,1)}, u32[]{:S(2)}, u32[]{:S(2)}) collective-permute-start(bf16[768,512]{1,0:T(8,128)(2,1)} %compact_rest.1.rest.refs_2_.refs_4_.refs_5_), channel_id=1, source_target_pairs={{0,1},{1,2},{2,3},{3,0},{4,5},{5,6},{6,7},{7,4},{8,9},{9,10},{10,1... | collective-permute-start | bytes 2359304 | tf_op jit(solution)/shard_map/ppermute | solution.py:491
  94.9 21.5 %collective-permute-start.6 = (bf16[768,512]{1,0:T(8,128)(2,1)}, bf16[768,512]{1,0:T(8,128)(2,1)}, u32[]{:S(2)}, u32[]{:S(2)}) collective-permute-start(bf16[768,512]{1,0:T(8,128)(2,1)} %compact_rest.1.rest.refs_2_.refs_4_.refs_5_), channel_id=1, source_target_pairs={{0,3},{1,0},{2,1},{3,2},{4,7},{5,4},{6,5},{7,6},{8,11},{9,8},{10,9... | collective-permute-start | bytes 2359304 | tf_op jit(solution)/shard_map/ppermute | solution.py:491
  113.0 18.7 %collective-permute-start.9 = (bf16[768,512]{1,0:T(8,128)(2,1)}, bf16[768,512]{1,0:T(8,128)(2,1)S(1)}, u32[]{:S(2)}, u32[]{:S(2)}) collective-permute-start(bf16[768,512]{1,0:T(8,128)(2,1)} %collective-permute-done.8.refs_7_), channel_id=1, source_target_pairs={{0,1},{1,2},{2,3},{3,0},{4,5},{5,6},{6,7},{7,4},{8,9},{9,10},{10,1... | collective-permute-start | bytes 2359304 | tf_op jit(solution)/shard_map/ppermute | solution.py:491
  115.0 16.8 %collective-permute-start.7 = (bf16[768,512]{1,0:T(8,128)(2,1)}, bf16[768,512]{1,0:T(8,128)(2,1)S(1)}, u32[]{:S(2)}, u32[]{:S(2)}) collective-permute-start(bf16[768,512]{1,0:T(8,128)(2,1)} %collective-permute-done.5.refs_3_.refs_5_.refs_6_), channel_id=1, source_target_pairs={{0,12},{1,13},{2,14},{3,15},{4,0},{5,1},{6,2},{7,3},{8,4},{9,5},{1... | collective-permute-start | bytes 2359304 | tf_op jit(solution)/shard_map/ppermute | solution.py:491
  128.2 21.1 %collective-permute-start.13 = (f32[8,768]{1,0:T(8,128)}, f32[8,768]{1,0:T(8,128)S(1)}, u32[]{:S(2)}, u32[]{:S(2)}) collective-permute-start(f32[8,768]{1,0:T(8,128)} %get-tuple-element.59), channel_id=1, source_target_pairs={{0,3},{1,0},{2,1},{3,2},{4,7},{5,4},{6,5},{7,6},{8,11},{9,8},{10,9... | collective-permute-start | bytes 73736 | tf_op jit(solution)/shard_map/ppermute | solution.py:491
  131.8 0.9 copy-start.11
  131.8 1.2 copy-start.12
  144.2 5.1 %collective-permute-start.10 = (f32[8,768]{1,0:T(8,128)}, f32[8,768]{1,0:T(8,128)S(1)}, u32[]{:S(2)}, u32[]{:S(2)}) collective-permute-start(f32[8,768]{1,0:T(8,128)} %get-tuple-element.56), channel_id=1, source_target_pairs={{0,4},{1,5},{2,6},{3,7},{4,8},{5,9},{6,10},{7,11},{8,12},{9,13},{1... | collective-permute-start | bytes 73736 | tf_op jit(solution)/shard_map/ppermute | solution.py:491
  144.3 5.6 %collective-permute-start.11 = (f32[8,768]{1,0:T(8,128)}, f32[8,768]{1,0:T(8,128)S(1)}, u32[]{:S(2)}, u32[]{:S(2)}) collective-permute-start(f32[8,768]{1,0:T(8,128)} %get-tuple-element.57), channel_id=1, source_target_pairs={{0,8},{1,9},{2,10},{3,11},{4,12},{5,13},{6,14},{7,15},{8,0},{9,1},... | collective-permute-start | bytes 73736 | tf_op jit(solution)/shard_map/ppermute | solution.py:491
  147.9 5.2 %collective-permute-start.12 = (f32[8,768]{1,0:T(8,128)}, f32[8,768]{1,0:T(8,128)S(1)}, u32[]{:S(2)}, u32[]{:S(2)}) collective-permute-start(f32[8,768]{1,0:T(8,128)} %get-tuple-element.58), channel_id=1, source_target_pairs={{0,1},{1,2},{2,3},{3,0},{4,5},{5,6},{6,7},{7,4},{8,9},{9,10},{10,1... | collective-permute-start | bytes 73736 | tf_op jit(solution)/shard_map/ppermute | solution.py:491
  147.9 5.5 %collective-permute-start.14 = (f32[8,768]{1,0:T(8,128)}, f32[8,768]{1,0:T(8,128)S(1)}, u32[]{:S(2)}, u32[]{:S(2)}) collective-permute-start(f32[8,768]{1,0:T(8,128)} %get-tuple-element.60), channel_id=1, source_target_pairs={{0,2},{1,3},{2,0},{3,1},{4,6},{5,7},{6,4},{7,5},{8,10},{9,11},{10,... | collective-permute-start | bytes 73736 | tf_op jit(solution)/shard_map/ppermute | solution.py:491
  149.4 4.1 %copy-start.1 = (f32[8,768]{1,0:T(8,128)}, f32[8,768]{1,0:T(8,128)S(1)}, u32[]{:S(2)}) copy-start(f32[8,768]{1,0:T(8,128)S(1)} %collective-permute-done.13.refs_4_) | copy-start | bytes 73732
  149.4 4.0 %copy-start.2 = (f32[8,768]{1,0:T(8,128)}, f32[8,768]{1,0:T(8,128)S(1)}, u32[]{:S(2)}) copy-start(f32[8,768]{1,0:T(8,128)S(1)} %collective-permute-done.10.refs_1_) | copy-start | bytes 73732
  149.9 3.5 %copy-start.3 = (f32[8,768]{1,0:T(8,128)}, f32[8,768]{1,0:T(8,128)S(1)}, u32[]{:S(2)}) copy-start(f32[8,768]{1,0:T(8,128)S(1)} %collective-permute-done.11.refs_2_) | copy-start | bytes 73732
  153.1 0.6 copy-start.4
  153.4 0.6 copy-start.5

commit v4 on v3

--- a/solution.py
+++ b/solution.py
@@ -28,7 +28,7 @@
 CHUNK = 256
 HALF = 384
 STRIP = 32
-VMEM = 56 * 1024 * 1024
+VMEM = 24 * 1024 * 1024
 BF = jnp.bfloat16
 F32 = jnp.float32
 
@@ -290,21 +290,9 @@
     n, n_old = len(blocks), len(old)
     ins, rests, olds = refs[:n], refs[n : 2 * n], refs[2 * n : 2 * n + n_old]
     outs = refs[2 * n + n_old : 3 * n + n_old]
-    held, held2, marks, names, rows, tops, totals, weights, scores0, scores1, sems = refs[
-        3 * n + n_old :
-    ]
+    marks, names, rows, tops, totals, weights, scores0, scores1 = refs[3 * n + n_old :]
     scores = (scores0, scores1)
     place = {b: i for i, b in enumerate(blocks)}
-    copies = [
-        (
-            pltpu.make_async_copy(ins[i], held.at[i], sems.at[2 * i]),
-            pltpu.make_async_copy(rests[i], held2.at[i], sems.at[2 * i + 1]),
-        )
-        for i in range(n)
-    ]
-    for first, second in copies:
-        first.start()
-        second.start()
     lane = iota((1, 128), 1)
     empty = jnp.where(lane % 4 == 0, NEGATIVE, 0.0)
     for i in range(n):
@@ -317,9 +305,7 @@
     def need(i):
         if i not in ready:
             ready.add(i)
-            copies[i][0].wait()
-            copies[i][1].wait()
-            one, many = spread_names(held.at[i])
+            one, many = spread_names(ins[i])
             names[i] = jnp.broadcast_to(one, (8, ROWS))
             marks[i] = many
 
@@ -327,25 +313,31 @@
     for k, (left, right, axis) in enumerate(plan):
         left, right = place[left], place[right]
         if axis is None:
-            steps += [(k, left, right, 0, (left, right)), (k, left, right, HALF, (left, right))]
+            steps += [(k, left, right, s, (left, right), None) for s in (0, HALF)]
         else:
             half = half_ref[axis]
             first = jnp.where(half == 0, left, right)
             second = jnp.where(half == 0, right, left)
             start = pl.multiple_of(half * HALF, HALF)
-            steps.append((k, first, second, start, (left, right)))
+            steps.append((k, first, second, start, (left, right), half == 0))
 
     def product(step, out):
-        _, left, right, start, both = step
+        _, _, _, start, both, first = step
         for i in both:
             need(i)
         here = pl.ds(start, HALF)
-        out[...] = dot_nt(held[left, here], held[right, :ROWS]) + dot_nt(
-            held2[left, here], held2[right]
-        )
+
+        def multiply(pieces):
+            left, right = pieces[both[0]], pieces[both[1]]
+            if first is None:
+                return dot_nt(left[here], right[:ROWS])
+            keys = jnp.where(first, left[here], right[here])
+            return dot_nt(keys, jnp.where(first, right[:ROWS], left[:ROWS]))
+
+        out[...] = multiply(ins) + multiply(rests)
 
     def reduce(step, data):
-        k, left, right, start, _ = step
+        k, left, right, start, _, _ = step
         name = names[right][:1]
         top = tops[right]
         peak = top
@@ -398,15 +390,12 @@
 def pairs(plan, blocks, old, halves):
     names, n = list(blocks), len(blocks)
     steps = sum(2 if axis is None else 1 for _, _, axis in plan)
-    anywhere = pl.BlockSpec(memory_space=pl.ANY)
     return pl.pallas_call(
         functools.partial(pair_kernel, plan, names, list(old)),
         out_shape=[jax.ShapeDtypeStruct((8, ROWS), F32)] * n,
-        in_specs=[smem()] + [anywhere] * (2 * n) + [vmem()] * len(old),
+        in_specs=[smem()] + [vmem()] * (2 * n) + [vmem()] * len(old),
         out_specs=[vmem()] * n,
         scratch_shapes=[
-            pltpu.VMEM((n, BLOCK, PIECE), BF),
-            pltpu.VMEM((n, ROWS, WIDTH - PIECE), BF),
             pltpu.VMEM((n, ROWS, 128), F32),
             pltpu.VMEM((n, 8, ROWS), F32),
             pltpu.VMEM((n, ROWS, 128), F32),
@@ -415,7 +404,6 @@
             pltpu.VMEM((n, 8, ROWS), F32),
             pltpu.VMEM((HALF, ROWS), F32),
             pltpu.VMEM((HALF, ROWS), F32),
-            pltpu.SemaphoreType.DMA((2 * n,)),
         ],
         compiler_params=params(),
         cost_estimate=pl.CostEstimate(

time: 169 us -> 158 us (0.935); the launches traced: 168 us -> 155 us
  Pallas kernels: 58.7 us -> 36.5 us
  local copies, waits for them, and re-layouts: 1.81 us -> 7.69 us
  waiting for transfers between devices: 63.4 us -> 66.6 us
    pallas_call x3, Pallas kernels: 28.4 us -> 19.5 us  [pairs(): pl.pallas_call(functools.partial(pair_kernel, plan, names, list(old)), ou...]
    unnamed x26 -> x22, local copies, waits for them, and re-layouts: 1.81 us -> 7.69 us
    pallas_call x1, Pallas kernels: 6.05 us -> 3.22 us  [pack_rest(): pl.pallas_call(pack_rest_kernel, grid=(TILE_ROWS,), in_specs=[whole((ROWS...]
    pallas_call x1, Pallas kernels: 7.55 us -> 4.78 us  [pack_first(): pl.pallas_call(pack_first_kernel, grid=(TILE_ROWS,), in_specs=[whole((ROW...]
    pallas_call x1, Pallas kernels: 4.27 us -> 1.62 us  [compact_first(): pl.pallas_call(compact_first_kernel, in_specs=[vmem()], out_specs=[vmem()...]
    pallas_call x1, Pallas kernels: 3.88 us -> 1.98 us  [own_pairs(): pl.pallas_call(own_kernel, out_shape=jax.ShapeDtypeStruct((8, ROWS), F32)...]
    ppermute x15, waiting for transfers between devices: 38 us -> 39.8 us  [shift(): return lax.ppermute(array, ('tr', 'tc'), moves)]
  transfers between devices with their start and end apart: 17 -> 17, of which waited for: 9 -> 7; matrix products, arithmetic and copies ran while one was open for 0% -> 0% of each run, Pallas kernels for 25% -> 17%
where the time goes in v4:
time: 158 us; the launch traced here: 155 us
  waiting for transfers between devices  66.6 us (42%)
  Pallas kernels  36.5 us (23%)
  starting transfers between devices  34.1 us (22%)
  blocking collectives  9.71 us (6%)
  local copies, waits for them, and re-layouts  7.69 us (5%)
    ppermute x15, waiting for transfers between devices, shift(): return lax.ppermute(array, ('tr', 'tc'), moves)  39.8 us
    all_to_all x2, waiting for transfers between devices, exchange(): return lax.all_to_all(packed, 'tr', split_axis=0, concat_axis=0, tiled=True)  26.7 us
    ppermute x15, starting transfers between devices, shift(): return lax.ppermute(array, ('tr', 'tc'), moves)  24.3 us
    pallas_call x3, Pallas kernels, pairs(): pl.pallas_call(functools.partial(pair_kernel, plan, names, list(old)), ou...  19.5 us
    all_to_all x2, starting transfers between devices, exchange(): return lax.all_to_all(packed, 'tr', split_axis=0, concat_axis=0, tiled=True)  9.81 us
    all_to_all x1, blocking collectives, exchange(): return lax.all_to_all(packed, 'tr', split_axis=0, concat_axis=0, tiled=True)  9.71 us
    unnamed x22, local copies, waits for them, and re-layouts  7.69 us
    pallas_call x1, Pallas kernels, pack_first(): pl.pallas_call(pack_first_kernel, grid=(TILE_ROWS,), in_specs=[whole((ROW...  4.78 us
  transfers between devices with their start and end apart: 17, of which 7 were waited for; matrix products, arithmetic and copies ran while one was open for 0% of the time, Pallas kernels for 17%

profile of v4, /device:TPU:2, one launch (start us, length us, event | category | flops | bytes accessed | tf_op | source)
XLA Modules:
  0.0 155.4 jit_solution(17888499936561626700)
XLA Ops:
  0.6 0.0 copy-start.2
  0.6 1.4 copy-done.2
  2.0 0.0 copy-start.3
  2.0 0.7 copy-done.3
  2.7 4.8 %pack_first.1 = (bf16[8,304,512]{2,1,0:T(8,128)(2,1)S(1)}, s32[1,768]{1,0:T(1,128)S(1)}, bf16[768,512]{1,0:T(8,128)(2,1)S(1)}) custom-call(bf16[768,1024]{1,0:T(8,128)(2,1)S(1)} %copy-done.2, s32[768]{0:T(1024)S(1)} %copy-done.3), custom_call_target="tpu_custom_call" | custom-call | tf_op jit(solution)/shard_map/pack_first/pallas_call | solution.py:95
  7.5 0.0 copy-start
  7.5 1.5 copy-done
  9.0 0.0 copy-start.4
  9.0 5.4 %all-to-all-start = ((bf16[8,304,512]{2,1,0:T(8,128)(2,1)}), bf16[8,304,512]{2,1,0:T(8,128)(2,1)S(1)}, u32[]{:S(2)}, u32[]{:S(2)}) async-start(bf16[8,304,512]{2,1,0:T(8,128)(2,1)} %copy-done), calls=%async_computation | async-start | bytes 4980736 | tf_op jit(solution)/shard_map/all_to_all | solution.py:494
  14.4 0.0 copy-done.4
  14.4 3.2 %pack_rest.1 = bf16[8,288,512]{2,1,0:T(8,128)(2,1)S(1)} custom-call(bf16[768,512]{1,0:T(8,128)(2,1)S(1)} %get-tuple-element.32.unit_ref, s32[768]{0:T(1024)S(1)} %copy-done.4, s32[1,768]{1,0:T(1,128)S(1)} %get-tuple-element.33.rank_ref), custom_call_target="tpu_custom_call" | custom-call | flops 1811939328 | bytes 2359296 | tf_op jit(solution)/shard_map/pack_rest/pallas_call | solution.py:122
  17.6 0.0 copy-start.1
  17.7 1.4 copy-done.1
  19.1 26.7 %all-to-all-done.got_ref = bf16[8,304,512]{2,1,0:T(8,128)(2,1)S(1)} async-done(((bf16[8,304,512]{2,1,0:T(8,128)(2,1)}), bf16[8,304,512]{2,1,0:T(8,128)(2,1)S(1)}, u32[]{:S(2)}, u32[]{:S(2)}) %all-to-all-start) | async-done | bytes 2490400 | tf_op jit(solution)/shard_map/all_to_all | solution.py:494
  45.8 4.4 %all-to-all-start.1 = ((bf16[8,288,512]{2,1,0:T(8,128)(2,1)}), bf16[8,288,512]{2,1,0:T(8,128)(2,1)}, u32[]{:S(2)}, u32[]{:S(2)}) async-start(bf16[8,288,512]{2,1,0:T(8,128)(2,1)} %copy-done.1), calls=%async_computation.1 | async-start | bytes 4718592 | tf_op jit(solution)/shard_map/all_to_all | solution.py:494
  50.2 1.6 %compact_first.1 = (bf16[784,512]{1,0:T(8,128)(2,1)S(1)}, s32[16]{0:T(128)S(1)}) custom-call(bf16[8,304,512]{2,1,0:T(8,128)(2,1)S(1)} %all-to-all-done.got_ref), custom_call_target="tpu_custom_call" | custom-call | tf_op jit(solution)/shard_map/compact_first/pallas_call | solution.py:176
  51.8 1.7 %collective-permute-start.3 = (bf16[784,512]{1,0:T(8,128)(2,1)S(1)}, bf16[784,512]{1,0:T(8,128)(2,1)S(1)}, u32[]{:S(2)}, u32[]{:S(2)}) collective-permute-start(bf16[784,512]{1,0:T(8,128)(2,1)S(1)} %get-tuple-element.38.block.refs_0_), channel_id=1, source_target_pairs={{0,1},{1,2},{2,3},{3,0},{4,5},{5,6},{6,7},{7,4},{8,9},{9,10},{10,1... | collective-permute-start | bytes 2408456 | tf_op jit(solution)/shard_map/ppermute | solution.py:479
  53.5 0.5 collective-permute-start
  54.0 1.7 %collective-permute-start.2 = (bf16[784,512]{1,0:T(8,128)(2,1)S(1)}, bf16[784,512]{1,0:T(8,128)(2,1)S(1)}, u32[]{:S(2)}, u32[]{:S(2)}) collective-permute-start(bf16[784,512]{1,0:T(8,128)(2,1)S(1)} %get-tuple-element.38.block.refs_0_), channel_id=1, source_target_pairs={{0,3},{1,0},{2,1},{3,2},{4,7},{5,4},{6,5},{7,6},{8,11},{9,8},{10,9... | collective-permute-start | bytes 2408456 | tf_op jit(solution)/shard_map/ppermute | solution.py:479
  55.7 14.8 %collective-permute-done.3.refs_3_ = bf16[784,512]{1,0:T(8,128)(2,1)S(1)} collective-permute-done((bf16[784,512]{1,0:T(8,128)(2,1)S(1)}, bf16[784,512]{1,0:T(8,128)(2,1)S(1)}, u32[]{:S(2)}, u32[]{:S(2)}) %collective-permute-start.3) | collective-permute-done | bytes 802848 | tf_op jit(solution)/shard_map/ppermute | solution.py:479
  70.5 2.1 %collective-permute-start.4 = (bf16[784,512]{1,0:T(8,128)(2,1)S(1)}, bf16[784,512]{1,0:T(8,128)(2,1)S(1)}, u32[]{:S(2)}, u32[]{:S(2)}) collective-permute-start(bf16[784,512]{1,0:T(8,128)(2,1)S(1)} %collective-permute-done.3.refs_3_), channel_id=1, source_target_pairs={{0,1},{1,2},{2,3},{3,0},{4,5},{5,6},{6,7},{7,4},{8,9},{9,10},{10,1... | collective-permute-start | bytes 2408456 | tf_op jit(solution)/shard_map/ppermute | solution.py:479
  72.6 0.0 copy-start.9
  72.6 0.9 copy-done.9
  73.5 0.0 collective-permute-done.refs_1_
  73.5 0.5 collective-permute-start.1
  74.0 0.0 collective-permute-done.2.refs_2_
  74.0 10.7 %collective-permute-done.4.refs_4_ = bf16[784,512]{1,0:T(8,128)(2,1)S(1)} collective-permute-done((bf16[784,512]{1,0:T(8,128)(2,1)S(1)}, bf16[784,512]{1,0:T(8,128)(2,1)S(1)}, u32[]{:S(2)}, u32[]{:S(2)}) %collective-permute-start.4) | collective-permute-done | bytes 802848 | tf_op jit(solution)/shard_map/ppermute | solution.py:479
  84.7 0.9 copy-done.5
  85.6 0.0 collective-permute-done.1.refs_3_
  85.6 0.9 copy-done.7
  86.6 0.0 all-to-all-done.1.got_ref
  86.6 3.2 %compact_rest.1.rest.refs_2_.refs_4_.refs_5_ = bf16[768,512]{1,0:T(8,128)(2,1)S(1)} custom-call(s32[16]{0:T(128)S(1)} %get-tuple-element.36.place_ref.offset_ref, bf16[8,288,512]{2,1,0:T(8,128)(2,1)} %all-to-all-done.1.got_ref), custom_call_target="tpu_custom_call" | custom-call | tf_op jit(solution)/shard_map/compact_rest/pallas_call | solution.py:198
  89.8 1.5 collective-permute-start.5
  91.2 2.4 %collective-permute-start.8 = (bf16[768,512]{1,0:T(8,128)(2,1)S(1)}, bf16[768,512]{1,0:T(8,128)(2,1)}, u32[]{:S(2)}, u32[]{:S(2)}) collective-permute-start(bf16[768,512]{1,0:T(8,128)(2,1)S(1)} %compact_rest.1.rest.refs_2_.refs_4_.refs_5_), channel_id=1, source_target_pairs={{0,1},{1,2},{2,3},{3,0},{4,5},{5,6},{6,7},{7,4},{8,9},{9,10},{10,1... | collective-permute-start | bytes 2359304 | tf_op jit(solution)/shard_map/ppermute | solution.py:479
  93.7 0.8 collective-permute-start.6
  94.5 0.1 pad_add_fusion.half_ref
  94.6 2.0 %own.1.refs_4_ = f32[8,768]{1,0:T(8,128)S(1)} custom-call(bf16[784,512]{1,0:T(8,128)(2,1)S(1)} %get-tuple-element.38.block.refs_0_, bf16[768,512]{1,0:T(8,128)(2,1)S(1)} %compact_rest.1.rest.refs_2_.refs_4_.refs_5_), custom_call_target="tpu_custom_call" | custom-call | flops 1207959552 | bytes 1605632 | tf_op jit(solution)/shard_map/own/pallas_call | solution.py:273
  96.5 0.0 copy-start.10
  96.5 5.4 %collective-permute-done.5.refs_3_.refs_5_.refs_6_ = bf16[768,512]{1,0:T(8,128)(2,1)} collective-permute-done((bf16[768,512]{1,0:T(8,128)(2,1)S(1)}, bf16[768,512]{1,0:T(8,128)(2,1)}, u32[]{:S(2)}, u32[]{:S(2)}) %collective-permute-start.5) | collective-permute-done | bytes 786464 | tf_op jit(solution)/shard_map/ppermute | solution.py:479
  101.9 3.4 %pairs.3 = (f32[8,768]{1,0:T(8,128)S(1)}, f32[8,768]{1,0:T(8,128)S(1)}) custom-call(s32[2]{0:T(128)S(1)} %pad_add_fusion.half_ref, bf16[784,512]{1,0:T(8,128)(2,1)S(1)} %get-tuple-element.38.block.refs_0_, bf16[784,512]{1,0:T(8,128)(2,1)S(1)} %collective-permute-done.refs_1_, bf16[768,512]{1,0:T(8,128)(2,1)S(1)} %compact_rest.1.rest.refs_2_.refs_4_.refs_5_, ...), custom_call_target="tpu_custom_call" | custom-call | flops 1207959552 | bytes 3211264 | tf_op jit(solution)/shard_map/pairs/pallas_call | solution.py:393
  105.3 6.5 %collective-permute-done.8.refs_7_ = bf16[768,512]{1,0:T(8,128)(2,1)} collective-permute-done((bf16[768,512]{1,0:T(8,128)(2,1)S(1)}, bf16[768,512]{1,0:T(8,128)(2,1)}, u32[]{:S(2)}, u32[]{:S(2)}) %collective-permute-start.8) | collective-permute-done | bytes 786464 | tf_op jit(solution)/shard_map/ppermute | solution.py:479
  111.8 1.6 %collective-permute-start.9 = (bf16[768,512]{1,0:T(8,128)(2,1)}, bf16[768,512]{1,0:T(8,128)(2,1)S(1)}, u32[]{:S(2)}, u32[]{:S(2)}) collective-permute-start(bf16[768,512]{1,0:T(8,128)(2,1)} %collective-permute-done.8.refs_7_), channel_id=1, source_target_pairs={{0,1},{1,2},{2,3},{3,0},{4,5},{5,6},{6,7},{7,4},{8,9},{9,10},{10,1... | collective-permute-start | bytes 2359304 | tf_op jit(solution)/shard_map/ppermute | solution.py:479
  113.4 1.2 collective-permute-start.7
  114.7 0.0 collective-permute-done.6.refs_6_.refs_7_
  114.7 0.0 copy-done.10
  114.7 8.8 %pairs.4 = (f32[8,768]{1,0:T(8,128)S(1)}, f32[8,768]{1,0:T(8,128)S(1)}, f32[8,768]{1,0:T(8,128)S(1)}, f32[8,768]{1,0:T(8,128)S(1)}) custom-call(s32[2]{0:T(128)S(1)} %pad_add_fusion.half_ref, bf16[784,512]{1,0:T(8,128)(2,1)S(1)} %get-tuple-element.38.block.refs_0_, bf16[784,512]{1,0:T(8,128)(2,1)S(1)} %collective-permute-done.refs_1_, ...), custom_call_target="tpu_custom_call" | custom-call | flops 4227858432 | bytes 6422528 | tf_op jit(solution)/shard_map/pairs/pallas_call | solution.py:393
  123.5 3.5 %collective-permute-start.13 = (f32[8,768]{1,0:T(8,128)S(1)}, f32[8,768]{1,0:T(8,128)S(1)}, u32[]{:S(2)}, u32[]{:S(2)}) collective-permute-start(f32[8,768]{1,0:T(8,128)S(1)} %get-tuple-element.59), channel_id=1, source_target_pairs={{0,3},{1,0},{2,1},{3,2},{4,7},{5,4},{6,5},{7,6},{8,11},{9,8},{10,9... | collective-permute-start | bytes 73736 | tf_op jit(solution)/shard_map/ppermute | solution.py:479
  127.0 0.0 collective-permute-done.9.refs_9_
  127.0 0.0 collective-permute-done.7.refs_8_
  127.0 0.0 copy-done.6
  127.0 0.0 copy-done.8
  127.0 7.3 %pairs.5 = (f32[8,768]{1,0:T(8,128)S(1)}, f32[8,768]{1,0:T(8,128)S(1)}, f32[8,768]{1,0:T(8,128)S(1)}, f32[8,768]{1,0:T(8,128)S(1)}, f32[8,768]{1,0:T(8,128)S(1)}) custom-call(s32[2]{0:T(128)S(1)} %pad_add_fusion.half_ref, bf16[784,512]{1,0:T(8,128)(2,1)S(1)} %get-tuple-element.38.block.refs_0_, bf16[784,512]{1,0:T(8,128)(2,1)S(1)} %collective-permute-done.refs_1_, ...), custom_call_target="tpu_custom_call" | custom-call | flops 3623878656 | bytes 8028160 | tf_op jit(solution)/shard_map/pairs/pallas_call | solution.py:393
  134.4 0.1 collective-permute-start.10
  134.5 3.7 %collective-permute-start.11 = (f32[8,768]{1,0:T(8,128)S(1)}, f32[8,768]{1,0:T(8,128)S(1)}, u32[]{:S(2)}, u32[]{:S(2)}) collective-permute-start(f32[8,768]{1,0:T(8,128)S(1)} %get-tuple-element.57), channel_id=1, source_target_pairs={{0,8},{1,9},{2,10},{3,11},{4,12},{5,13},{6,14},{7,15},{8,0},{9,1},... | collective-permute-start | bytes 73736 | tf_op jit(solution)/shard_map/ppermute | solution.py:479
  138.1 0.0 collective-permute-start.12
  138.2 2.9 %collective-permute-start.14 = (f32[8,768]{1,0:T(8,128)S(1)}, f32[8,768]{1,0:T(8,128)S(1)}, u32[]{:S(2)}, u32[]{:S(2)}) collective-permute-start(f32[8,768]{1,0:T(8,128)S(1)} %get-tuple-element.60), channel_id=1, source_target_pairs={{0,2},{1,3},{2,0},{3,1},{4,6},{5,7},{6,4},{7,5},{8,10},{9,11},{10,... | collective-permute-start | bytes 73736 | tf_op jit(solution)/shard_map/ppermute | solution.py:479
  141.1 0.0 collective-permute-done.13.refs_4_
  141.1 0.0 collective-permute-done.10.refs_1_
  141.1 0.0 collective-permute-done.11.refs_2_
  141.1 2.1 %collective-permute-done.12.refs_3_ = f32[8,768]{1,0:T(8,128)S(1)} collective-permute-done((f32[8,768]{1,0:T(8,128)S(1)}, f32[8,768]{1,0:T(8,128)S(1)}, u32[]{:S(2)}, u32[]{:S(2)}) %collective-permute-start.12) | collective-permute-done | bytes 24608 | tf_op jit(solution)/shard_map/ppermute | solution.py:479
  143.2 0.3 collective-permute-done.14.refs_5_
  143.5 0.7 spread.1
  144.2 9.7 %all_to_all.15.back_ref = f32[8,8,384]{2,1,0:T(8,128)S(1)} all-to-all(f32[8,8,384]{2,1,0:T(8,128)S(1)} %spread.1), channel_id=1, replica_groups=mesh['tr'=8,'tc'=16] {'tr'}, dimensions={0} | all-to-all | bytes 196608 | tf_op jit(solution)/shard_map/all_to_all | solution.py:494
  153.9 1.5 unpack.1
  (4 shorter events, 0.0 us)
Async XLA Ops:
  0.6 1.4 copy-start.2
  2.0 0.7 copy-start.3
  7.5 1.5 copy-start
  9.0 5.5 %copy-start.4 = (s32[768]{0:T(1024)S(1)}, s32[768]{0:T(1024)}, u32[]{:S(2)}) copy-start(s32[768]{0:T(1024)} %lab_ref.5) | copy-start | bytes 9220
  9.0 36.9 %all-to-all-start = ((bf16[8,304,512]{2,1,0:T(8,128)(2,1)}), bf16[8,304,512]{2,1,0:T(8,128)(2,1)S(1)}, u32[]{:S(2)}, u32[]{:S(2)}) async-start(bf16[8,304,512]{2,1,0:T(8,128)(2,1)} %copy-done), calls=%async_computation | async-start | bytes 4980736 | tf_op jit(solution)/shard_map/all_to_all | solution.py:494
  17.6 1.4 copy-start.1
  45.8 40.7 %all-to-all-start.1 = ((bf16[8,288,512]{2,1,0:T(8,128)(2,1)}), bf16[8,288,512]{2,1,0:T(8,128)(2,1)}, u32[]{:S(2)}, u32[]{:S(2)}) async-start(bf16[8,288,512]{2,1,0:T(8,128)(2,1)} %copy-done.1), calls=%async_computation.1 | async-start | bytes 4718592 | tf_op jit(solution)/shard_map/all_to_all | solution.py:494
  51.8 18.6 %collective-permute-start.3 = (bf16[784,512]{1,0:T(8,128)(2,1)S(1)}, bf16[784,512]{1,0:T(8,128)(2,1)S(1)}, u32[]{:S(2)}, u32[]{:S(2)}) collective-permute-start(bf16[784,512]{1,0:T(8,128)(2,1)S(1)} %get-tuple-element.38.block.refs_0_), channel_id=1, source_target_pairs={{0,1},{1,2},{2,3},{3,0},{4,5},{5,6},{6,7},{7,4},{8,9},{9,10},{10,1... | collective-permute-start | bytes 2408456 | tf_op jit(solution)/shard_map/ppermute | solution.py:479
  53.5 20.0 %collective-permute-start = (bf16[784,512]{1,0:T(8,128)(2,1)S(1)}, bf16[784,512]{1,0:T(8,128)(2,1)S(1)}, u32[]{:S(2)}, u32[]{:S(2)}) collective-permute-start(bf16[784,512]{1,0:T(8,128)(2,1)S(1)} %get-tuple-element.38.block.refs_0_), channel_id=1, source_target_pairs={{0,12},{1,13},{2,14},{3,15},{4,0},{5,1},{6,2},{7,3},{8,4},{9,5},{1... | collective-permute-start | bytes 2408456 | tf_op jit(solution)/shard_map/ppermute | solution.py:479
  54.0 20.0 %collective-permute-start.2 = (bf16[784,512]{1,0:T(8,128)(2,1)S(1)}, bf16[784,512]{1,0:T(8,128)(2,1)S(1)}, u32[]{:S(2)}, u32[]{:S(2)}) collective-permute-start(bf16[784,512]{1,0:T(8,128)(2,1)S(1)} %get-tuple-element.38.block.refs_0_), channel_id=1, source_target_pairs={{0,3},{1,0},{2,1},{3,2},{4,7},{5,4},{6,5},{7,6},{8,11},{9,8},{10,9... | collective-permute-start | bytes 2408456 | tf_op jit(solution)/shard_map/ppermute | solution.py:479
  70.5 14.3 %collective-permute-start.4 = (bf16[784,512]{1,0:T(8,128)(2,1)S(1)}, bf16[784,512]{1,0:T(8,128)(2,1)S(1)}, u32[]{:S(2)}, u32[]{:S(2)}) collective-permute-start(bf16[784,512]{1,0:T(8,128)(2,1)S(1)} %collective-permute-done.3.refs_3_), channel_id=1, source_target_pairs={{0,1},{1,2},{2,3},{3,0},{4,5},{5,6},{6,7},{7,4},{8,9},{9,10},{10,1... | collective-permute-start | bytes 2408456 | tf_op jit(solution)/shard_map/ppermute | solution.py:479
  72.6 0.9 copy-start.9
  73.5 12.2 %collective-permute-start.1 = (bf16[784,512]{1,0:T(8,128)(2,1)S(1)}, bf16[784,512]{1,0:T(8,128)(2,1)S(1)}, u32[]{:S(2)}, u32[]{:S(2)}) collective-permute-start(bf16[784,512]{1,0:T(8,128)(2,1)S(1)} %collective-permute-done.refs_1_), channel_id=1, source_target_pairs={{0,12},{1,13},{2,14},{3,15},{4,0},{5,1},{6,2},{7,3},{8,4},{9,5},{1... | collective-permute-start | bytes 2408456 | tf_op jit(solution)/shard_map/ppermute | solution.py:479
  84.7 0.9 copy-start.5
  85.6 0.9 copy-start.7
  89.8 12.2 %collective-permute-start.5 = (bf16[768,512]{1,0:T(8,128)(2,1)S(1)}, bf16[768,512]{1,0:T(8,128)(2,1)}, u32[]{:S(2)}, u32[]{:S(2)}) collective-permute-start(bf16[768,512]{1,0:T(8,128)(2,1)S(1)} %compact_rest.1.rest.refs_2_.refs_4_.refs_5_), channel_id=1, source_target_pairs={{0,12},{1,13},{2,14},{3,15},{4,0},{5,1},{6,2},{7,3},{8,4},{9,5},{1... | collective-permute-start | bytes 2359304 | tf_op jit(solution)/shard_map/ppermute | solution.py:479
  91.2 20.6 %collective-permute-start.8 = (bf16[768,512]{1,0:T(8,128)(2,1)S(1)}, bf16[768,512]{1,0:T(8,128)(2,1)}, u32[]{:S(2)}, u32[]{:S(2)}) collective-permute-start(bf16[768,512]{1,0:T(8,128)(2,1)S(1)} %compact_rest.1.rest.refs_2_.refs_4_.refs_5_), channel_id=1, source_target_pairs={{0,1},{1,2},{2,3},{3,0},{4,5},{5,6},{6,7},{7,4},{8,9},{9,10},{10,1... | collective-permute-start | bytes 2359304 | tf_op jit(solution)/shard_map/ppermute | solution.py:479
  93.7 21.0 %collective-permute-start.6 = (bf16[768,512]{1,0:T(8,128)(2,1)S(1)}, bf16[768,512]{1,0:T(8,128)(2,1)}, u32[]{:S(2)}, u32[]{:S(2)}) collective-permute-start(bf16[768,512]{1,0:T(8,128)(2,1)S(1)} %compact_rest.1.rest.refs_2_.refs_4_.refs_5_), channel_id=1, source_target_pairs={{0,3},{1,0},{2,1},{3,2},{4,7},{5,4},{6,5},{7,6},{8,11},{9,8},{10,9... | collective-permute-start | bytes 2359304 | tf_op jit(solution)/shard_map/ppermute | solution.py:479
  96.5 18.2 %copy-start.10 = (bf16[784,512]{1,0:T(8,128)(2,1)S(1)}, bf16[784,512]{1,0:T(8,128)(2,1)}, u32[]{:S(2)}) copy-start(bf16[784,512]{1,0:T(8,128)(2,1)} %copy-done.9) | copy-start | bytes 2408452
  111.8 15.2 %collective-permute-start.9 = (bf16[768,512]{1,0:T(8,128)(2,1)}, bf16[768,512]{1,0:T(8,128)(2,1)S(1)}, u32[]{:S(2)}, u32[]{:S(2)}) collective-permute-start(bf16[768,512]{1,0:T(8,128)(2,1)} %collective-permute-done.8.refs_7_), channel_id=1, source_target_pairs={{0,1},{1,2},{2,3},{3,0},{4,5},{5,6},{6,7},{7,4},{8,9},{9,10},{10,1... | collective-permute-start | bytes 2359304 | tf_op jit(solution)/shard_map/ppermute | solution.py:479
  113.4 13.6 %collective-permute-start.7 = (bf16[768,512]{1,0:T(8,128)(2,1)}, bf16[768,512]{1,0:T(8,128)(2,1)S(1)}, u32[]{:S(2)}, u32[]{:S(2)}) collective-permute-start(bf16[768,512]{1,0:T(8,128)(2,1)} %collective-permute-done.5.refs_3_.refs_5_.refs_6_), channel_id=1, source_target_pairs={{0,12},{1,13},{2,14},{3,15},{4,0},{5,1},{6,2},{7,3},{8,4},{9,5},{1... | collective-permute-start | bytes 2359304 | tf_op jit(solution)/shard_map/ppermute | solution.py:479
  114.7 12.3 %copy-start.6 = (bf16[784,512]{1,0:T(8,128)(2,1)S(1)}, bf16[784,512]{1,0:T(8,128)(2,1)}, u32[]{:S(2)}) copy-start(bf16[784,512]{1,0:T(8,128)(2,1)} %copy-done.5) | copy-start | bytes 2408452
  114.7 12.4 %copy-start.8 = (bf16[784,512]{1,0:T(8,128)(2,1)S(1)}, bf16[784,512]{1,0:T(8,128)(2,1)}, u32[]{:S(2)}) copy-start(bf16[784,512]{1,0:T(8,128)(2,1)} %copy-done.7) | copy-start | bytes 2408452
  123.5 17.6 %collective-permute-start.13 = (f32[8,768]{1,0:T(8,128)S(1)}, f32[8,768]{1,0:T(8,128)S(1)}, u32[]{:S(2)}, u32[]{:S(2)}) collective-permute-start(f32[8,768]{1,0:T(8,128)S(1)} %get-tuple-element.59), channel_id=1, source_target_pairs={{0,3},{1,0},{2,1},{3,2},{4,7},{5,4},{6,5},{7,6},{8,11},{9,8},{10,9... | collective-permute-start | bytes 73736 | tf_op jit(solution)/shard_map/ppermute | solution.py:479
  134.4 6.7 %collective-permute-start.10 = (f32[8,768]{1,0:T(8,128)S(1)}, f32[8,768]{1,0:T(8,128)S(1)}, u32[]{:S(2)}, u32[]{:S(2)}) collective-permute-start(f32[8,768]{1,0:T(8,128)S(1)} %get-tuple-element.56), channel_id=1, source_target_pairs={{0,4},{1,5},{2,6},{3,7},{4,8},{5,9},{6,10},{7,11},{8,12},{9,13},{1... | collective-permute-start | bytes 73736 | tf_op jit(solution)/shard_map/ppermute | solution.py:479
  134.5 6.6 %collective-permute-start.11 = (f32[8,768]{1,0:T(8,128)S(1)}, f32[8,768]{1,0:T(8,128)S(1)}, u32[]{:S(2)}, u32[]{:S(2)}) collective-permute-start(f32[8,768]{1,0:T(8,128)S(1)} %get-tuple-element.57), channel_id=1, source_target_pairs={{0,8},{1,9},{2,10},{3,11},{4,12},{5,13},{6,14},{7,15},{8,0},{9,1},... | collective-permute-start | bytes 73736 | tf_op jit(solution)/shard_map/ppermute | solution.py:479
  138.1 5.0 %collective-permute-start.12 = (f32[8,768]{1,0:T(8,128)S(1)}, f32[8,768]{1,0:T(8,128)S(1)}, u32[]{:S(2)}, u32[]{:S(2)}) collective-permute-start(f32[8,768]{1,0:T(8,128)S(1)} %get-tuple-element.58), channel_id=1, source_target_pairs={{0,1},{1,2},{2,3},{3,0},{4,5},{5,6},{6,7},{7,4},{8,9},{9,10},{10,1... | collective-permute-start | bytes 73736 | tf_op jit(solution)/shard_map/ppermute | solution.py:479
  138.2 5.3 %collective-permute-start.14 = (f32[8,768]{1,0:T(8,128)S(1)}, f32[8,768]{1,0:T(8,128)S(1)}, u32[]{:S(2)}, u32[]{:S(2)}) collective-permute-start(f32[8,768]{1,0:T(8,128)S(1)} %get-tuple-element.60), channel_id=1, source_target_pairs={{0,2},{1,3},{2,0},{3,1},{4,6},{5,7},{6,4},{7,5},{8,10},{9,11},{10,... | collective-permute-start | bytes 73736 | tf_op jit(solution)/shard_map/ppermute | solution.py:479

commit v5 on v4

--- a/solution.py
+++ b/solution.py
@@ -12,7 +12,8 @@
 SIDE = 4
 ROWS = 768
 WIDTH = 1024
-PIECE = 512
+PIECES = (384, 384, 256)
+PIECE = PIECES[0]
 CAP = 288
 TAIL = 16
 PAIR = CAP + TAIL
@@ -67,7 +68,8 @@
     return (iota((slots, ROWS), 0) == slot).astype(F32).astype(BF)
 
 
-def pack_first_kernel(emb_ref, lab_ref, out_ref, rank_ref, rest_ref, unit):
+def pack_first_kernel(emb_ref, lab_ref, out_ref, rank_ref, *refs):
+    *rests, unit = refs
     g = pl.program_id(0)
     lab = lab_ref[...].reshape(1, ROWS)
 
@@ -76,8 +78,11 @@
         values = emb_ref[...].astype(F32)
         total = jnp.sum(values * values, axis=1, keepdims=True)
         rows = (values * lax.rsqrt(total + EPSILON)).astype(BF)
-        unit[...] = rows[:, :PIECE]
-        rest_ref[...] = rows[:, PIECE:]
+        start = 0
+        for ref in (unit, *rests):
+            stop = start + ref.shape[1]
+            ref[...] = rows[:, start:stop]
+            start = stop
         owner = lax.shift_right_logical(lab, GROUP_SHIFT)
         onehot = (iota((TILE_ROWS, ROWS), 0) == owner).astype(F32)
         before = (iota((ROWS, ROWS), 0) < iota((ROWS, ROWS), 1)).astype(F32).astype(BF)
@@ -87,8 +92,7 @@
     chosen = pick(lab_ref, rank_ref, g, LANES)
     out_ref[0] = dot(chosen[:PAIR], unit[...]).astype(BF)
     marks = jnp.broadcast_to(lab.astype(F32) + 1.0, (TAIL, ROWS)).astype(BF)
-    out_ref[0, CAP:, :LANES] = (dot_nt(marks, chosen) - 1.0).astype(BF)
-    out_ref[0, CAP:, LANES:] = jnp.zeros((TAIL, PIECE - LANES), BF)
+    out_ref[0, CAP:] = (dot_nt(marks, chosen) - 1.0).astype(BF)
 
 
 def pack_first(embeddings, labels):
@@ -99,13 +103,13 @@
         out_specs=[
             pl.BlockSpec((1, PAIR, PIECE), lambda g: (g, 0, 0)),
             whole((1, ROWS)),
-            whole((ROWS, WIDTH - PIECE)),
-        ],
+        ]
+        + [whole((ROWS, w)) for w in PIECES[1:]],
         out_shape=[
             jax.ShapeDtypeStruct((TILE_ROWS, PAIR, PIECE), BF),
             jax.ShapeDtypeStruct((1, ROWS), jnp.int32),
-            jax.ShapeDtypeStruct((ROWS, WIDTH - PIECE), BF),
-        ],
+        ]
+        + [jax.ShapeDtypeStruct((ROWS, w), BF) for w in PIECES[1:]],
         scratch_shapes=[pltpu.VMEM((ROWS, PIECE), BF)],
         compiler_params=params(),
         name="pack_first",
@@ -166,10 +170,7 @@
         offset = offset + count
     close_gaps(got_ref, rows, offsets, counts)
     out_ref[:ROWS] = rows[:ROWS]
-    second = jnp.concatenate(
-        [names[:, PIECE:ROWS], jnp.zeros((8, 2 * PIECE - ROWS), F32)], axis=1
-    )
-    out_ref[ROWS:] = jnp.concatenate([names[:, :PIECE], second], axis=0).astype(BF)
+    out_ref[ROWS:] = jnp.concatenate([names[:, :PIECE], names[:, PIECE:ROWS]], axis=0).astype(BF)
 
 
 def compact_first(got):
@@ -229,7 +230,7 @@
 
 def spread_names(block):
     tail = block[ROWS:].astype(F32)
-    names = jnp.concatenate([tail[:1], tail[8:9, : ROWS - PIECE]], axis=1)
+    names = jnp.concatenate([tail[:1], tail[8:9]], axis=1)
     return names, jnp.transpose(jnp.broadcast_to(names, (128, ROWS)))
 
 
@@ -247,12 +248,15 @@
     )
 
 
-def own_kernel(block, rest, out, scores):
+def own_kernel(block, *refs):
+    *rests, out, scores = refs
     names, marks = spread_names(block)
     top = jnp.full((8, ROWS), FLOOR, F32)
     for start in range(0, ROWS, CHUNK):
         sims = dot_nt(block[start : start + CHUNK], block[:ROWS])
-        sims = (sims + dot_nt(rest[start : start + CHUNK], rest[...])) * SCALE2
+        for rest in rests:
+            sims += dot_nt(rest[start : start + CHUNK], rest[...])
+        sims = sims * SCALE2
         mask = (across(marks[start : start + CHUNK]) == names) & (
             iota((CHUNK, ROWS), 0) + start != iota((CHUNK, ROWS), 1)
         )
@@ -269,11 +273,11 @@
     put_stats(out, gather_columns(top, total, weight))
 
 
-def own_pairs(block, rest):
+def own_pairs(pieces):
     return pl.pallas_call(
         own_kernel,
         out_shape=jax.ShapeDtypeStruct((8, ROWS), F32),
-        in_specs=[vmem(), vmem()],
+        in_specs=[vmem()] * len(pieces),
         out_specs=vmem(),
         scratch_shapes=[pltpu.VMEM((ROWS, ROWS), F32)],
         compiler_params=params(),
@@ -283,14 +287,16 @@
             transcendentals=ROWS * ROWS,
         ),
         name="own",
-    )(block, rest)
+    )(*pieces)
 
 
 def pair_kernel(plan, blocks, old, half_ref, *refs):
     n, n_old = len(blocks), len(old)
-    ins, rests, olds = refs[:n], refs[n : 2 * n], refs[2 * n : 2 * n + n_old]
-    outs = refs[2 * n + n_old : 3 * n + n_old]
-    marks, names, rows, tops, totals, weights, scores0, scores1 = refs[3 * n + n_old :]
+    m = len(PIECES)
+    pieces = [refs[i * n : (i + 1) * n] for i in range(m)]
+    ins, olds = pieces[0], refs[m * n : m * n + n_old]
+    outs = refs[m * n + n_old : (m + 1) * n + n_old]
+    marks, names, rows, tops, totals, weights, scores0, scores1 = refs[(m + 1) * n + n_old :]
     scores = (scores0, scores1)
     place = {b: i for i, b in enumerate(blocks)}
     lane = iota((1, 128), 1)
@@ -334,7 +340,7 @@
             keys = jnp.where(first, left[here], right[here])
             return dot_nt(keys, jnp.where(first, right[:ROWS], left[:ROWS]))
 
-        out[...] = multiply(ins) + multiply(rests)
+        out[...] = sum(multiply(p) for p in pieces)
 
     def reduce(step, data):
         k, left, right, start, _, _ = step
@@ -393,7 +399,7 @@
     return pl.pallas_call(
         functools.partial(pair_kernel, plan, names, list(old)),
         out_shape=[jax.ShapeDtypeStruct((8, ROWS), F32)] * n,
-        in_specs=[smem()] + [vmem()] * (2 * n) + [vmem()] * len(old),
+        in_specs=[smem()] + [vmem()] * (len(PIECES) * n) + [vmem()] * len(old),
         out_specs=[vmem()] * n,
         scratch_shapes=[
             pltpu.VMEM((n, ROWS, 128), F32),
@@ -412,7 +418,7 @@
             transcendentals=2 * steps * HALF * ROWS,
         ),
         name="pairs",
-    )(halves, *[b[0] for b in blocks.values()], *[b[1] for b in blocks.values()], *old.values())
+    )(halves, *[b[i] for i in range(len(PIECES)) for b in blocks.values()], *old.values())
 
 
 def spread_kernel(offset_ref, *refs):
@@ -425,13 +431,17 @@
     values = jnp.concatenate([values, jnp.zeros((8, SPAN - ROWS), F32)], axis=1)
     for r in range(TILE_ROWS):
         offset = offset_ref[r]
-        out_ref[r] = pltpu.roll(values, lax.rem(SPAN - offset, SPAN), 1)[:, :LANES]
+        moved = pltpu.roll(values, lax.rem(SPAN - offset, SPAN), 1)
+        for k in range(6):
+            lanes = slice(k % 3 * 128, k % 3 * 128 + 128)
+            out_ref[r, k : k + 1] = moved[k // 3 : k // 3 + 1, lanes]
+        out_ref[r, 6:] = jnp.zeros((2, 128), F32)
 
 
 def spread(offsets, stats):
     return pl.pallas_call(
         spread_kernel,
-        out_shape=jax.ShapeDtypeStruct((TILE_ROWS, 8, LANES), F32),
+        out_shape=jax.ShapeDtypeStruct((TILE_ROWS, 8, 128), F32),
         in_specs=[pl.BlockSpec(memory_space=pltpu.SMEM)]
         + [pl.BlockSpec(memory_space=pltpu.VMEM)] * len(stats),
         out_specs=pl.BlockSpec(memory_space=pltpu.VMEM),
@@ -444,7 +454,9 @@
     found = jnp.zeros((24, ROWS), F32)
     for g in range(TILE_ROWS):
         chosen = pick(lab_ref, rank_ref, g, LANES)
-        values = back_ref[g]
+        rows = [back_ref[g, k : k + 1] for k in range(6)]
+        best, mean = jnp.concatenate(rows[:3], axis=1), jnp.concatenate(rows[3:], axis=1)
+        values = jnp.concatenate([best, mean, jnp.zeros((6, LANES), F32)], axis=0)
         high = values.astype(BF).astype(F32)
         mid = (values - high).astype(BF).astype(F32)
         low = values - high - mid
@@ -493,30 +505,40 @@
     def exchange(packed):
         return lax.all_to_all(packed, "tr", split_axis=0, concat_axis=0, tiled=True)
 
-    packed, rank, unit = pack_first(embeddings, labels)
+    packed, rank, *units = pack_first(embeddings, labels)
     got = exchange(packed)
-    packed = pack_rest(unit, labels, rank)
-    packed, got = tie((packed, got))
-    got_rest = exchange(packed)
-    mine, place = compact_first(got)
-    a, c, d = shift(mine, -1, 0), shift(mine, 0, -1), shift(mine, 0, 1)
-    b, e = shift(a, -1, 0), shift(d, 0, 1)
-    got_rest, a, b, c, d, e = tie((got_rest, a, b, c, d, e))
-    mine2 = compact_rest(place, got_rest)
-    a2, c2, d2 = shift(mine2, -1, 0), shift(mine2, 0, -1), shift(mine2, 0, 1)
-    own = own_pairs(mine, mine2)
-    a2, own, halves = tie((a2, own, halves))
-    b2 = shift(a2, -1, 0)
-    blocks = {"O": (mine, mine2), "A": (a, a2)}
-    stats = dict(zip(blocks, pairs(FIRST, blocks, {"O": own}, halves)))
-    d2, stats["O"] = tie((d2, stats["O"]))
-    e2 = shift(d2, 0, 1)
-    blocks.update(C=(c, c2), D=(d, d2))
-    stats.update(zip(blocks, pairs(NEAR, blocks, stats, halves)))
-    blocks.update(B=(b, b2), E=(e, e2))
-    del blocks["D"]
-    far = pairs(FAR, blocks, {q: stats[q] for q in "OAC"}, halves)
-    stats.update(zip(blocks, far))
+    blocks = {q: [] for q in "OABCDE"}
+    place = None
+    last = len(PIECES) - 1
+    for k in range(len(PIECES)):
+        if k < last:
+            packed = pack_rest(units[k], labels, rank)
+            packed, got = tie((packed, got))
+            later = exchange(packed)
+        if k == 0:
+            mine, place = compact_first(got)
+        else:
+            mine = compact_rest(place, got)
+        a, c, d = shift(mine, -1, 0), shift(mine, 0, -1), shift(mine, 0, 1)
+        if k == last:
+            own = own_pairs([*blocks["O"], mine])
+            a, own, halves = tie((a, own, halves))
+        b = shift(a, -1, 0)
+        if k == last:
+            sides = {"O": [*blocks["O"], mine], "A": [*blocks["A"], a]}
+            stats = dict(zip(sides, pairs(FIRST, sides, {"O": own}, halves)))
+            d, stats["O"] = tie((d, stats["O"]))
+        e = shift(d, 0, 1)
+        if k < last:
+            got, a, b, c, d, e = tie((later, a, b, c, d, e))
+        for q, piece in zip("OABCDE", (mine, a, b, c, d, e)):
+            blocks[q].append(piece)
+    near = {q: blocks[q] for q in "OACD"}
+    stats.update(zip(near, pairs(NEAR, near, stats, halves)))
+    wide = {q: blocks[q] for q in "OACBE"}
+    far = pairs(FAR, wide, {q: stats[q] for q in "OAC"}, halves)
+    stats.update(zip(wide, far))
+    stats["D"], stats["B"] = tie((stats["D"], stats["B"]))
     parts = [stats["O"]] + [shift(stats[q], *PLACES[q]) for q in "ABCDE"]
     sent = spread(place, parts)
     back = exchange(sent)

time: 158 us -> 164 us (1.038); the launches traced: 155 us -> 164 us
  waiting for transfers between devices: 66.6 us -> 52.2 us
  starting transfers between devices: 34.1 us -> 45.5 us
  Pallas kernels: 36.5 us -> 46.4 us
    ppermute x15 -> x20, waiting for transfers between devices: 39.8 us -> 30.4 us  [shift(): return lax.ppermute(array, ('tr', 'tc'), moves)]
    ppermute x15 -> x20, starting transfers between devices: 24.3 us -> 31.3 us  [shift(): return lax.ppermute(array, ('tr', 'tc'), moves)]
    all_to_all x2 -> x3, waiting for transfers between devices: 26.7 us -> 21.8 us  [exchange(): return lax.all_to_all(packed, 'tr', split_axis=0, concat_axis=0, tiled=True)]
    all_to_all x2 -> x3, starting transfers between devices: 9.81 us -> 14.2 us  [exchange(): return lax.all_to_all(packed, 'tr', split_axis=0, concat_axis=0, tiled=True)]
    pallas_call x3, Pallas kernels: 19.5 us -> 23.8 us  [pairs(): pl.pallas_call(functools.partial(pair_kernel, plan, names, list(old)), ou...]
    pallas_call x1 -> x2, Pallas kernels: 3.22 us -> 7.43 us  [pack_rest(): pl.pallas_call(pack_rest_kernel, grid=(TILE_ROWS,), in_specs=[whole((ROWS...]
    pallas_call x1 -> x2, Pallas kernels: 3.17 us -> 4.38 us  [compact_rest(): pl.pallas_call(compact_rest_kernel, in_specs=[smem(), vmem()], out_specs=...]
    unnamed x22 -> x34, local copies, waits for them, and re-layouts: 7.69 us -> 8.67 us
  transfers between devices with their start and end apart: 17 -> 23, of which waited for: 7 -> 8; matrix products, arithmetic and copies ran while one was open for 0% -> 0% of each run, Pallas kernels for 17% -> 16%
where the time goes in v5:
time: 164 us
  waiting for transfers between devices  52.2 us (32%)
  Pallas kernels  46.4 us (28%)
  starting transfers between devices  45.5 us (28%)
  blocking collectives  10 us (6%)
  local copies, waits for them, and re-layouts  8.67 us (5%)
    ppermute x20, starting transfers between devices, shift(): return lax.ppermute(array, ('tr', 'tc'), moves)  31.3 us
    ppermute x20, waiting for transfers between devices, shift(): return lax.ppermute(array, ('tr', 'tc'), moves)  30.4 us
    pallas_call x3, Pallas kernels, pairs(): pl.pallas_call(functools.partial(pair_kernel, plan, names, list(old)), ou...  23.8 us
    all_to_all x3, waiting for transfers between devices, exchange(): return lax.all_to_all(packed, 'tr', split_axis=0, concat_axis=0, tiled=True)  21.8 us
    all_to_all x3, starting transfers between devices, exchange(): return lax.all_to_all(packed, 'tr', split_axis=0, concat_axis=0, tiled=True)  14.2 us
    all_to_all x1, blocking collectives, exchange(): return lax.all_to_all(packed, 'tr', split_axis=0, concat_axis=0, tiled=True)  10 us
    unnamed x34, local copies, waits for them, and re-layouts  8.67 us
    pallas_call x2, Pallas kernels, pack_rest(): pl.pallas_call(pack_rest_kernel, grid=(TILE_ROWS,), in_specs=[whole((ROWS...  7.43 us
  transfers between devices with their start and end apart: 23, of which 8 were waited for; matrix products, arithmetic and copies ran while one was open for 0% of the time, Pallas kernels for 16%

profile of v5, /device:TPU:2, one launch (start us, length us, event | category | flops | bytes accessed | tf_op | source)
XLA Modules:
  0.0 163.7 jit_solution(9730642820460103521)
XLA Ops:
  0.6 1.4 copy-done.2
  2.0 0.7 copy-done.3
  2.7 4.7 %pack_first.1 = (bf16[8,304,384]{2,1,0:T(8,128)(2,1)S(1)}, s32[1,768]{1,0:T(1,128)S(1)}, bf16[768,384]{1,0:T(8,128)(2,1)S(1)}, bf16[768,256]{1,0:T(8,128)(2,1)S(1)}) custom-call(bf16[768,1024]{1,0:T(8,128)(2,1)S(1)} %copy-done.2, s32[768]{0:T(1024)S(1)} %copy-done.3), custom_call_target="tpu_custom_call" | custom-call | tf_op jit(solution)/shard_map/pack_first/pallas_call | solution.py:99
  7.5 1.2 copy-done
  8.7 0.8 copy-done.15
  9.5 5.4 %all-to-all-start = ((bf16[8,304,384]{2,1,0:T(8,128)(2,1)}), bf16[8,304,384]{2,1,0:T(8,128)(2,1)S(1)}, u32[]{:S(2)}, u32[]{:S(2)}) async-start(bf16[8,304,384]{2,1,0:T(8,128)(2,1)} %copy-done), calls=%async_computation | async-start | bytes 3735552 | tf_op jit(solution)/shard_map/all_to_all | solution.py:506
  14.9 3.2 %pack_rest.2 = bf16[8,288,384]{2,1,0:T(8,128)(2,1)S(1)} custom-call(bf16[768,384]{1,0:T(8,128)(2,1)S(1)} %get-tuple-element.43.unit_ref, s32[768]{0:T(1024)S(1)} %copy-done.4, s32[1,768]{1,0:T(1,128)S(1)} %get-tuple-element.44.rank_ref), custom_call_target="tpu_custom_call" | custom-call | flops 1358954496 | bytes 1769472 | tf_op jit(solution)/shard_map/pack_rest/pallas_call | solution.py:126
  18.2 1.2 copy-done.1
  19.4 20.2 %all-to-all-done.got_ref = bf16[8,304,384]{2,1,0:T(8,128)(2,1)S(1)} async-done(((bf16[8,304,384]{2,1,0:T(8,128)(2,1)}), bf16[8,304,384]{2,1,0:T(8,128)(2,1)S(1)}, u32[]{:S(2)}, u32[]{:S(2)}) %all-to-all-start) | async-done | bytes 1867808 | tf_op jit(solution)/shard_map/all_to_all | solution.py:506
  39.7 4.3 %all-to-all-start.1 = ((bf16[8,288,384]{2,1,0:T(8,128)(2,1)}), bf16[8,288,384]{2,1,0:T(8,128)(2,1)}, u32[]{:S(2)}, u32[]{:S(2)}) async-start(bf16[8,288,384]{2,1,0:T(8,128)(2,1)} %copy-done.1), calls=%async_computation.1 | async-start | bytes 3538944 | tf_op jit(solution)/shard_map/all_to_all | solution.py:506
  44.0 1.6 compact_first.1
  45.6 1.6 %collective-permute-start.3 = (bf16[784,384]{1,0:T(8,128)(2,1)S(1)}, bf16[784,384]{1,0:T(8,128)(2,1)S(1)}, u32[]{:S(2)}, u32[]{:S(2)}) collective-permute-start(bf16[784,384]{1,0:T(8,128)(2,1)S(1)} %get-tuple-element.50.block.refs_0_), channel_id=1, source_target_pairs={{0,1},{1,2},{2,3},{3,0},{4,5},{5,6},{6,7},{7,4},{8,9},{9,10},{10,1... | collective-permute-start | bytes 1806344 | tf_op jit(solution)/shard_map/ppermute | solution.py:491
  47.3 0.5 collective-permute-start
  47.8 1.7 %collective-permute-start.2 = (bf16[784,384]{1,0:T(8,128)(2,1)S(1)}, bf16[784,384]{1,0:T(8,128)(2,1)S(1)}, u32[]{:S(2)}, u32[]{:S(2)}) collective-permute-start(bf16[784,384]{1,0:T(8,128)(2,1)S(1)} %get-tuple-element.50.block.refs_0_), channel_id=1, source_target_pairs={{0,3},{1,0},{2,1},{3,2},{4,7},{5,4},{6,5},{7,6},{8,11},{9,8},{10,9... | collective-permute-start | bytes 1806344 | tf_op jit(solution)/shard_map/ppermute | solution.py:491
  49.5 10.5 %collective-permute-done.3.refs_3_ = bf16[784,384]{1,0:T(8,128)(2,1)S(1)} collective-permute-done((bf16[784,384]{1,0:T(8,128)(2,1)S(1)}, bf16[784,384]{1,0:T(8,128)(2,1)S(1)}, u32[]{:S(2)}, u32[]{:S(2)}) %collective-permute-start.3) | collective-permute-done | bytes 602144 | tf_op jit(solution)/shard_map/ppermute | solution.py:491
  59.9 2.1 %collective-permute-start.4 = (bf16[784,384]{1,0:T(8,128)(2,1)S(1)}, bf16[784,384]{1,0:T(8,128)(2,1)S(1)}, u32[]{:S(2)}, u32[]{:S(2)}) collective-permute-start(bf16[784,384]{1,0:T(8,128)(2,1)S(1)} %collective-permute-done.3.refs_3_), channel_id=1, source_target_pairs={{0,1},{1,2},{2,3},{3,0},{4,5},{5,6},{6,7},{7,4},{8,9},{9,10},{10,1... | collective-permute-start | bytes 1806344 | tf_op jit(solution)/shard_map/ppermute | solution.py:491
  62.1 0.0 collective-permute-done.refs_1_
  62.1 0.5 collective-permute-start.1
  62.6 4.2 %pack_rest.3 = bf16[8,288,256]{2,1,0:T(8,128)(2,1)} custom-call(bf16[768,256]{1,0:T(8,128)(2,1)S(1)} %copy-done.16, s32[768]{0:T(1024)S(1)} %copy-done.4, s32[1,768]{1,0:T(1,128)S(1)} %get-tuple-element.44.rank_ref), custom_call_target="tpu_custom_call" | custom-call | flops 905969664 | bytes 1179648 | tf_op jit(solution)/shard_map/pack_rest/pallas_call | solution.py:126
  66.8 0.8 copy-done.5
  67.7 4.4 %collective-permute-done.4.refs_4_ = bf16[784,384]{1,0:T(8,128)(2,1)S(1)} collective-permute-done((bf16[784,384]{1,0:T(8,128)(2,1)S(1)}, bf16[784,384]{1,0:T(8,128)(2,1)S(1)}, u32[]{:S(2)}, u32[]{:S(2)}) %collective-permute-start.4) | collective-permute-done | bytes 602144 | tf_op jit(solution)/shard_map/ppermute | solution.py:491
  72.1 0.8 copy-done.7
  72.9 0.0 collective-permute-done.1.refs_3_
  72.9 0.8 copy-done.11
  73.7 0.0 all-to-all-done.1.got_ref
  73.7 3.0 %compact_rest.2.refs_0_.refs_2_.refs_4_.refs_5_ = bf16[768,384]{1,0:T(8,128)(2,1)S(1)} custom-call(s32[16]{0:T(128)S(1)} %get-tuple-element.47.place_ref.offset_ref, bf16[8,288,384]{2,1,0:T(8,128)(2,1)} %all-to-all-done.1.got_ref), custom_call_target="tpu_custom_call" | custom-call | tf_op jit(solution)/shard_map/compact_rest/pallas_call | solution.py:199
  76.7 1.8 %collective-permute-start.8 = (bf16[768,384]{1,0:T(8,128)(2,1)S(1)}, bf16[768,384]{1,0:T(8,128)(2,1)}, u32[]{:S(2)}, u32[]{:S(2)}) collective-permute-start(bf16[768,384]{1,0:T(8,128)(2,1)S(1)} %compact_rest.2.refs_0_.refs_2_.refs_4_.refs_5_), channel_id=1, source_target_pairs={{0,1},{1,2},{2,3},{3,0},{4,5},{5,6},{6,7},{7,4},{8,9},{9,10},{10,1... | collective-permute-start | bytes 1769480 | tf_op jit(solution)/shard_map/ppermute | solution.py:491
  78.5 1.3 collective-permute-start.5
  79.8 4.4 %all-to-all-start.2 = ((bf16[8,288,256]{2,1,0:T(8,128)(2,1)}), bf16[8,288,256]{2,1,0:T(8,128)(2,1)S(1)}, u32[]{:S(2)}, u32[]{:S(2)}) async-start(bf16[8,288,256]{2,1,0:T(8,128)(2,1)} %pack_rest.3), calls=%async_computation.2 | async-start | bytes 2359296 | tf_op jit(solution)/shard_map/all_to_all | solution.py:506
  84.3 1.3 collective-permute-start.7
  85.6 2.4 %collective-permute-done.8.refs_7_ = bf16[768,384]{1,0:T(8,128)(2,1)} collective-permute-done((bf16[768,384]{1,0:T(8,128)(2,1)S(1)}, bf16[768,384]{1,0:T(8,128)(2,1)}, u32[]{:S(2)}, u32[]{:S(2)}) %collective-permute-start.8) | collective-permute-done | bytes 589856 | tf_op jit(solution)/shard_map/ppermute | solution.py:491
  88.0 0.5 collective-permute-start.9
  88.5 0.0 collective-permute-done.5.refs_3_.refs_5_.refs_6_
  88.5 2.4 %collective-permute-start.6 = (bf16[768,384]{1,0:T(8,128)(2,1)}, bf16[768,384]{1,0:T(8,128)(2,1)}, u32[]{:S(2)}, u32[]{:S(2)}) collective-permute-start(bf16[768,384]{1,0:T(8,128)(2,1)} %collective-permute-done.5.refs_3_.refs_5_.refs_6_), channel_id=1, source_target_pairs={{0,12},{1,13},{2,14},{3,15},{4,0},{5,1},{6,2},{7,3},{8,4},{9,5},{1... | collective-permute-start | bytes 1769480 | tf_op jit(solution)/shard_map/ppermute | solution.py:491
  90.9 8.4 %collective-permute-done.7.refs_6_.refs_7_ = bf16[768,384]{1,0:T(8,128)(2,1)S(1)} collective-permute-done((bf16[768,384]{1,0:T(8,128)(2,1)S(1)}, bf16[768,384]{1,0:T(8,128)(2,1)S(1)}, u32[]{:S(2)}, u32[]{:S(2)}) %collective-permute-start.7) | collective-permute-done | bytes 589856 | tf_op jit(solution)/shard_map/ppermute | solution.py:491
  99.3 0.8 copy-done.13
  100.1 1.5 all-to-all-done.2.got_ref
  101.6 0.0 collective-permute-done.9.refs_9_
  101.6 0.0 collective-permute-done.6.refs_8_
  101.6 1.4 compact_rest.3.refs_1_.refs_4_.refs_8_.refs_10_
  103.0 3.8 %collective-permute-start.10 = (bf16[768,256]{1,0:T(8,128)(2,1)S(1)}, bf16[768,256]{1,0:T(8,128)(2,1)S(1)}, u32[]{:S(2)}, u32[]{:S(2)}) collective-permute-start(bf16[768,256]{1,0:T(8,128)(2,1)S(1)} %compact_rest.3.refs_1_.refs_4_.refs_8_.refs_10_), channel_id=1, source_target_pairs={{0,12},{1,13},{2,14},{3,15},{4,0},{5,1},{6,2},{7,3},{8,4},{9,5},{1... | collective-permute-start | bytes 1179656 | tf_op jit(solution)/shard_map/ppermute | solution.py:491
  106.8 1.6 collective-permute-start.13
  108.4 1.6 %collective-permute-start.11 = (bf16[768,256]{1,0:T(8,128)(2,1)S(1)}, bf16[768,256]{1,0:T(8,128)(2,1)S(1)}, u32[]{:S(2)}, u32[]{:S(2)}) collective-permute-start(bf16[768,256]{1,0:T(8,128)(2,1)S(1)} %compact_rest.3.refs_1_.refs_4_.refs_8_.refs_10_), channel_id=1, source_target_pairs={{0,3},{1,0},{2,1},{3,2},{4,7},{5,4},{6,5},{7,6},{8,11},{9,8},{10,9... | collective-permute-start | bytes 1179656 | tf_op jit(solution)/shard_map/ppermute | solution.py:491
  110.0 0.1 pad_add_fusion.half_ref
  110.1 2.3 %own.1.refs_6_ = f32[8,768]{1,0:T(8,128)S(1)} custom-call(bf16[784,384]{1,0:T(8,128)(2,1)S(1)} %get-tuple-element.50.block.refs_0_, bf16[768,384]{1,0:T(8,128)(2,1)S(1)} %compact_rest.2.refs_0_.refs_2_.refs_4_.refs_5_, bf16[768,256]{1,0:T(8,128)(2,1)S(1)} %compact_rest.3.refs_1_.refs_4_.refs_8_.refs_10_), custom_call_target="tpu_custom_call" | custom-call | flops 1207959552 | bytes 1605632 | tf_op jit(solution)/shard_map/own/pallas_call | solution.py:277
  112.4 2.1 %collective-permute-start.12 = (bf16[768,256]{1,0:T(8,128)(2,1)S(1)}, bf16[768,256]{1,0:T(8,128)(2,1)S(1)}, u32[]{:S(2)}, u32[]{:S(2)}) collective-permute-start(bf16[768,256]{1,0:T(8,128)(2,1)S(1)} %collective-permute-done.10.refs_5_.refs_9_.refs_11_), channel_id=1, source_target_pairs={{0,12},{1,13},{2,14},{3,15},{4,0},{5,1},{6,2},{7,3},{8,4},{9,5},{1... | collective-permute-start | bytes 1179656 | tf_op jit(solution)/shard_map/ppermute | solution.py:491
  114.6 4.0 %pairs.3 = (f32[8,768]{1,0:T(8,128)S(1)}, f32[8,768]{1,0:T(8,128)S(1)}) custom-call(s32[2]{0:T(128)S(1)} %pad_add_fusion.half_ref, bf16[784,384]{1,0:T(8,128)(2,1)S(1)} %get-tuple-element.50.block.refs_0_, bf16[784,384]{1,0:T(8,128)(2,1)S(1)} %collective-permute-done.refs_1_, bf16[768,384]{1,0:T(8,128)(2,1)S(1)} %compact_rest.2.refs_0_.refs_2_.refs_4_.refs_5_, ...), custom_call_target="tpu_custom_call" | custom-call | flops 1207959552 | bytes 3211264 | tf_op jit(solution)/shard_map/pairs/pallas_call | solution.py:399
  118.5 0.0 collective-permute-done.13.refs_11_
  118.6 1.7 %collective-permute-start.14 = (bf16[768,256]{1,0:T(8,128)(2,1)S(1)}, bf16[768,256]{1,0:T(8,128)(2,1)S(1)}, u32[]{:S(2)}, u32[]{:S(2)}) collective-permute-start(bf16[768,256]{1,0:T(8,128)(2,1)S(1)} %collective-permute-done.13.refs_11_), channel_id=1, source_target_pairs={{0,1},{1,2},{2,3},{3,0},{4,5},{5,6},{6,7},{7,4},{8,9},{9,10},{10,1... | collective-permute-start | bytes 1179656 | tf_op jit(solution)/shard_map/ppermute | solution.py:491
  120.2 0.0 collective-permute-done.11.refs_10_.refs_12_
  120.3 10.3 %pairs.4 = (f32[8,768]{1,0:T(8,128)S(1)}, f32[8,768]{1,0:T(8,128)S(1)}, f32[8,768]{1,0:T(8,128)S(1)}, f32[8,768]{1,0:T(8,128)S(1)}) custom-call(s32[2]{0:T(128)S(1)} %pad_add_fusion.half_ref, bf16[784,384]{1,0:T(8,128)(2,1)S(1)} %get-tuple-element.50.block.refs_0_, bf16[784,384]{1,0:T(8,128)(2,1)S(1)} %collective-permute-done.refs_1_, ...), custom_call_target="tpu_custom_call" | custom-call | flops 4227858432 | bytes 6422528 | tf_op jit(solution)/shard_map/pairs/pallas_call | solution.py:399
  130.6 0.0 collective-permute-done.12.refs_13_
  130.6 9.6 %pairs.5 = (f32[8,768]{1,0:T(8,128)S(1)}, f32[8,768]{1,0:T(8,128)S(1)}, f32[8,768]{1,0:T(8,128)S(1)}, f32[8,768]{1,0:T(8,128)S(1)}, f32[8,768]{1,0:T(8,128)S(1)}) custom-call(s32[2]{0:T(128)S(1)} %pad_add_fusion.half_ref, bf16[784,384]{1,0:T(8,128)(2,1)S(1)} %get-tuple-element.50.block.refs_0_, bf16[784,384]{1,0:T(8,128)(2,1)S(1)} %collective-permute-done.refs_1_, ...), custom_call_target="tpu_custom_call" | custom-call | flops 3623878656 | bytes 8028160 | tf_op jit(solution)/shard_map/pairs/pallas_call | solution.py:399
  140.2 1.3 collective-permute-start.16
  141.5 1.2 collective-permute-start.18
  142.7 2.6 %collective-permute-start.15 = (f32[8,768]{1,0:T(8,128)S(1)}, f32[8,768]{1,0:T(8,128)S(1)}, u32[]{:S(2)}, u32[]{:S(2)}) collective-permute-start(f32[8,768]{1,0:T(8,128)S(1)} %get-tuple-element.76), channel_id=1, source_target_pairs={{0,4},{1,5},{2,6},{3,7},{4,8},{5,9},{6,10},{7,11},{8,12},{9,13},{1... | collective-permute-start | bytes 73736 | tf_op jit(solution)/shard_map/ppermute | solution.py:491
  145.3 0.8 collective-permute-start.17
  146.2 0.6 collective-permute-start.19
  146.8 0.0 collective-permute-done.15.refs_1_
  146.8 3.5 %collective-permute-done.17.refs_3_ = f32[8,768]{1,0:T(8,128)S(1)} collective-permute-done((f32[8,768]{1,0:T(8,128)S(1)}, f32[8,768]{1,0:T(8,128)S(1)}, u32[]{:S(2)}, u32[]{:S(2)}) %collective-permute-start.17) | collective-permute-done | bytes 24608 | tf_op jit(solution)/shard_map/ppermute | solution.py:491
  150.4 1.1 collective-permute-done.19.refs_5_
  151.5 0.7 spread.1
  152.2 10.0 %all_to_all.20.back_ref = f32[8,8,128]{2,1,0:T(8,128)S(1)} all-to-all(f32[8,8,128]{2,1,0:T(8,128)S(1)} %spread.1), channel_id=1, replica_groups=mesh['tr'=8,'tc'=16] {'tr'}, dimensions={0} | all-to-all | bytes 65536 | tf_op jit(solution)/shard_map/all_to_all | solution.py:506
  162.2 1.5 unpack.1
  (30 shorter events, 0.1 us)
Async XLA Ops:
  0.6 1.4 copy-start.2
  2.0 0.7 copy-start.3
  7.5 1.2 copy-start
  8.7 0.8 copy-start.15
  9.5 5.5 %copy-start.4 = (s32[768]{0:T(1024)S(1)}, s32[768]{0:T(1024)}, u32[]{:S(2)}) copy-start(s32[768]{0:T(1024)} %lab_ref.7) | copy-start | bytes 9220
  9.5 30.2 %all-to-all-start = ((bf16[8,304,384]{2,1,0:T(8,128)(2,1)}), bf16[8,304,384]{2,1,0:T(8,128)(2,1)S(1)}, u32[]{:S(2)}, u32[]{:S(2)}) async-start(bf16[8,304,384]{2,1,0:T(8,128)(2,1)} %copy-done), calls=%async_computation | async-start | bytes 3735552 | tf_op jit(solution)/shard_map/all_to_all | solution.py:506
  18.2 1.2 copy-start.1
  39.7 34.1 %all-to-all-start.1 = ((bf16[8,288,384]{2,1,0:T(8,128)(2,1)}), bf16[8,288,384]{2,1,0:T(8,128)(2,1)}, u32[]{:S(2)}, u32[]{:S(2)}) async-start(bf16[8,288,384]{2,1,0:T(8,128)(2,1)} %copy-done.1), calls=%async_computation.1 | async-start | bytes 3538944 | tf_op jit(solution)/shard_map/all_to_all | solution.py:506
  44.0 18.7 %copy-start.16 = (bf16[768,256]{1,0:T(8,128)(2,1)S(1)}, bf16[768,256]{1,0:T(8,128)(2,1)}, u32[]{:S(2)}) copy-start(bf16[768,256]{1,0:T(8,128)(2,1)} %copy-done.15) | copy-start | bytes 1179652
  45.6 14.3 %collective-permute-start.3 = (bf16[784,384]{1,0:T(8,128)(2,1)S(1)}, bf16[784,384]{1,0:T(8,128)(2,1)S(1)}, u32[]{:S(2)}, u32[]{:S(2)}) collective-permute-start(bf16[784,384]{1,0:T(8,128)(2,1)S(1)} %get-tuple-element.50.block.refs_0_), channel_id=1, source_target_pairs={{0,1},{1,2},{2,3},{3,0},{4,5},{5,6},{6,7},{7,4},{8,9},{9,10},{10,1... | collective-permute-start | bytes 1806344 | tf_op jit(solution)/shard_map/ppermute | solution.py:491
  47.3 14.8 %collective-permute-start = (bf16[784,384]{1,0:T(8,128)(2,1)S(1)}, bf16[784,384]{1,0:T(8,128)(2,1)S(1)}, u32[]{:S(2)}, u32[]{:S(2)}) collective-permute-start(bf16[784,384]{1,0:T(8,128)(2,1)S(1)} %get-tuple-element.50.block.refs_0_), channel_id=1, source_target_pairs={{0,12},{1,13},{2,14},{3,15},{4,0},{5,1},{6,2},{7,3},{8,4},{9,5},{1... | collective-permute-start | bytes 1806344 | tf_op jit(solution)/shard_map/ppermute | solution.py:491
  47.8 19.0 %collective-permute-start.2 = (bf16[784,384]{1,0:T(8,128)(2,1)S(1)}, bf16[784,384]{1,0:T(8,128)(2,1)S(1)}, u32[]{:S(2)}, u32[]{:S(2)}) collective-permute-start(bf16[784,384]{1,0:T(8,128)(2,1)S(1)} %get-tuple-element.50.block.refs_0_), channel_id=1, source_target_pairs={{0,3},{1,0},{2,1},{3,2},{4,7},{5,4},{6,5},{7,6},{8,11},{9,8},{10,9... | collective-permute-start | bytes 1806344 | tf_op jit(solution)/shard_map/ppermute | solution.py:491
  59.9 12.1 %copy-start.9 = (bf16[784,384]{1,0:T(8,128)(2,1)}, bf16[784,384]{1,0:T(8,128)(2,1)S(1)}, u32[]{:S(2)}) copy-start(bf16[784,384]{1,0:T(8,128)(2,1)S(1)} %collective-permute-done.3.refs_3_) | copy-start | bytes 1806340
  59.9 12.1 %collective-permute-start.4 = (bf16[784,384]{1,0:T(8,128)(2,1)S(1)}, bf16[784,384]{1,0:T(8,128)(2,1)S(1)}, u32[]{:S(2)}, u32[]{:S(2)}) collective-permute-start(bf16[784,384]{1,0:T(8,128)(2,1)S(1)} %collective-permute-done.3.refs_3_), channel_id=1, source_target_pairs={{0,1},{1,2},{2,3},{3,0},{4,5},{5,6},{6,7},{7,4},{8,9},{9,10},{10,1... | collective-permute-start | bytes 1806344 | tf_op jit(solution)/shard_map/ppermute | solution.py:491
  62.1 10.8 %collective-permute-start.1 = (bf16[784,384]{1,0:T(8,128)(2,1)S(1)}, bf16[784,384]{1,0:T(8,128)(2,1)S(1)}, u32[]{:S(2)}, u32[]{:S(2)}) collective-permute-start(bf16[784,384]{1,0:T(8,128)(2,1)S(1)} %collective-permute-done.refs_1_), channel_id=1, source_target_pairs={{0,12},{1,13},{2,14},{3,15},{4,0},{5,1},{6,2},{7,3},{8,4},{9,5},{1... | collective-permute-start | bytes 1806344 | tf_op jit(solution)/shard_map/ppermute | solution.py:491
  66.8 0.8 copy-start.5
  72.1 0.8 copy-start.7
  72.9 0.8 copy-start.11
  76.7 11.3 %collective-permute-start.8 = (bf16[768,384]{1,0:T(8,128)(2,1)S(1)}, bf16[768,384]{1,0:T(8,128)(2,1)}, u32[]{:S(2)}, u32[]{:S(2)}) collective-permute-start(bf16[768,384]{1,0:T(8,128)(2,1)S(1)} %compact_rest.2.refs_0_.refs_2_.refs_4_.refs_5_), channel_id=1, source_target_pairs={{0,1},{1,2},{2,3},{3,0},{4,5},{5,6},{6,7},{7,4},{8,9},{9,10},{10,1... | collective-permute-start | bytes 1769480 | tf_op jit(solution)/shard_map/ppermute | solution.py:491
  78.5 10.0 %collective-permute-start.5 = (bf16[768,384]{1,0:T(8,128)(2,1)S(1)}, bf16[768,384]{1,0:T(8,128)(2,1)}, u32[]{:S(2)}, u32[]{:S(2)}) collective-permute-start(bf16[768,384]{1,0:T(8,128)(2,1)S(1)} %compact_rest.2.refs_0_.refs_2_.refs_4_.refs_5_), channel_id=1, source_target_pairs={{0,12},{1,13},{2,14},{3,15},{4,0},{5,1},{6,2},{7,3},{8,4},{9,5},{1... | collective-permute-start | bytes 1769480 | tf_op jit(solution)/shard_map/ppermute | solution.py:491
  79.8 21.8 %all-to-all-start.2 = ((bf16[8,288,256]{2,1,0:T(8,128)(2,1)}), bf16[8,288,256]{2,1,0:T(8,128)(2,1)S(1)}, u32[]{:S(2)}, u32[]{:S(2)}) async-start(bf16[8,288,256]{2,1,0:T(8,128)(2,1)} %pack_rest.3), calls=%async_computation.2 | async-start | bytes 2359296 | tf_op jit(solution)/shard_map/all_to_all | solution.py:506
  84.3 15.0 %collective-permute-start.7 = (bf16[768,384]{1,0:T(8,128)(2,1)S(1)}, bf16[768,384]{1,0:T(8,128)(2,1)S(1)}, u32[]{:S(2)}, u32[]{:S(2)}) collective-permute-start(bf16[768,384]{1,0:T(8,128)(2,1)S(1)} %compact_rest.2.refs_0_.refs_2_.refs_4_.refs_5_), channel_id=1, source_target_pairs={{0,3},{1,0},{2,1},{3,2},{4,7},{5,4},{6,5},{7,6},{8,11},{9,8},{10,9... | collective-permute-start | bytes 1769480 | tf_op jit(solution)/shard_map/ppermute | solution.py:491
  88.0 13.6 %collective-permute-start.9 = (bf16[768,384]{1,0:T(8,128)(2,1)}, bf16[768,384]{1,0:T(8,128)(2,1)}, u32[]{:S(2)}, u32[]{:S(2)}) collective-permute-start(bf16[768,384]{1,0:T(8,128)(2,1)} %collective-permute-done.8.refs_7_), channel_id=1, source_target_pairs={{0,1},{1,2},{2,3},{3,0},{4,5},{5,6},{6,7},{7,4},{8,9},{9,10},{10,1... | collective-permute-start | bytes 1769480 | tf_op jit(solution)/shard_map/ppermute | solution.py:491
  88.5 13.2 %collective-permute-start.6 = (bf16[768,384]{1,0:T(8,128)(2,1)}, bf16[768,384]{1,0:T(8,128)(2,1)}, u32[]{:S(2)}, u32[]{:S(2)}) collective-permute-start(bf16[768,384]{1,0:T(8,128)(2,1)} %collective-permute-done.5.refs_3_.refs_5_.refs_6_), channel_id=1, source_target_pairs={{0,12},{1,13},{2,14},{3,15},{4,0},{5,1},{6,2},{7,3},{8,4},{9,5},{1... | collective-permute-start | bytes 1769480 | tf_op jit(solution)/shard_map/ppermute | solution.py:491
  99.3 0.8 copy-start.13
  103.0 9.4 %collective-permute-start.10 = (bf16[768,256]{1,0:T(8,128)(2,1)S(1)}, bf16[768,256]{1,0:T(8,128)(2,1)S(1)}, u32[]{:S(2)}, u32[]{:S(2)}) collective-permute-start(bf16[768,256]{1,0:T(8,128)(2,1)S(1)} %compact_rest.3.refs_1_.refs_4_.refs_8_.refs_10_), channel_id=1, source_target_pairs={{0,12},{1,13},{2,14},{3,15},{4,0},{5,1},{6,2},{7,3},{8,4},{9,5},{1... | collective-permute-start | bytes 1179656 | tf_op jit(solution)/shard_map/ppermute | solution.py:491
  106.8 11.7 %collective-permute-start.13 = (bf16[768,256]{1,0:T(8,128)(2,1)S(1)}, bf16[768,256]{1,0:T(8,128)(2,1)S(1)}, u32[]{:S(2)}, u32[]{:S(2)}) collective-permute-start(bf16[768,256]{1,0:T(8,128)(2,1)S(1)} %compact_rest.3.refs_1_.refs_4_.refs_8_.refs_10_), channel_id=1, source_target_pairs={{0,1},{1,2},{2,3},{3,0},{4,5},{5,6},{6,7},{7,4},{8,9},{9,10},{10,1... | collective-permute-start | bytes 1179656 | tf_op jit(solution)/shard_map/ppermute | solution.py:491
  108.4 11.8 %collective-permute-start.11 = (bf16[768,256]{1,0:T(8,128)(2,1)S(1)}, bf16[768,256]{1,0:T(8,128)(2,1)S(1)}, u32[]{:S(2)}, u32[]{:S(2)}) collective-permute-start(bf16[768,256]{1,0:T(8,128)(2,1)S(1)} %compact_rest.3.refs_1_.refs_4_.refs_8_.refs_10_), channel_id=1, source_target_pairs={{0,3},{1,0},{2,1},{3,2},{4,7},{5,4},{6,5},{7,6},{8,11},{9,8},{10,9... | collective-permute-start | bytes 1179656 | tf_op jit(solution)/shard_map/ppermute | solution.py:491
  112.4 7.8 %copy-start.6 = (bf16[784,384]{1,0:T(8,128)(2,1)S(1)}, bf16[784,384]{1,0:T(8,128)(2,1)}, u32[]{:S(2)}) copy-start(bf16[784,384]{1,0:T(8,128)(2,1)} %copy-done.5) | copy-start | bytes 1806340
  112.4 7.8 %copy-start.10 = (bf16[784,384]{1,0:T(8,128)(2,1)S(1)}, bf16[784,384]{1,0:T(8,128)(2,1)}, u32[]{:S(2)}) copy-start(bf16[784,384]{1,0:T(8,128)(2,1)} %copy-done.9) | copy-start | bytes 1806340
  112.4 7.8 %copy-start.14 = (bf16[768,384]{1,0:T(8,128)(2,1)S(1)}, bf16[768,384]{1,0:T(8,128)(2,1)}, u32[]{:S(2)}) copy-start(bf16[768,384]{1,0:T(8,128)(2,1)} %copy-done.13) | copy-start | bytes 1769476
  112.4 18.1 %collective-permute-start.12 = (bf16[768,256]{1,0:T(8,128)(2,1)S(1)}, bf16[768,256]{1,0:T(8,128)(2,1)S(1)}, u32[]{:S(2)}, u32[]{:S(2)}) collective-permute-start(bf16[768,256]{1,0:T(8,128)(2,1)S(1)} %collective-permute-done.10.refs_5_.refs_9_.refs_11_), channel_id=1, source_target_pairs={{0,12},{1,13},{2,14},{3,15},{4,0},{5,1},{6,2},{7,3},{8,4},{9,5},{1... | collective-permute-start | bytes 1179656 | tf_op jit(solution)/shard_map/ppermute | solution.py:491
  118.6 12.0 %collective-permute-start.14 = (bf16[768,256]{1,0:T(8,128)(2,1)S(1)}, bf16[768,256]{1,0:T(8,128)(2,1)S(1)}, u32[]{:S(2)}, u32[]{:S(2)}) collective-permute-start(bf16[768,256]{1,0:T(8,128)(2,1)S(1)} %collective-permute-done.13.refs_11_), channel_id=1, source_target_pairs={{0,1},{1,2},{2,3},{3,0},{4,5},{5,6},{6,7},{7,4},{8,9},{9,10},{10,1... | collective-permute-start | bytes 1179656 | tf_op jit(solution)/shard_map/ppermute | solution.py:491
  120.2 10.3 %copy-start.8 = (bf16[784,384]{1,0:T(8,128)(2,1)S(1)}, bf16[784,384]{1,0:T(8,128)(2,1)}, u32[]{:S(2)}) copy-start(bf16[784,384]{1,0:T(8,128)(2,1)} %copy-done.7) | copy-start | bytes 1806340
  120.3 10.3 %copy-start.12 = (bf16[784,384]{1,0:T(8,128)(2,1)S(1)}, bf16[784,384]{1,0:T(8,128)(2,1)}, u32[]{:S(2)}) copy-start(bf16[784,384]{1,0:T(8,128)(2,1)} %copy-done.11) | copy-start | bytes 1806340
  140.2 6.6 %collective-permute-start.16 = (f32[8,768]{1,0:T(8,128)S(1)}, f32[8,768]{1,0:T(8,128)S(1)}, u32[]{:S(2)}, u32[]{:S(2)}) collective-permute-start(f32[8,768]{1,0:T(8,128)S(1)} %get-tuple-element.79), channel_id=1, source_target_pairs={{0,8},{1,9},{2,10},{3,11},{4,12},{5,13},{6,14},{7,15},{8,0},{9,1},... | collective-permute-start | bytes 73736 | tf_op jit(solution)/shard_map/ppermute | solution.py:491
  141.5 5.3 %collective-permute-start.18 = (f32[8,768]{1,0:T(8,128)S(1)}, f32[8,768]{1,0:T(8,128)S(1)}, u32[]{:S(2)}, u32[]{:S(2)}) collective-permute-start(f32[8,768]{1,0:T(8,128)S(1)} %get-tuple-element.81), channel_id=1, source_target_pairs={{0,3},{1,0},{2,1},{3,2},{4,7},{5,4},{6,5},{7,6},{8,11},{9,8},{10,9... | collective-permute-start | bytes 73736 | tf_op jit(solution)/shard_map/ppermute | solution.py:491
  142.7 4.1 %collective-permute-start.15 = (f32[8,768]{1,0:T(8,128)S(1)}, f32[8,768]{1,0:T(8,128)S(1)}, u32[]{:S(2)}, u32[]{:S(2)}) collective-permute-start(f32[8,768]{1,0:T(8,128)S(1)} %get-tuple-element.76), channel_id=1, source_target_pairs={{0,4},{1,5},{2,6},{3,7},{4,8},{5,9},{6,10},{7,11},{8,12},{9,13},{1... | collective-permute-start | bytes 73736 | tf_op jit(solution)/shard_map/ppermute | solution.py:491
  145.3 5.0 %collective-permute-start.17 = (f32[8,768]{1,0:T(8,128)S(1)}, f32[8,768]{1,0:T(8,128)S(1)}, u32[]{:S(2)}, u32[]{:S(2)}) collective-permute-start(f32[8,768]{1,0:T(8,128)S(1)} %get-tuple-element.80), channel_id=1, source_target_pairs={{0,1},{1,2},{2,3},{3,0},{4,5},{5,6},{6,7},{7,4},{8,9},{9,10},{10,1... | collective-permute-start | bytes 73736 | tf_op jit(solution)/shard_map/ppermute | solution.py:491
  146.2 5.3 %collective-permute-start.19 = (f32[8,768]{1,0:T(8,128)S(1)}, f32[8,768]{1,0:T(8,128)S(1)}, u32[]{:S(2)}, u32[]{:S(2)}) collective-permute-start(f32[8,768]{1,0:T(8,128)S(1)} %get-tuple-element.82), channel_id=1, source_target_pairs={{0,2},{1,3},{2,0},{3,1},{4,6},{5,7},{6,4},{7,5},{8,10},{9,11},{10,... | collective-permute-start | bytes 73736 | tf_op jit(solution)/shard_map/ppermute | solution.py:491

commit v6 on v5

--- a/solution.py
+++ b/solution.py
@@ -12,7 +12,7 @@
 SIDE = 4
 ROWS = 768
 WIDTH = 1024
-PIECES = (384, 384, 256)
+PIECES = (512, 512)
 PIECE = PIECES[0]
 CAP = 288
 TAIL = 16
@@ -30,6 +30,7 @@
 HALF = 384
 STRIP = 32
 VMEM = 24 * 1024 * 1024
+PACK_VMEM = 56 * 1024 * 1024
 BF = jnp.bfloat16
 F32 = jnp.float32
 
@@ -46,8 +47,8 @@
     return lax.dot_general(a, b, (((1,), (1,)), ((), ())), preferred_element_type=F32)
 
 
-def params(**more):
-    return pltpu.CompilerParams(vmem_limit_bytes=VMEM, **more)
+def params(limit=VMEM):
+    return pltpu.CompilerParams(vmem_limit_bytes=limit)
 
 
 def whole(shape):
@@ -92,7 +93,8 @@
     chosen = pick(lab_ref, rank_ref, g, LANES)
     out_ref[0] = dot(chosen[:PAIR], unit[...]).astype(BF)
     marks = jnp.broadcast_to(lab.astype(F32) + 1.0, (TAIL, ROWS)).astype(BF)
-    out_ref[0, CAP:] = (dot_nt(marks, chosen) - 1.0).astype(BF)
+    out_ref[0, CAP:, :LANES] = (dot_nt(marks, chosen) - 1.0).astype(BF)
+    out_ref[0, CAP:, LANES:] = jnp.zeros((TAIL, PIECE - LANES), BF)
 
 
 def pack_first(embeddings, labels):
@@ -111,7 +113,7 @@
         ]
         + [jax.ShapeDtypeStruct((ROWS, w), BF) for w in PIECES[1:]],
         scratch_shapes=[pltpu.VMEM((ROWS, PIECE), BF)],
-        compiler_params=params(),
+        compiler_params=params(PACK_VMEM),
         name="pack_first",
     )(embeddings, labels)
 
@@ -129,7 +131,7 @@
         in_specs=[whole((ROWS, width)), whole((ROWS,)), whole((1, ROWS))],
         out_specs=pl.BlockSpec((1, CAP, width), lambda g: (g, 0, 0)),
         out_shape=jax.ShapeDtypeStruct((TILE_ROWS, CAP, width), BF),
-        compiler_params=params(),
+        compiler_params=params(PACK_VMEM),
         cost_estimate=pl.CostEstimate(
             flops=2 * TILE_ROWS * CAP * ROWS * width,
             bytes_accessed=2 * TILE_ROWS * CAP * width,
@@ -170,7 +172,7 @@
         offset = offset + count
     close_gaps(got_ref, rows, offsets, counts)
     out_ref[:ROWS] = rows[:ROWS]
-    out_ref[ROWS:] = jnp.concatenate([names[:, :PIECE], names[:, PIECE:ROWS]], axis=0).astype(BF)
+    out_ref[ROWS:] = jnp.concatenate([names[:, :PIECE], names[:, PIECE : 2 * PIECE]], axis=0).astype(BF)
 
 
 def compact_first(got):
@@ -230,7 +232,7 @@
 
 def spread_names(block):
     tail = block[ROWS:].astype(F32)
-    names = jnp.concatenate([tail[:1], tail[8:9]], axis=1)
+    names = jnp.concatenate([tail[:1], tail[8:9, : ROWS - PIECE]], axis=1)
     return names, jnp.transpose(jnp.broadcast_to(names, (128, ROWS)))
 
 
@@ -530,7 +532,7 @@
             d, stats["O"] = tie((d, stats["O"]))
         e = shift(d, 0, 1)
         if k < last:
-            got, a, b, c, d, e = tie((later, a, b, c, d, e))
+            got, e, d, c, b, a = tie((later, e, d, c, b, a))
         for q, piece in zip("OABCDE", (mine, a, b, c, d, e)):
             blocks[q].append(piece)
     near = {q: blocks[q] for q in "OACD"}

time: 164 us -> 159 us (0.970)
  waiting for transfers between devices: 52.2 us -> 70.8 us
  starting transfers between devices: 45.5 us -> 30.3 us
  local copies, waits for them, and re-layouts: 8.67 us -> 2.73 us
  Pallas kernels: 46.4 us -> 42.7 us
    ppermute x20 -> x15, waiting for transfers between devices: 30.4 us -> 45.4 us  [shift(): return lax.ppermute(array, ('tr', 'tc'), moves)]
    ppermute x20 -> x15, starting transfers between devices: 31.3 us -> 20.6 us  [shift(): return lax.ppermute(array, ('tr', 'tc'), moves)]
    unnamed x34 -> x16, local copies, waits for them, and re-layouts: 8.67 us -> 2.73 us
    all_to_all x3 -> x2, starting transfers between devices: 14.2 us -> 9.68 us  [exchange(): return lax.all_to_all(packed, 'tr', split_axis=0, concat_axis=0, tiled=True)]
    pallas_call x3, Pallas kernels: 23.8 us -> 20.1 us  [pairs(): pl.pallas_call(functools.partial(pair_kernel, plan, names, list(old)), ou...]
    all_to_all x3 -> x2, waiting for transfers between devices: 21.8 us -> 25.3 us  [exchange(): return lax.all_to_all(packed, 'tr', split_axis=0, concat_axis=0, tiled=True)]
    pallas_call x1, Pallas kernels: 4.74 us -> 7.57 us  [pack_first(): pl.pallas_call(pack_first_kernel, grid=(TILE_ROWS,), in_specs=[whole((ROW...]
    pallas_call x2 -> x1, Pallas kernels: 7.43 us -> 6.07 us  [pack_rest(): pl.pallas_call(pack_rest_kernel, grid=(TILE_ROWS,), in_specs=[whole((ROWS...]
  transfers between devices with their start and end apart: 23 -> 17, of which waited for: 8 -> 11; matrix products, arithmetic and copies ran while one was open for 0% -> 0% of each run, Pallas kernels for 16% -> 14%
where the time goes in v6:
time: 159 us; the launch traced here: 157 us
  waiting for transfers between devices  70.8 us (45%)
  Pallas kernels  42.7 us (27%)
  starting transfers between devices  30.3 us (19%)
  blocking collectives  9.9 us (6%)
  local copies, waits for them, and re-layouts  2.73 us (2%)
    ppermute x15, waiting for transfers between devices, shift(): return lax.ppermute(array, ('tr', 'tc'), moves)  45.4 us
    all_to_all x2, waiting for transfers between devices, exchange(): return lax.all_to_all(packed, 'tr', split_axis=0, concat_axis=0, tiled=True)  25.3 us
    ppermute x15, starting transfers between devices, shift(): return lax.ppermute(array, ('tr', 'tc'), moves)  20.6 us
    pallas_call x3, Pallas kernels, pairs(): pl.pallas_call(functools.partial(pair_kernel, plan, names, list(old)), ou...  20.1 us
    all_to_all x1, blocking collectives, exchange(): return lax.all_to_all(packed, 'tr', split_axis=0, concat_axis=0, tiled=True)  9.9 us
    all_to_all x2, starting transfers between devices, exchange(): return lax.all_to_all(packed, 'tr', split_axis=0, concat_axis=0, tiled=True)  9.68 us
    pallas_call x1, Pallas kernels, pack_first(): pl.pallas_call(pack_first_kernel, grid=(TILE_ROWS,), in_specs=[whole((ROW...  7.57 us
    pallas_call x1, Pallas kernels, pack_rest(): pl.pallas_call(pack_rest_kernel, grid=(TILE_ROWS,), in_specs=[whole((ROWS...  6.07 us
  transfers between devices with their start and end apart: 17, of which 11 were waited for; matrix products, arithmetic and copies ran while one was open for 0% of the time, Pallas kernels for 14%

profile of v6, /device:TPU:2, one launch (start us, length us, event | category | flops | bytes accessed | tf_op | source)
XLA Modules:
  0.0 157.2 jit_solution(6736212019530373829)
XLA Ops:
  0.6 7.6 %pack_first.1 = (bf16[8,304,512]{2,1,0:T(8,128)(2,1)}, s32[1,768]{1,0:T(1,128)}, bf16[768,512]{1,0:T(8,128)(2,1)}) custom-call(bf16[768,1024]{1,0:T(8,128)(2,1)} %emb_ref.1, s32[768]{0:T(1024)} %lab_ref.5), custom_call_target="tpu_custom_call" | custom-call | tf_op jit(solution)/shard_map/pack_first/pallas_call | solution.py:101
  8.2 5.3 %all-to-all-start = ((bf16[8,304,512]{2,1,0:T(8,128)(2,1)}), bf16[8,304,512]{2,1,0:T(8,128)(2,1)S(1)}, u32[]{:S(2)}, u32[]{:S(2)}) async-start(bf16[8,304,512]{2,1,0:T(8,128)(2,1)} %get-tuple-element.36), calls=%async_computation | async-start | bytes 4980736 | tf_op jit(solution)/shard_map/all_to_all | solution.py:508
  13.5 6.1 %pack_rest.1 = bf16[8,288,512]{2,1,0:T(8,128)(2,1)} custom-call(bf16[768,512]{1,0:T(8,128)(2,1)} %get-tuple-element.34.unit_ref, s32[768]{0:T(1024)} %lab_ref.5, s32[1,768]{1,0:T(1,128)} %get-tuple-element.35.rank_ref), custom_call_target="tpu_custom_call" | custom-call | flops 1811939328 | bytes 2359296 | tf_op jit(solution)/shard_map/pack_rest/pallas_call | solution.py:128
  19.6 25.3 %all-to-all-done.got_ref = bf16[8,304,512]{2,1,0:T(8,128)(2,1)S(1)} async-done(((bf16[8,304,512]{2,1,0:T(8,128)(2,1)}), bf16[8,304,512]{2,1,0:T(8,128)(2,1)S(1)}, u32[]{:S(2)}, u32[]{:S(2)}) %all-to-all-start) | async-done | bytes 2490400 | tf_op jit(solution)/shard_map/all_to_all | solution.py:508
  44.9 4.4 %all-to-all-start.1 = ((bf16[8,288,512]{2,1,0:T(8,128)(2,1)}), bf16[8,288,512]{2,1,0:T(8,128)(2,1)}, u32[]{:S(2)}, u32[]{:S(2)}) async-start(bf16[8,288,512]{2,1,0:T(8,128)(2,1)} %pack_rest.1), calls=%async_computation.1 | async-start | bytes 4718592 | tf_op jit(solution)/shard_map/all_to_all | solution.py:508
  49.3 1.6 %compact_first.1 = (bf16[784,512]{1,0:T(8,128)(2,1)S(1)}, s32[16]{0:T(128)S(1)}) custom-call(bf16[8,304,512]{2,1,0:T(8,128)(2,1)S(1)} %all-to-all-done.got_ref), custom_call_target="tpu_custom_call" | custom-call | tf_op jit(solution)/shard_map/compact_first/pallas_call | solution.py:179
  50.9 0.6 collective-permute-start.3
  51.5 1.6 %collective-permute-start = (bf16[784,512]{1,0:T(8,128)(2,1)S(1)}, bf16[784,512]{1,0:T(8,128)(2,1)S(1)}, u32[]{:S(2)}, u32[]{:S(2)}) collective-permute-start(bf16[784,512]{1,0:T(8,128)(2,1)S(1)} %get-tuple-element.40.block.refs_0_), channel_id=1, source_target_pairs={{0,1},{1,2},{2,3},{3,0},{4,5},{5,6},{6,7},{7,4},{8,9},{9,10},{10,1... | collective-permute-start | bytes 2408456 | tf_op jit(solution)/shard_map/ppermute | solution.py:493
  53.1 1.7 %collective-permute-start.2 = (bf16[784,512]{1,0:T(8,128)(2,1)S(1)}, bf16[784,512]{1,0:T(8,128)(2,1)S(1)}, u32[]{:S(2)}, u32[]{:S(2)}) collective-permute-start(bf16[784,512]{1,0:T(8,128)(2,1)S(1)} %get-tuple-element.40.block.refs_0_), channel_id=1, source_target_pairs={{0,3},{1,0},{2,1},{3,2},{4,7},{5,4},{6,5},{7,6},{8,11},{9,8},{10,9... | collective-permute-start | bytes 2408456 | tf_op jit(solution)/shard_map/ppermute | solution.py:493
  54.8 8.4 %collective-permute-done.3.refs_1_ = bf16[784,512]{1,0:T(8,128)(2,1)S(1)} collective-permute-done((bf16[784,512]{1,0:T(8,128)(2,1)S(1)}, bf16[784,512]{1,0:T(8,128)(2,1)S(1)}, u32[]{:S(2)}, u32[]{:S(2)}) %collective-permute-start.3) | collective-permute-done | bytes 802848 | tf_op jit(solution)/shard_map/ppermute | solution.py:493
  63.2 0.8 collective-permute-start.4
  64.0 6.6 %collective-permute-done.refs_3_ = bf16[784,512]{1,0:T(8,128)(2,1)S(1)} collective-permute-done((bf16[784,512]{1,0:T(8,128)(2,1)S(1)}, bf16[784,512]{1,0:T(8,128)(2,1)S(1)}, u32[]{:S(2)}, u32[]{:S(2)}) %collective-permute-start) | collective-permute-done | bytes 802848 | tf_op jit(solution)/shard_map/ppermute | solution.py:493
  70.6 2.1 %collective-permute-start.1 = (bf16[784,512]{1,0:T(8,128)(2,1)S(1)}, bf16[784,512]{1,0:T(8,128)(2,1)S(1)}, u32[]{:S(2)}, u32[]{:S(2)}) collective-permute-start(bf16[784,512]{1,0:T(8,128)(2,1)S(1)} %collective-permute-done.refs_3_), channel_id=1, source_target_pairs={{0,1},{1,2},{2,3},{3,0},{4,5},{5,6},{6,7},{7,4},{8,9},{9,10},{10,1... | collective-permute-start | bytes 2408456 | tf_op jit(solution)/shard_map/ppermute | solution.py:493
  72.7 0.0 copy-start.6
  72.7 0.9 copy-done.6
  73.6 0.0 collective-permute-done.2.refs_2_
  73.6 1.7 %collective-permute-done.4.refs_3_ = bf16[784,512]{1,0:T(8,128)(2,1)S(1)} collective-permute-done((bf16[784,512]{1,0:T(8,128)(2,1)S(1)}, bf16[784,512]{1,0:T(8,128)(2,1)S(1)}, u32[]{:S(2)}, u32[]{:S(2)}) %collective-permute-start.4) | collective-permute-done | bytes 802848 | tf_op jit(solution)/shard_map/ppermute | solution.py:493
  75.3 0.0 copy-start.2
  75.3 0.9 copy-done.2
  76.2 8.7 %collective-permute-done.1.refs_4_ = bf16[784,512]{1,0:T(8,128)(2,1)S(1)} collective-permute-done((bf16[784,512]{1,0:T(8,128)(2,1)S(1)}, bf16[784,512]{1,0:T(8,128)(2,1)S(1)}, u32[]{:S(2)}, u32[]{:S(2)}) %collective-permute-start.1) | collective-permute-done | bytes 802848 | tf_op jit(solution)/shard_map/ppermute | solution.py:493
  85.0 0.0 copy-start.4
  85.0 0.9 copy-done.4
  85.9 0.0 all-to-all-done.1.got_ref
  85.9 3.2 %compact_rest.1.refs_0_.refs_2_.refs_4_.refs_5_ = bf16[768,512]{1,0:T(8,128)(2,1)S(1)} custom-call(s32[16]{0:T(128)S(1)} %get-tuple-element.38.place_ref.offset_ref, bf16[8,288,512]{2,1,0:T(8,128)(2,1)} %all-to-all-done.1.got_ref), custom_call_target="tpu_custom_call" | custom-call | tf_op jit(solution)/shard_map/compact_rest/pallas_call | solution.py:201
  89.0 4.2 %collective-permute-start.5 = (bf16[768,512]{1,0:T(8,128)(2,1)S(1)}, bf16[768,512]{1,0:T(8,128)(2,1)}, u32[]{:S(2)}, u32[]{:S(2)}) collective-permute-start(bf16[768,512]{1,0:T(8,128)(2,1)S(1)} %compact_rest.1.refs_0_.refs_2_.refs_4_.refs_5_), channel_id=1, source_target_pairs={{0,12},{1,13},{2,14},{3,15},{4,0},{5,1},{6,2},{7,3},{8,4},{9,5},{1... | collective-permute-start | bytes 2359304 | tf_op jit(solution)/shard_map/ppermute | solution.py:493
  93.3 0.0 collective-permute-start.8
  93.3 3.2 %collective-permute-start.6 = (bf16[768,512]{1,0:T(8,128)(2,1)S(1)}, bf16[768,512]{1,0:T(8,128)(2,1)}, u32[]{:S(2)}, u32[]{:S(2)}) collective-permute-start(bf16[768,512]{1,0:T(8,128)(2,1)S(1)} %compact_rest.1.refs_0_.refs_2_.refs_4_.refs_5_), channel_id=1, source_target_pairs={{0,3},{1,0},{2,1},{3,2},{4,7},{5,4},{6,5},{7,6},{8,11},{9,8},{10,9... | collective-permute-start | bytes 2359304 | tf_op jit(solution)/shard_map/ppermute | solution.py:493
  96.5 0.1 pad_add_fusion.half_ref
  96.6 2.0 %own.1.refs_4_ = f32[8,768]{1,0:T(8,128)S(1)} custom-call(bf16[784,512]{1,0:T(8,128)(2,1)S(1)} %get-tuple-element.40.block.refs_0_, bf16[768,512]{1,0:T(8,128)(2,1)S(1)} %compact_rest.1.refs_0_.refs_2_.refs_4_.refs_5_), custom_call_target="tpu_custom_call" | custom-call | flops 1207959552 | bytes 1605632 | tf_op jit(solution)/shard_map/own/pallas_call | solution.py:279
  98.6 0.0 copy-start.7
  98.6 4.2 %collective-permute-done.5.refs_3_.refs_5_.refs_6_ = bf16[768,512]{1,0:T(8,128)(2,1)} collective-permute-done((bf16[768,512]{1,0:T(8,128)(2,1)S(1)}, bf16[768,512]{1,0:T(8,128)(2,1)}, u32[]{:S(2)}, u32[]{:S(2)}) %collective-permute-start.5) | collective-permute-done | bytes 786464 | tf_op jit(solution)/shard_map/ppermute | solution.py:493
  102.8 3.4 %pairs.3 = (f32[8,768]{1,0:T(8,128)S(1)}, f32[8,768]{1,0:T(8,128)S(1)}) custom-call(s32[2]{0:T(128)S(1)} %pad_add_fusion.half_ref, bf16[784,512]{1,0:T(8,128)(2,1)S(1)} %get-tuple-element.40.block.refs_0_, bf16[784,512]{1,0:T(8,128)(2,1)S(1)} %collective-permute-done.3.refs_1_, bf16[768,512]{1,0:T(8,128)(2,1)S(1)} %compact_rest.1.refs_0_.refs_2_.refs_4_.refs_5_, ...), custom_call_target="tpu_custom_call" | custom-call | flops 1207959552 | bytes 3211264 | tf_op jit(solution)/shard_map/pairs/pallas_call | solution.py:401
  106.2 8.0 %collective-permute-done.8.refs_7_ = bf16[768,512]{1,0:T(8,128)(2,1)} collective-permute-done((bf16[768,512]{1,0:T(8,128)(2,1)S(1)}, bf16[768,512]{1,0:T(8,128)(2,1)}, u32[]{:S(2)}, u32[]{:S(2)}) %collective-permute-start.8) | collective-permute-done | bytes 786464 | tf_op jit(solution)/shard_map/ppermute | solution.py:493
  114.2 0.0 collective-permute-start.9
  114.2 0.7 collective-permute-start.7
  114.9 0.0 collective-permute-done.6.refs_6_.refs_7_
  114.9 0.0 copy-done.7
  114.9 0.0 copy-start.3
  114.9 0.0 copy-start.5
  114.9 8.8 %pairs.4 = (f32[8,768]{1,0:T(8,128)S(1)}, f32[8,768]{1,0:T(8,128)S(1)}, f32[8,768]{1,0:T(8,128)S(1)}, f32[8,768]{1,0:T(8,128)S(1)}) custom-call(s32[2]{0:T(128)S(1)} %pad_add_fusion.half_ref, bf16[784,512]{1,0:T(8,128)(2,1)S(1)} %get-tuple-element.40.block.refs_0_, bf16[784,512]{1,0:T(8,128)(2,1)S(1)} %collective-permute-done.3.refs_1_, ...), custom_call_target="tpu_custom_call" | custom-call | flops 4227858432 | bytes 6422528 | tf_op jit(solution)/shard_map/pairs/pallas_call | solution.py:401
  123.7 3.9 %collective-permute-done.9.refs_9_ = bf16[768,512]{1,0:T(8,128)(2,1)S(1)} collective-permute-done((bf16[768,512]{1,0:T(8,128)(2,1)}, bf16[768,512]{1,0:T(8,128)(2,1)S(1)}, u32[]{:S(2)}, u32[]{:S(2)}) %collective-permute-start.9) | collective-permute-done | bytes 786464 | tf_op jit(solution)/shard_map/ppermute | solution.py:493
  127.6 0.0 collective-permute-done.7.refs_8_
  127.6 0.0 copy-done.3
  127.6 0.0 copy-done.5
  127.6 0.0 copy-start
  127.6 0.0 copy-start.1
  127.6 7.9 %pairs.5 = (f32[8,768]{1,0:T(8,128)S(1)}, f32[8,768]{1,0:T(8,128)S(1)}, f32[8,768]{1,0:T(8,128)S(1)}, f32[8,768]{1,0:T(8,128)S(1)}, f32[8,768]{1,0:T(8,128)S(1)}) custom-call(s32[2]{0:T(128)S(1)} %pad_add_fusion.half_ref, bf16[784,512]{1,0:T(8,128)(2,1)S(1)} %get-tuple-element.40.block.refs_0_, bf16[784,512]{1,0:T(8,128)(2,1)S(1)} %collective-permute-done.3.refs_1_, ...), custom_call_target="tpu_custom_call" | custom-call | flops 3623878656 | bytes 8028160 | tf_op jit(solution)/shard_map/pairs/pallas_call | solution.py:401
  135.5 0.1 collective-permute-start.11
  135.6 2.8 %collective-permute-start.13 = (f32[8,768]{1,0:T(8,128)S(1)}, f32[8,768]{1,0:T(8,128)S(1)}, u32[]{:S(2)}, u32[]{:S(2)}) collective-permute-start(f32[8,768]{1,0:T(8,128)S(1)} %get-tuple-element.63), channel_id=1, source_target_pairs={{0,3},{1,0},{2,1},{3,2},{4,7},{5,4},{6,5},{7,6},{8,11},{9,8},{10,9... | collective-permute-start | bytes 73736 | tf_op jit(solution)/shard_map/ppermute | solution.py:493
  138.4 1.4 collective-permute-start.10
  139.8 0.0 collective-permute-start.12
  139.8 1.5 collective-permute-start.14
  141.3 0.0 collective-permute-done.11.refs_2_
  141.3 0.0 collective-permute-done.13.refs_4_
  141.3 0.9 collective-permute-done.10.refs_1_
  142.2 2.6 %collective-permute-done.12.refs_3_ = f32[8,768]{1,0:T(8,128)S(1)} collective-permute-done((f32[8,768]{1,0:T(8,128)S(1)}, f32[8,768]{1,0:T(8,128)S(1)}, u32[]{:S(2)}, u32[]{:S(2)}) %collective-permute-start.12) | collective-permute-done | bytes 24608 | tf_op jit(solution)/shard_map/ppermute | solution.py:493
  144.8 0.3 collective-permute-done.14.refs_5_
  145.2 0.7 spread.1
  145.9 9.9 %all_to_all.15.back_ref = f32[8,8,128]{2,1,0:T(8,128)S(1)} all-to-all(f32[8,8,128]{2,1,0:T(8,128)S(1)} %spread.1), channel_id=1, replica_groups=mesh['tr'=8,'tc'=16] {'tr'}, dimensions={0} | all-to-all | bytes 65536 | tf_op jit(solution)/shard_map/all_to_all | solution.py:508
  155.8 0.0 copy-done
  155.8 0.0 copy-done.1
  155.8 1.5 unpack.1
Async XLA Ops:
  8.2 36.7 %all-to-all-start = ((bf16[8,304,512]{2,1,0:T(8,128)(2,1)}), bf16[8,304,512]{2,1,0:T(8,128)(2,1)S(1)}, u32[]{:S(2)}, u32[]{:S(2)}) async-start(bf16[8,304,512]{2,1,0:T(8,128)(2,1)} %get-tuple-element.36), calls=%async_computation | async-start | bytes 4980736 | tf_op jit(solution)/shard_map/all_to_all | solution.py:508
  44.9 40.9 %all-to-all-start.1 = ((bf16[8,288,512]{2,1,0:T(8,128)(2,1)}), bf16[8,288,512]{2,1,0:T(8,128)(2,1)}, u32[]{:S(2)}, u32[]{:S(2)}) async-start(bf16[8,288,512]{2,1,0:T(8,128)(2,1)} %pack_rest.1), calls=%async_computation.1 | async-start | bytes 4718592 | tf_op jit(solution)/shard_map/all_to_all | solution.py:508
  50.9 12.2 %collective-permute-start.3 = (bf16[784,512]{1,0:T(8,128)(2,1)S(1)}, bf16[784,512]{1,0:T(8,128)(2,1)S(1)}, u32[]{:S(2)}, u32[]{:S(2)}) collective-permute-start(bf16[784,512]{1,0:T(8,128)(2,1)S(1)} %get-tuple-element.40.block.refs_0_), channel_id=1, source_target_pairs={{0,12},{1,13},{2,14},{3,15},{4,0},{5,1},{6,2},{7,3},{8,4},{9,5},{1... | collective-permute-start | bytes 2408456 | tf_op jit(solution)/shard_map/ppermute | solution.py:493
  51.5 19.1 %collective-permute-start = (bf16[784,512]{1,0:T(8,128)(2,1)S(1)}, bf16[784,512]{1,0:T(8,128)(2,1)S(1)}, u32[]{:S(2)}, u32[]{:S(2)}) collective-permute-start(bf16[784,512]{1,0:T(8,128)(2,1)S(1)} %get-tuple-element.40.block.refs_0_), channel_id=1, source_target_pairs={{0,1},{1,2},{2,3},{3,0},{4,5},{5,6},{6,7},{7,4},{8,9},{9,10},{10,1... | collective-permute-start | bytes 2408456 | tf_op jit(solution)/shard_map/ppermute | solution.py:493
  53.1 20.5 %collective-permute-start.2 = (bf16[784,512]{1,0:T(8,128)(2,1)S(1)}, bf16[784,512]{1,0:T(8,128)(2,1)S(1)}, u32[]{:S(2)}, u32[]{:S(2)}) collective-permute-start(bf16[784,512]{1,0:T(8,128)(2,1)S(1)} %get-tuple-element.40.block.refs_0_), channel_id=1, source_target_pairs={{0,3},{1,0},{2,1},{3,2},{4,7},{5,4},{6,5},{7,6},{8,11},{9,8},{10,9... | collective-permute-start | bytes 2408456 | tf_op jit(solution)/shard_map/ppermute | solution.py:493
  63.2 12.2 %collective-permute-start.4 = (bf16[784,512]{1,0:T(8,128)(2,1)S(1)}, bf16[784,512]{1,0:T(8,128)(2,1)S(1)}, u32[]{:S(2)}, u32[]{:S(2)}) collective-permute-start(bf16[784,512]{1,0:T(8,128)(2,1)S(1)} %collective-permute-done.3.refs_1_), channel_id=1, source_target_pairs={{0,12},{1,13},{2,14},{3,15},{4,0},{5,1},{6,2},{7,3},{8,4},{9,5},{1... | collective-permute-start | bytes 2408456 | tf_op jit(solution)/shard_map/ppermute | solution.py:493
  70.6 14.3 %collective-permute-start.1 = (bf16[784,512]{1,0:T(8,128)(2,1)S(1)}, bf16[784,512]{1,0:T(8,128)(2,1)S(1)}, u32[]{:S(2)}, u32[]{:S(2)}) collective-permute-start(bf16[784,512]{1,0:T(8,128)(2,1)S(1)} %collective-permute-done.refs_3_), channel_id=1, source_target_pairs={{0,1},{1,2},{2,3},{3,0},{4,5},{5,6},{6,7},{7,4},{8,9},{9,10},{10,1... | collective-permute-start | bytes 2408456 | tf_op jit(solution)/shard_map/ppermute | solution.py:493
  72.7 0.9 copy-start.6
  75.3 0.9 copy-start.2
  85.0 0.9 copy-start.4
  89.0 13.7 %collective-permute-start.5 = (bf16[768,512]{1,0:T(8,128)(2,1)S(1)}, bf16[768,512]{1,0:T(8,128)(2,1)}, u32[]{:S(2)}, u32[]{:S(2)}) collective-permute-start(bf16[768,512]{1,0:T(8,128)(2,1)S(1)} %compact_rest.1.refs_0_.refs_2_.refs_4_.refs_5_), channel_id=1, source_target_pairs={{0,12},{1,13},{2,14},{3,15},{4,0},{5,1},{6,2},{7,3},{8,4},{9,5},{1... | collective-permute-start | bytes 2359304 | tf_op jit(solution)/shard_map/ppermute | solution.py:493
  93.3 20.9 %collective-permute-start.8 = (bf16[768,512]{1,0:T(8,128)(2,1)S(1)}, bf16[768,512]{1,0:T(8,128)(2,1)}, u32[]{:S(2)}, u32[]{:S(2)}) collective-permute-start(bf16[768,512]{1,0:T(8,128)(2,1)S(1)} %compact_rest.1.refs_0_.refs_2_.refs_4_.refs_5_), channel_id=1, source_target_pairs={{0,1},{1,2},{2,3},{3,0},{4,5},{5,6},{6,7},{7,4},{8,9},{9,10},{10,1... | collective-permute-start | bytes 2359304 | tf_op jit(solution)/shard_map/ppermute | solution.py:493
  93.3 21.6 %collective-permute-start.6 = (bf16[768,512]{1,0:T(8,128)(2,1)S(1)}, bf16[768,512]{1,0:T(8,128)(2,1)}, u32[]{:S(2)}, u32[]{:S(2)}) collective-permute-start(bf16[768,512]{1,0:T(8,128)(2,1)S(1)} %compact_rest.1.refs_0_.refs_2_.refs_4_.refs_5_), channel_id=1, source_target_pairs={{0,3},{1,0},{2,1},{3,2},{4,7},{5,4},{6,5},{7,6},{8,11},{9,8},{10,9... | collective-permute-start | bytes 2359304 | tf_op jit(solution)/shard_map/ppermute | solution.py:493
  98.6 16.3 %copy-start.7 = (bf16[784,512]{1,0:T(8,128)(2,1)S(1)}, bf16[784,512]{1,0:T(8,128)(2,1)}, u32[]{:S(2)}) copy-start(bf16[784,512]{1,0:T(8,128)(2,1)} %copy-done.6) | copy-start | bytes 2408452
  114.2 13.4 %collective-permute-start.9 = (bf16[768,512]{1,0:T(8,128)(2,1)}, bf16[768,512]{1,0:T(8,128)(2,1)S(1)}, u32[]{:S(2)}, u32[]{:S(2)}) collective-permute-start(bf16[768,512]{1,0:T(8,128)(2,1)} %collective-permute-done.8.refs_7_), channel_id=1, source_target_pairs={{0,1},{1,2},{2,3},{3,0},{4,5},{5,6},{6,7},{7,4},{8,9},{9,10},{10,1... | collective-permute-start | bytes 2359304 | tf_op jit(solution)/shard_map/ppermute | solution.py:493
  114.2 13.4 %collective-permute-start.7 = (bf16[768,512]{1,0:T(8,128)(2,1)}, bf16[768,512]{1,0:T(8,128)(2,1)S(1)}, u32[]{:S(2)}, u32[]{:S(2)}) collective-permute-start(bf16[768,512]{1,0:T(8,128)(2,1)} %collective-permute-done.5.refs_3_.refs_5_.refs_6_), channel_id=1, source_target_pairs={{0,12},{1,13},{2,14},{3,15},{4,0},{5,1},{6,2},{7,3},{8,4},{9,5},{1... | collective-permute-start | bytes 2359304 | tf_op jit(solution)/shard_map/ppermute | solution.py:493
  114.9 12.7 %copy-start.3 = (bf16[784,512]{1,0:T(8,128)(2,1)S(1)}, bf16[784,512]{1,0:T(8,128)(2,1)}, u32[]{:S(2)}) copy-start(bf16[784,512]{1,0:T(8,128)(2,1)} %copy-done.2) | copy-start | bytes 2408452
  114.9 12.7 %copy-start.5 = (bf16[784,512]{1,0:T(8,128)(2,1)S(1)}, bf16[784,512]{1,0:T(8,128)(2,1)}, u32[]{:S(2)}) copy-start(bf16[784,512]{1,0:T(8,128)(2,1)} %copy-done.4) | copy-start | bytes 2408452
  127.6 28.2 %copy-start = (s32[768]{0:T(1024)S(1)}, s32[768]{0:T(1024)}, u32[]{:S(2)}) copy-start(s32[768]{0:T(1024)} %lab_ref.5) | copy-start | bytes 9220
  127.6 28.2 %copy-start.1 = (s32[1,768]{1,0:T(1,128)S(1)}, s32[1,768]{1,0:T(1,128)}, u32[]{:S(2)}) copy-start(s32[1,768]{1,0:T(1,128)} %get-tuple-element.35.rank_ref) | copy-start | bytes 9220
  135.5 5.7 %collective-permute-start.11 = (f32[8,768]{1,0:T(8,128)S(1)}, f32[8,768]{1,0:T(8,128)S(1)}, u32[]{:S(2)}, u32[]{:S(2)}) collective-permute-start(f32[8,768]{1,0:T(8,128)S(1)} %get-tuple-element.61), channel_id=1, source_target_pairs={{0,8},{1,9},{2,10},{3,11},{4,12},{5,13},{6,14},{7,15},{8,0},{9,1},... | collective-permute-start | bytes 73736 | tf_op jit(solution)/shard_map/ppermute | solution.py:493
  135.6 5.7 %collective-permute-start.13 = (f32[8,768]{1,0:T(8,128)S(1)}, f32[8,768]{1,0:T(8,128)S(1)}, u32[]{:S(2)}, u32[]{:S(2)}) collective-permute-start(f32[8,768]{1,0:T(8,128)S(1)} %get-tuple-element.63), channel_id=1, source_target_pairs={{0,3},{1,0},{2,1},{3,2},{4,7},{5,4},{6,5},{7,6},{8,11},{9,8},{10,9... | collective-permute-start | bytes 73736 | tf_op jit(solution)/shard_map/ppermute | solution.py:493
  138.4 3.8 %collective-permute-start.10 = (f32[8,768]{1,0:T(8,128)S(1)}, f32[8,768]{1,0:T(8,128)S(1)}, u32[]{:S(2)}, u32[]{:S(2)}) collective-permute-start(f32[8,768]{1,0:T(8,128)S(1)} %get-tuple-element.58), channel_id=1, source_target_pairs={{0,4},{1,5},{2,6},{3,7},{4,8},{5,9},{6,10},{7,11},{8,12},{9,13},{1... | collective-permute-start | bytes 73736 | tf_op jit(solution)/shard_map/ppermute | solution.py:493
  139.8 5.0 %collective-permute-start.12 = (f32[8,768]{1,0:T(8,128)S(1)}, f32[8,768]{1,0:T(8,128)S(1)}, u32[]{:S(2)}, u32[]{:S(2)}) collective-permute-start(f32[8,768]{1,0:T(8,128)S(1)} %get-tuple-element.62), channel_id=1, source_target_pairs={{0,1},{1,2},{2,3},{3,0},{4,5},{5,6},{6,7},{7,4},{8,9},{9,10},{10,1... | collective-permute-start | bytes 73736 | tf_op jit(solution)/shard_map/ppermute | solution.py:493
  139.8 5.3 %collective-permute-start.14 = (f32[8,768]{1,0:T(8,128)S(1)}, f32[8,768]{1,0:T(8,128)S(1)}, u32[]{:S(2)}, u32[]{:S(2)}) collective-permute-start(f32[8,768]{1,0:T(8,128)S(1)} %get-tuple-element.64), channel_id=1, source_target_pairs={{0,2},{1,3},{2,0},{3,1},{4,6},{5,7},{6,4},{7,5},{8,10},{9,11},{10,... | collective-permute-start | bytes 73736 | tf_op jit(solution)/shard_map/ppermute | solution.py:493

commit v7 on v6

--- a/solution.py
+++ b/solution.py
@@ -496,7 +496,8 @@
 PLACES = {"O": (0, 0), "A": (1, 0), "B": (2, 0), "C": (0, 1), "D": (0, -1), "E": (0, 2)}
 FIRST = [("O", "A", None)]
 NEAR = [("O", "C", None), ("A", "C", None), ("D", "A", None), ("C", "D", 1)]
-FAR = [("B", "O", 0), ("B", "C", None), ("E", "A", None), ("E", "B", 0)]
+FAR_X = [("B", "O", 0), ("B", "C", None)]
+FAR_Y = [("E", "A", None), ("E", "B", 0)]
 
 
 def per_device(embeddings, labels):
@@ -537,9 +538,10 @@
             blocks[q].append(piece)
     near = {q: blocks[q] for q in "OACD"}
     stats.update(zip(near, pairs(NEAR, near, stats, halves)))
-    wide = {q: blocks[q] for q in "OACBE"}
-    far = pairs(FAR, wide, {q: stats[q] for q in "OAC"}, halves)
-    stats.update(zip(wide, far))
+    wide = {q: blocks[q] for q in "OCB"}
+    stats.update(zip(wide, pairs(FAR_X, wide, {q: stats[q] for q in "OC"}, halves)))
+    wide = {q: blocks[q] for q in "ABE"}
+    stats.update(zip(wide, pairs(FAR_Y, wide, {q: stats[q] for q in "AB"}, halves)))
     stats["D"], stats["B"] = tie((stats["D"], stats["B"]))
     parts = [stats["O"]] + [shift(stats[q], *PLACES[q]) for q in "ABCDE"]
     sent = spread(place, parts)

time: 159 us -> 156 us (0.981)
  waiting for transfers between devices: 70.8 us -> 64.9 us
  starting transfers between devices: 30.3 us -> 32.8 us
    ppermute x15, waiting for transfers between devices: 45.4 us -> 39.5 us  [shift(): return lax.ppermute(array, ('tr', 'tc'), moves)]
    ppermute x15, starting transfers between devices: 20.6 us -> 23.1 us  [shift(): return lax.ppermute(array, ('tr', 'tc'), moves)]
    pallas_call x3 -> x4, Pallas kernels: 20.1 us -> 21.7 us  [pairs(): pl.pallas_call(functools.partial(pair_kernel, plan, names, list(old)), ou...]
  transfers between devices with their start and end apart: 17 -> 17, of which waited for: 11 -> 9; matrix products, arithmetic and copies ran while one was open for 0% -> 0% of each run, Pallas kernels for 14% -> 17%
where the time goes in v7:
time: 156 us; the launch traced here: 155 us
  waiting for transfers between devices  64.9 us (42%)
  Pallas kernels  44.2 us (28%)
  starting transfers between devices  32.8 us (21%)
  blocking collectives  9.89 us (6%)
  local copies, waits for them, and re-layouts  2.77 us (2%)
    ppermute x15, waiting for transfers between devices, shift(): return lax.ppermute(array, ('tr', 'tc'), moves)  39.5 us
    all_to_all x2, waiting for transfers between devices, exchange(): return lax.all_to_all(packed, 'tr', split_axis=0, concat_axis=0, tiled=True)  25.4 us
    ppermute x15, starting transfers between devices, shift(): return lax.ppermute(array, ('tr', 'tc'), moves)  23.1 us
    pallas_call x4, Pallas kernels, pairs(): pl.pallas_call(functools.partial(pair_kernel, plan, names, list(old)), ou...  21.7 us
    all_to_all x1, blocking collectives, exchange(): return lax.all_to_all(packed, 'tr', split_axis=0, concat_axis=0, tiled=True)  9.89 us
    all_to_all x2, starting transfers between devices, exchange(): return lax.all_to_all(packed, 'tr', split_axis=0, concat_axis=0, tiled=True)  9.68 us
    pallas_call x1, Pallas kernels, pack_first(): pl.pallas_call(pack_first_kernel, grid=(TILE_ROWS,), in_specs=[whole((ROW...  7.55 us
    pallas_call x1, Pallas kernels, pack_rest(): pl.pallas_call(pack_rest_kernel, grid=(TILE_ROWS,), in_specs=[whole((ROWS...  6.05 us
  transfers between devices with their start and end apart: 17, of which 9 were waited for; matrix products, arithmetic and copies ran while one was open for 0% of the time, Pallas kernels for 17%

profile of v7, /device:TPU:2, one launch (start us, length us, event | category | flops | bytes accessed | tf_op | source)
XLA Modules:
  0.0 155.4 jit_solution(13540286834849768264)
XLA Ops:
  0.6 7.6 %pack_first.1 = (bf16[8,304,512]{2,1,0:T(8,128)(2,1)}, s32[1,768]{1,0:T(1,128)}, bf16[768,512]{1,0:T(8,128)(2,1)}) custom-call(bf16[768,1024]{1,0:T(8,128)(2,1)} %emb_ref.1, s32[768]{0:T(1024)} %lab_ref.5), custom_call_target="tpu_custom_call" | custom-call | tf_op jit(solution)/shard_map/pack_first/pallas_call | solution.py:101
  8.2 5.3 %all-to-all-start = ((bf16[8,304,512]{2,1,0:T(8,128)(2,1)}), bf16[8,304,512]{2,1,0:T(8,128)(2,1)S(1)}, u32[]{:S(2)}, u32[]{:S(2)}) async-start(bf16[8,304,512]{2,1,0:T(8,128)(2,1)} %get-tuple-element.37), calls=%async_computation | async-start | bytes 4980736 | tf_op jit(solution)/shard_map/all_to_all | solution.py:509
  13.5 6.1 %pack_rest.1 = bf16[8,288,512]{2,1,0:T(8,128)(2,1)} custom-call(bf16[768,512]{1,0:T(8,128)(2,1)} %get-tuple-element.35.unit_ref, s32[768]{0:T(1024)} %lab_ref.5, s32[1,768]{1,0:T(1,128)} %get-tuple-element.36.rank_ref), custom_call_target="tpu_custom_call" | custom-call | flops 1811939328 | bytes 2359296 | tf_op jit(solution)/shard_map/pack_rest/pallas_call | solution.py:128
  19.6 25.4 %all-to-all-done.got_ref = bf16[8,304,512]{2,1,0:T(8,128)(2,1)S(1)} async-done(((bf16[8,304,512]{2,1,0:T(8,128)(2,1)}), bf16[8,304,512]{2,1,0:T(8,128)(2,1)S(1)}, u32[]{:S(2)}, u32[]{:S(2)}) %all-to-all-start) | async-done | bytes 2490400 | tf_op jit(solution)/shard_map/all_to_all | solution.py:509
  44.9 4.4 %all-to-all-start.1 = ((bf16[8,288,512]{2,1,0:T(8,128)(2,1)}), bf16[8,288,512]{2,1,0:T(8,128)(2,1)}, u32[]{:S(2)}, u32[]{:S(2)}) async-start(bf16[8,288,512]{2,1,0:T(8,128)(2,1)} %pack_rest.1), calls=%async_computation.1 | async-start | bytes 4718592 | tf_op jit(solution)/shard_map/all_to_all | solution.py:509
  49.3 1.6 %compact_first.1 = (bf16[784,512]{1,0:T(8,128)(2,1)S(1)}, s32[16]{0:T(128)S(1)}) custom-call(bf16[8,304,512]{2,1,0:T(8,128)(2,1)S(1)} %all-to-all-done.got_ref), custom_call_target="tpu_custom_call" | custom-call | tf_op jit(solution)/shard_map/compact_first/pallas_call | solution.py:179
  50.9 0.6 collective-permute-start.3
  51.5 1.6 %collective-permute-start = (bf16[784,512]{1,0:T(8,128)(2,1)S(1)}, bf16[784,512]{1,0:T(8,128)(2,1)S(1)}, u32[]{:S(2)}, u32[]{:S(2)}) collective-permute-start(bf16[784,512]{1,0:T(8,128)(2,1)S(1)} %get-tuple-element.41.block.refs_0_), channel_id=1, source_target_pairs={{0,1},{1,2},{2,3},{3,0},{4,5},{5,6},{6,7},{7,4},{8,9},{9,10},{10,1... | collective-permute-start | bytes 2408456 | tf_op jit(solution)/shard_map/ppermute | solution.py:493
  53.1 1.7 %collective-permute-start.2 = (bf16[784,512]{1,0:T(8,128)(2,1)S(1)}, bf16[784,512]{1,0:T(8,128)(2,1)S(1)}, u32[]{:S(2)}, u32[]{:S(2)}) collective-permute-start(bf16[784,512]{1,0:T(8,128)(2,1)S(1)} %get-tuple-element.41.block.refs_0_), channel_id=1, source_target_pairs={{0,3},{1,0},{2,1},{3,2},{4,7},{5,4},{6,5},{7,6},{8,11},{9,8},{10,9... | collective-permute-start | bytes 2408456 | tf_op jit(solution)/shard_map/ppermute | solution.py:493
  54.8 8.4 %collective-permute-done.3.refs_1_.refs_0_ = bf16[784,512]{1,0:T(8,128)(2,1)S(1)} collective-permute-done((bf16[784,512]{1,0:T(8,128)(2,1)S(1)}, bf16[784,512]{1,0:T(8,128)(2,1)S(1)}, u32[]{:S(2)}, u32[]{:S(2)}) %collective-permute-start.3) | collective-permute-done | bytes 802848 | tf_op jit(solution)/shard_map/ppermute | solution.py:493
  63.1 0.8 collective-permute-start.4
  64.0 6.7 %collective-permute-done.refs_3_ = bf16[784,512]{1,0:T(8,128)(2,1)S(1)} collective-permute-done((bf16[784,512]{1,0:T(8,128)(2,1)S(1)}, bf16[784,512]{1,0:T(8,128)(2,1)S(1)}, u32[]{:S(2)}, u32[]{:S(2)}) %collective-permute-start) | collective-permute-done | bytes 802848 | tf_op jit(solution)/shard_map/ppermute | solution.py:493
  70.6 2.1 %collective-permute-start.1 = (bf16[784,512]{1,0:T(8,128)(2,1)S(1)}, bf16[784,512]{1,0:T(8,128)(2,1)S(1)}, u32[]{:S(2)}, u32[]{:S(2)}) collective-permute-start(bf16[784,512]{1,0:T(8,128)(2,1)S(1)} %collective-permute-done.refs_3_), channel_id=1, source_target_pairs={{0,1},{1,2},{2,3},{3,0},{4,5},{5,6},{6,7},{7,4},{8,9},{9,10},{10,1... | collective-permute-start | bytes 2408456 | tf_op jit(solution)/shard_map/ppermute | solution.py:493
  72.7 0.0 copy-start.6
  72.7 0.9 copy-done.6
  73.6 0.0 collective-permute-done.2.refs_2_.refs_1_
  73.6 0.0 copy-start.4
  73.6 0.9 copy-done.4
  74.5 0.8 collective-permute-done.4.refs_2_.refs_1_
  75.3 9.6 %collective-permute-done.1.refs_2_ = bf16[784,512]{1,0:T(8,128)(2,1)S(1)} collective-permute-done((bf16[784,512]{1,0:T(8,128)(2,1)S(1)}, bf16[784,512]{1,0:T(8,128)(2,1)S(1)}, u32[]{:S(2)}, u32[]{:S(2)}) %collective-permute-start.1) | collective-permute-done | bytes 802848 | tf_op jit(solution)/shard_map/ppermute | solution.py:493
  84.9 0.0 copy-start.2
  84.9 0.9 copy-done.2
  85.9 0.0 all-to-all-done.1.got_ref
  85.9 3.2 %compact_rest.1.refs_0_.refs_2_.refs_4_.refs_3_ = bf16[768,512]{1,0:T(8,128)(2,1)S(1)} custom-call(s32[16]{0:T(128)S(1)} %get-tuple-element.39.place_ref.offset_ref, bf16[8,288,512]{2,1,0:T(8,128)(2,1)} %all-to-all-done.1.got_ref), custom_call_target="tpu_custom_call" | custom-call | tf_op jit(solution)/shard_map/compact_rest/pallas_call | solution.py:201
  89.0 4.2 %collective-permute-start.5 = (bf16[768,512]{1,0:T(8,128)(2,1)S(1)}, bf16[768,512]{1,0:T(8,128)(2,1)}, u32[]{:S(2)}, u32[]{:S(2)}) collective-permute-start(bf16[768,512]{1,0:T(8,128)(2,1)S(1)} %compact_rest.1.refs_0_.refs_2_.refs_4_.refs_3_), channel_id=1, source_target_pairs={{0,12},{1,13},{2,14},{3,15},{4,0},{5,1},{6,2},{7,3},{8,4},{9,5},{1... | collective-permute-start | bytes 2359304 | tf_op jit(solution)/shard_map/ppermute | solution.py:493
  93.3 0.0 collective-permute-start.8
  93.3 3.2 %collective-permute-start.6 = (bf16[768,512]{1,0:T(8,128)(2,1)S(1)}, bf16[768,512]{1,0:T(8,128)(2,1)}, u32[]{:S(2)}, u32[]{:S(2)}) collective-permute-start(bf16[768,512]{1,0:T(8,128)(2,1)S(1)} %compact_rest.1.refs_0_.refs_2_.refs_4_.refs_3_), channel_id=1, source_target_pairs={{0,3},{1,0},{2,1},{3,2},{4,7},{5,4},{6,5},{7,6},{8,11},{9,8},{10,9... | collective-permute-start | bytes 2359304 | tf_op jit(solution)/shard_map/ppermute | solution.py:493
  96.5 0.1 pad_add_fusion.half_ref
  96.6 2.0 %own.1.refs_4_ = f32[8,768]{1,0:T(8,128)S(1)} custom-call(bf16[784,512]{1,0:T(8,128)(2,1)S(1)} %get-tuple-element.41.block.refs_0_, bf16[768,512]{1,0:T(8,128)(2,1)S(1)} %compact_rest.1.refs_0_.refs_2_.refs_4_.refs_3_), custom_call_target="tpu_custom_call" | custom-call | flops 1207959552 | bytes 1605632 | tf_op jit(solution)/shard_map/own/pallas_call | solution.py:279
  98.6 0.0 copy-start.5
  98.6 0.0 copy-start.7
  98.6 4.2 %collective-permute-done.5.refs_3_.refs_5_ = bf16[768,512]{1,0:T(8,128)(2,1)} collective-permute-done((bf16[768,512]{1,0:T(8,128)(2,1)S(1)}, bf16[768,512]{1,0:T(8,128)(2,1)}, u32[]{:S(2)}, u32[]{:S(2)}) %collective-permute-start.5) | collective-permute-done | bytes 786464 | tf_op jit(solution)/shard_map/ppermute | solution.py:493
  102.8 2.6 %collective-permute-start.7 = (bf16[768,512]{1,0:T(8,128)(2,1)}, bf16[768,512]{1,0:T(8,128)(2,1)S(1)}, u32[]{:S(2)}, u32[]{:S(2)}) collective-permute-start(bf16[768,512]{1,0:T(8,128)(2,1)} %collective-permute-done.5.refs_3_.refs_5_), channel_id=1, source_target_pairs={{0,12},{1,13},{2,14},{3,15},{4,0},{5,1},{6,2},{7,3},{8,4},{9,5},{1... | collective-permute-start | bytes 2359304 | tf_op jit(solution)/shard_map/ppermute | solution.py:493
  105.4 3.4 %pairs.4 = (f32[8,768]{1,0:T(8,128)S(1)}, f32[8,768]{1,0:T(8,128)S(1)}) custom-call(s32[2]{0:T(128)S(1)} %pad_add_fusion.half_ref, bf16[784,512]{1,0:T(8,128)(2,1)S(1)} %get-tuple-element.41.block.refs_0_, bf16[784,512]{1,0:T(8,128)(2,1)S(1)} %collective-permute-done.3.refs_1_.refs_0_, bf16[768,512]{1,0:T(8,128)(2,1)S(1)} %compact_rest.1.refs_0_.refs_2_.refs_4_.refs_3_, ...), custom_call_target="tpu_custom_call" | custom-call | flops 1207959552 | bytes 3211264 | tf_op jit(solution)/shard_map/pairs/pallas_call | solution.py:401
  108.8 5.3 %collective-permute-done.8.refs_7_ = bf16[768,512]{1,0:T(8,128)(2,1)} collective-permute-done((bf16[768,512]{1,0:T(8,128)(2,1)S(1)}, bf16[768,512]{1,0:T(8,128)(2,1)}, u32[]{:S(2)}, u32[]{:S(2)}) %collective-permute-start.8) | collective-permute-done | bytes 786464 | tf_op jit(solution)/shard_map/ppermute | solution.py:493
  114.1 0.0 collective-permute-start.9
  114.1 0.0 collective-permute-done.6.refs_6_.refs_4_
  114.1 0.0 copy-done.5
  114.2 0.0 copy-done.7
  114.2 8.8 %pairs.5 = (f32[8,768]{1,0:T(8,128)S(1)}, f32[8,768]{1,0:T(8,128)S(1)}, f32[8,768]{1,0:T(8,128)S(1)}, f32[8,768]{1,0:T(8,128)S(1)}) custom-call(s32[2]{0:T(128)S(1)} %pad_add_fusion.half_ref, bf16[784,512]{1,0:T(8,128)(2,1)S(1)} %get-tuple-element.41.block.refs_0_, bf16[784,512]{1,0:T(8,128)(2,1)S(1)} %collective-permute-done.3.refs_1_.refs_0_, ...), custom_call_target="tpu_custom_call" | custom-call | flops 4227858432 | bytes 6422528 | tf_op jit(solution)/shard_map/pairs/pallas_call | solution.py:401
  123.0 0.0 collective-permute-done.7.refs_5_.refs_4_
  123.0 0.0 copy-start.3
  123.0 4.6 %pairs.6 = (f32[8,768]{1,0:T(8,128)S(1)}, f32[8,768]{1,0:T(8,128)S(1)}, f32[8,768]{1,0:T(8,128)S(1)}) custom-call(s32[2]{0:T(128)S(1)} %pad_add_fusion.half_ref, bf16[784,512]{1,0:T(8,128)(2,1)S(1)} %get-tuple-element.41.block.refs_0_, bf16[784,512]{1,0:T(8,128)(2,1)S(1)} %copy-done.5, bf16[784,512]{1,0:T(8,128)(2,1)S(1)} %collective-permute-done.4.refs_2_.refs_1_, ...), custom_call_target="tpu_custom_call" | custom-call | flops 1811939328 | bytes 4816896 | tf_op jit(solution)/shard_map/pairs/pallas_call | solution.py:401
  127.6 0.0 collective-permute-done.9.refs_5_
  127.6 0.0 copy-done.3
  127.6 0.0 copy-start
  127.6 0.0 copy-start.1
  127.6 4.8 %pairs.7 = (f32[8,768]{1,0:T(8,128)S(1)}, f32[8,768]{1,0:T(8,128)S(1)}, f32[8,768]{1,0:T(8,128)S(1)}) custom-call(s32[2]{0:T(128)S(1)} %pad_add_fusion.half_ref, bf16[784,512]{1,0:T(8,128)(2,1)S(1)} %collective-permute-done.3.refs_1_.refs_0_, bf16[784,512]{1,0:T(8,128)(2,1)S(1)} %collective-permute-done.4.refs_2_.refs_1_, bf16[784,512]{1,0:T(8,128)(2,1)S(1)} %copy-done.3, ...), custom_call_target="tpu_custom_call" | custom-call | flops 1811939328 | bytes 4816896 | tf_op jit(solution)/shard_map/pairs/pallas_call | solution.py:401
  132.5 0.1 collective-permute-start.11
  132.6 3.3 %collective-permute-start.13 = (f32[8,768]{1,0:T(8,128)S(1)}, f32[8,768]{1,0:T(8,128)S(1)}, u32[]{:S(2)}, u32[]{:S(2)}) collective-permute-start(f32[8,768]{1,0:T(8,128)S(1)} %get-tuple-element.65), channel_id=1, source_target_pairs={{0,3},{1,0},{2,1},{3,2},{4,7},{5,4},{6,5},{7,6},{8,11},{9,8},{10,9... | collective-permute-start | bytes 73736 | tf_op jit(solution)/shard_map/ppermute | solution.py:493
  135.9 2.1 %collective-permute-start.10 = (f32[8,768]{1,0:T(8,128)S(1)}, f32[8,768]{1,0:T(8,128)S(1)}, u32[]{:S(2)}, u32[]{:S(2)}) collective-permute-start(f32[8,768]{1,0:T(8,128)S(1)} %get-tuple-element.60), channel_id=1, source_target_pairs={{0,4},{1,5},{2,6},{3,7},{4,8},{5,9},{6,10},{7,11},{8,12},{9,13},{1... | collective-permute-start | bytes 73736 | tf_op jit(solution)/shard_map/ppermute | solution.py:493
  138.0 0.0 collective-permute-start.14
  138.0 0.9 collective-permute-start.12
  138.9 0.0 collective-permute-done.11.refs_2_
  138.9 0.0 collective-permute-done.13.refs_4_
  138.9 0.8 collective-permute-done.10.refs_1_
  139.7 3.6 %collective-permute-done.14.refs_5_ = f32[8,768]{1,0:T(8,128)S(1)} collective-permute-done((f32[8,768]{1,0:T(8,128)S(1)}, f32[8,768]{1,0:T(8,128)S(1)}, u32[]{:S(2)}, u32[]{:S(2)}) %collective-permute-start.14) | collective-permute-done | bytes 24608 | tf_op jit(solution)/shard_map/ppermute | solution.py:493
  143.3 0.0 collective-permute-done.12.refs_3_
  143.3 0.7 spread.1
  144.0 9.9 %all_to_all.15.back_ref = f32[8,8,128]{2,1,0:T(8,128)S(1)} all-to-all(f32[8,8,128]{2,1,0:T(8,128)S(1)} %spread.1), channel_id=1, replica_groups=mesh['tr'=8,'tc'=16] {'tr'}, dimensions={0} | all-to-all | bytes 65536 | tf_op jit(solution)/shard_map/all_to_all | solution.py:509
  153.9 0.0 copy-done
  153.9 0.0 copy-done.1
  153.9 1.5 unpack.1
Async XLA Ops:
  8.2 36.7 %all-to-all-start = ((bf16[8,304,512]{2,1,0:T(8,128)(2,1)}), bf16[8,304,512]{2,1,0:T(8,128)(2,1)S(1)}, u32[]{:S(2)}, u32[]{:S(2)}) async-start(bf16[8,304,512]{2,1,0:T(8,128)(2,1)} %get-tuple-element.37), calls=%async_computation | async-start | bytes 4980736 | tf_op jit(solution)/shard_map/all_to_all | solution.py:509
  44.9 40.9 %all-to-all-start.1 = ((bf16[8,288,512]{2,1,0:T(8,128)(2,1)}), bf16[8,288,512]{2,1,0:T(8,128)(2,1)}, u32[]{:S(2)}, u32[]{:S(2)}) async-start(bf16[8,288,512]{2,1,0:T(8,128)(2,1)} %pack_rest.1), calls=%async_computation.1 | async-start | bytes 4718592 | tf_op jit(solution)/shard_map/all_to_all | solution.py:509
  50.9 12.2 %collective-permute-start.3 = (bf16[784,512]{1,0:T(8,128)(2,1)S(1)}, bf16[784,512]{1,0:T(8,128)(2,1)S(1)}, u32[]{:S(2)}, u32[]{:S(2)}) collective-permute-start(bf16[784,512]{1,0:T(8,128)(2,1)S(1)} %get-tuple-element.41.block.refs_0_), channel_id=1, source_target_pairs={{0,12},{1,13},{2,14},{3,15},{4,0},{5,1},{6,2},{7,3},{8,4},{9,5},{1... | collective-permute-start | bytes 2408456 | tf_op jit(solution)/shard_map/ppermute | solution.py:493
  51.5 19.1 %collective-permute-start = (bf16[784,512]{1,0:T(8,128)(2,1)S(1)}, bf16[784,512]{1,0:T(8,128)(2,1)S(1)}, u32[]{:S(2)}, u32[]{:S(2)}) collective-permute-start(bf16[784,512]{1,0:T(8,128)(2,1)S(1)} %get-tuple-element.41.block.refs_0_), channel_id=1, source_target_pairs={{0,1},{1,2},{2,3},{3,0},{4,5},{5,6},{6,7},{7,4},{8,9},{9,10},{10,1... | collective-permute-start | bytes 2408456 | tf_op jit(solution)/shard_map/ppermute | solution.py:493
  53.1 20.5 %collective-permute-start.2 = (bf16[784,512]{1,0:T(8,128)(2,1)S(1)}, bf16[784,512]{1,0:T(8,128)(2,1)S(1)}, u32[]{:S(2)}, u32[]{:S(2)}) collective-permute-start(bf16[784,512]{1,0:T(8,128)(2,1)S(1)} %get-tuple-element.41.block.refs_0_), channel_id=1, source_target_pairs={{0,3},{1,0},{2,1},{3,2},{4,7},{5,4},{6,5},{7,6},{8,11},{9,8},{10,9... | collective-permute-start | bytes 2408456 | tf_op jit(solution)/shard_map/ppermute | solution.py:493
  63.1 12.2 %collective-permute-start.4 = (bf16[784,512]{1,0:T(8,128)(2,1)S(1)}, bf16[784,512]{1,0:T(8,128)(2,1)S(1)}, u32[]{:S(2)}, u32[]{:S(2)}) collective-permute-start(bf16[784,512]{1,0:T(8,128)(2,1)S(1)} %collective-permute-done.3.refs_1_.refs_0_), channel_id=1, source_target_pairs={{0,12},{1,13},{2,14},{3,15},{4,0},{5,1},{6,2},{7,3},{8,4},{9,5},{1... | collective-permute-start | bytes 2408456 | tf_op jit(solution)/shard_map/ppermute | solution.py:493
  70.6 14.3 %collective-permute-start.1 = (bf16[784,512]{1,0:T(8,128)(2,1)S(1)}, bf16[784,512]{1,0:T(8,128)(2,1)S(1)}, u32[]{:S(2)}, u32[]{:S(2)}) collective-permute-start(bf16[784,512]{1,0:T(8,128)(2,1)S(1)} %collective-permute-done.refs_3_), channel_id=1, source_target_pairs={{0,1},{1,2},{2,3},{3,0},{4,5},{5,6},{6,7},{7,4},{8,9},{9,10},{10,1... | collective-permute-start | bytes 2408456 | tf_op jit(solution)/shard_map/ppermute | solution.py:493
  72.7 0.9 copy-start.6
  73.6 0.9 copy-start.4
  84.9 0.9 copy-start.2
  89.0 13.7 %collective-permute-start.5 = (bf16[768,512]{1,0:T(8,128)(2,1)S(1)}, bf16[768,512]{1,0:T(8,128)(2,1)}, u32[]{:S(2)}, u32[]{:S(2)}) collective-permute-start(bf16[768,512]{1,0:T(8,128)(2,1)S(1)} %compact_rest.1.refs_0_.refs_2_.refs_4_.refs_3_), channel_id=1, source_target_pairs={{0,12},{1,13},{2,14},{3,15},{4,0},{5,1},{6,2},{7,3},{8,4},{9,5},{1... | collective-permute-start | bytes 2359304 | tf_op jit(solution)/shard_map/ppermute | solution.py:493
  93.3 20.9 %collective-permute-start.8 = (bf16[768,512]{1,0:T(8,128)(2,1)S(1)}, bf16[768,512]{1,0:T(8,128)(2,1)}, u32[]{:S(2)}, u32[]{:S(2)}) collective-permute-start(bf16[768,512]{1,0:T(8,128)(2,1)S(1)} %compact_rest.1.refs_0_.refs_2_.refs_4_.refs_3_), channel_id=1, source_target_pairs={{0,1},{1,2},{2,3},{3,0},{4,5},{5,6},{6,7},{7,4},{8,9},{9,10},{10,1... | collective-permute-start | bytes 2359304 | tf_op jit(solution)/shard_map/ppermute | solution.py:493
  93.3 20.9 %collective-permute-start.6 = (bf16[768,512]{1,0:T(8,128)(2,1)S(1)}, bf16[768,512]{1,0:T(8,128)(2,1)}, u32[]{:S(2)}, u32[]{:S(2)}) collective-permute-start(bf16[768,512]{1,0:T(8,128)(2,1)S(1)} %compact_rest.1.refs_0_.refs_2_.refs_4_.refs_3_), channel_id=1, source_target_pairs={{0,3},{1,0},{2,1},{3,2},{4,7},{5,4},{6,5},{7,6},{8,11},{9,8},{10,9... | collective-permute-start | bytes 2359304 | tf_op jit(solution)/shard_map/ppermute | solution.py:493
  98.6 15.6 %copy-start.5 = (bf16[784,512]{1,0:T(8,128)(2,1)S(1)}, bf16[784,512]{1,0:T(8,128)(2,1)}, u32[]{:S(2)}) copy-start(bf16[784,512]{1,0:T(8,128)(2,1)} %copy-done.4) | copy-start | bytes 2408452
  98.6 15.6 %copy-start.7 = (bf16[784,512]{1,0:T(8,128)(2,1)S(1)}, bf16[784,512]{1,0:T(8,128)(2,1)}, u32[]{:S(2)}) copy-start(bf16[784,512]{1,0:T(8,128)(2,1)} %copy-done.6) | copy-start | bytes 2408452
  102.8 20.2 %collective-permute-start.7 = (bf16[768,512]{1,0:T(8,128)(2,1)}, bf16[768,512]{1,0:T(8,128)(2,1)S(1)}, u32[]{:S(2)}, u32[]{:S(2)}) collective-permute-start(bf16[768,512]{1,0:T(8,128)(2,1)} %collective-permute-done.5.refs_3_.refs_5_), channel_id=1, source_target_pairs={{0,12},{1,13},{2,14},{3,15},{4,0},{5,1},{6,2},{7,3},{8,4},{9,5},{1... | collective-permute-start | bytes 2359304 | tf_op jit(solution)/shard_map/ppermute | solution.py:493
  114.1 13.5 %collective-permute-start.9 = (bf16[768,512]{1,0:T(8,128)(2,1)}, bf16[768,512]{1,0:T(8,128)(2,1)S(1)}, u32[]{:S(2)}, u32[]{:S(2)}) collective-permute-start(bf16[768,512]{1,0:T(8,128)(2,1)} %collective-permute-done.8.refs_7_), channel_id=1, source_target_pairs={{0,1},{1,2},{2,3},{3,0},{4,5},{5,6},{6,7},{7,4},{8,9},{9,10},{10,1... | collective-permute-start | bytes 2359304 | tf_op jit(solution)/shard_map/ppermute | solution.py:493
  123.0 4.6 %copy-start.3 = (bf16[784,512]{1,0:T(8,128)(2,1)S(1)}, bf16[784,512]{1,0:T(8,128)(2,1)}, u32[]{:S(2)}) copy-start(bf16[784,512]{1,0:T(8,128)(2,1)} %copy-done.2) | copy-start | bytes 2408452
  127.6 26.3 %copy-start = (s32[768]{0:T(1024)S(1)}, s32[768]{0:T(1024)}, u32[]{:S(2)}) copy-start(s32[768]{0:T(1024)} %lab_ref.5) | copy-start | bytes 9220
  127.6 26.3 %copy-start.1 = (s32[1,768]{1,0:T(1,128)S(1)}, s32[1,768]{1,0:T(1,128)}, u32[]{:S(2)}) copy-start(s32[1,768]{1,0:T(1,128)} %get-tuple-element.36.rank_ref) | copy-start | bytes 9220
  132.5 6.4 %collective-permute-start.11 = (f32[8,768]{1,0:T(8,128)S(1)}, f32[8,768]{1,0:T(8,128)S(1)}, u32[]{:S(2)}, u32[]{:S(2)}) collective-permute-start(f32[8,768]{1,0:T(8,128)S(1)} %get-tuple-element.63), channel_id=1, source_target_pairs={{0,8},{1,9},{2,10},{3,11},{4,12},{5,13},{6,14},{7,15},{8,0},{9,1},... | collective-permute-start | bytes 73736 | tf_op jit(solution)/shard_map/ppermute | solution.py:493
  132.6 6.3 %collective-permute-start.13 = (f32[8,768]{1,0:T(8,128)S(1)}, f32[8,768]{1,0:T(8,128)S(1)}, u32[]{:S(2)}, u32[]{:S(2)}) collective-permute-start(f32[8,768]{1,0:T(8,128)S(1)} %get-tuple-element.65), channel_id=1, source_target_pairs={{0,3},{1,0},{2,1},{3,2},{4,7},{5,4},{6,5},{7,6},{8,11},{9,8},{10,9... | collective-permute-start | bytes 73736 | tf_op jit(solution)/shard_map/ppermute | solution.py:493
  135.9 3.8 %collective-permute-start.10 = (f32[8,768]{1,0:T(8,128)S(1)}, f32[8,768]{1,0:T(8,128)S(1)}, u32[]{:S(2)}, u32[]{:S(2)}) collective-permute-start(f32[8,768]{1,0:T(8,128)S(1)} %get-tuple-element.60), channel_id=1, source_target_pairs={{0,4},{1,5},{2,6},{3,7},{4,8},{5,9},{6,10},{7,11},{8,12},{9,13},{1... | collective-permute-start | bytes 73736 | tf_op jit(solution)/shard_map/ppermute | solution.py:493
  138.0 5.3 %collective-permute-start.14 = (f32[8,768]{1,0:T(8,128)S(1)}, f32[8,768]{1,0:T(8,128)S(1)}, u32[]{:S(2)}, u32[]{:S(2)}) collective-permute-start(f32[8,768]{1,0:T(8,128)S(1)} %get-tuple-element.66), channel_id=1, source_target_pairs={{0,2},{1,3},{2,0},{3,1},{4,6},{5,7},{6,4},{7,5},{8,10},{9,11},{10,... | collective-permute-start | bytes 73736 | tf_op jit(solution)/shard_map/ppermute | solution.py:493
  138.0 5.3 %collective-permute-start.12 = (f32[8,768]{1,0:T(8,128)S(1)}, f32[8,768]{1,0:T(8,128)S(1)}, u32[]{:S(2)}, u32[]{:S(2)}) collective-permute-start(f32[8,768]{1,0:T(8,128)S(1)} %get-tuple-element.64), channel_id=1, source_target_pairs={{0,1},{1,2},{2,3},{3,0},{4,5},{5,6},{6,7},{7,4},{8,9},{9,10},{10,1... | collective-permute-start | bytes 73736 | tf_op jit(solution)/shard_map/ppermute | solution.py:493

commit v8 on v7

--- a/solution.py
+++ b/solution.py
@@ -524,7 +524,8 @@
             mine = compact_rest(place, got)
         a, c, d = shift(mine, -1, 0), shift(mine, 0, -1), shift(mine, 0, 1)
         if k == last:
-            own = own_pairs([*blocks["O"], mine])
+            here, blocks["E"][-1] = tie((mine, blocks["E"][-1]))
+            own = own_pairs([*blocks["O"], here])
             a, own, halves = tie((a, own, halves))
         b = shift(a, -1, 0)
         if k == last:
@@ -533,7 +534,7 @@
             d, stats["O"] = tie((d, stats["O"]))
         e = shift(d, 0, 1)
         if k < last:
-            got, e, d, c, b, a = tie((later, e, d, c, b, a))
+            got, d, c, b, a = tie((later, d, c, b, a))
         for q, piece in zip("OABCDE", (mine, a, b, c, d, e)):
             blocks[q].append(piece)
     near = {q: blocks[q] for q in "OACD"}

time: 156 us -> 148 us (0.949)
  waiting for transfers between devices: 64.9 us -> 60.8 us
  local copies, waits for them, and re-layouts: 2.77 us -> 0.92 us
  starting transfers between devices: 32.8 us -> 31.2 us
    ppermute x15, waiting for transfers between devices: 39.5 us -> 31.5 us  [shift(): return lax.ppermute(array, ('tr', 'tc'), moves)]
    all_to_all x2, waiting for transfers between devices: 25.4 us -> 29.3 us  [exchange(): return lax.all_to_all(packed, 'tr', split_axis=0, concat_axis=0, tiled=True)]
    unnamed x16 -> x8, local copies, waits for them, and re-layouts: 2.77 us -> 0.92 us
    ppermute x15, starting transfers between devices: 23.1 us -> 21.5 us  [shift(): return lax.ppermute(array, ('tr', 'tc'), moves)]
  transfers between devices with their start and end apart: 17 -> 17, of which waited for: 9 -> 10; matrix products, arithmetic and copies ran while one was open for 0% -> 0% of each run, Pallas kernels for 17% -> 20%
where the time goes in v8:
time: 148 us; the launch traced here: 147 us
  waiting for transfers between devices  60.8 us (41%)
  Pallas kernels  44.3 us (30%)
  starting transfers between devices  31.2 us (21%)
  blocking collectives  9.14 us (6%)
    ppermute x15, waiting for transfers between devices, shift(): return lax.ppermute(array, ('tr', 'tc'), moves)  31.5 us
    all_to_all x2, waiting for transfers between devices, exchange(): return lax.all_to_all(packed, 'tr', split_axis=0, concat_axis=0, tiled=True)  29.3 us
    pallas_call x4, Pallas kernels, pairs(): pl.pallas_call(functools.partial(pair_kernel, plan, names, list(old)), ou...  21.7 us
    ppermute x15, starting transfers between devices, shift(): return lax.ppermute(array, ('tr', 'tc'), moves)  21.5 us
    all_to_all x2, starting transfers between devices, exchange(): return lax.all_to_all(packed, 'tr', split_axis=0, concat_axis=0, tiled=True)  9.7 us
    all_to_all x1, blocking collectives, exchange(): return lax.all_to_all(packed, 'tr', split_axis=0, concat_axis=0, tiled=True)  9.14 us
    pallas_call x1, Pallas kernels, pack_first(): pl.pallas_call(pack_first_kernel, grid=(TILE_ROWS,), in_specs=[whole((ROW...  7.57 us
    pallas_call x1, Pallas kernels, pack_rest(): pl.pallas_call(pack_rest_kernel, grid=(TILE_ROWS,), in_specs=[whole((ROWS...  6.09 us
  transfers between devices with their start and end apart: 17, of which 10 were waited for; matrix products, arithmetic and copies ran while one was open for 0% of the time, Pallas kernels for 20%

profile of v8, /device:TPU:2, one launch (start us, length us, event | category | flops | bytes accessed | tf_op | source)
XLA Modules:
  0.0 147.2 jit_solution(2386992538771415482)
XLA Ops:
  0.6 7.6 %pack_first.1 = (bf16[8,304,512]{2,1,0:T(8,128)(2,1)}, s32[1,768]{1,0:T(1,128)}, bf16[768,512]{1,0:T(8,128)(2,1)}) custom-call(bf16[768,1024]{1,0:T(8,128)(2,1)} %emb_ref.1, s32[768]{0:T(1024)} %lab_ref.5), custom_call_target="tpu_custom_call" | custom-call | tf_op jit(solution)/shard_map/pack_first/pallas_call | solution.py:101
  8.2 5.3 %all-to-all-start = ((bf16[8,304,512]{2,1,0:T(8,128)(2,1)}), bf16[8,304,512]{2,1,0:T(8,128)(2,1)S(1)}, u32[]{:S(2)}, u32[]{:S(2)}) async-start(bf16[8,304,512]{2,1,0:T(8,128)(2,1)} %get-tuple-element.38), calls=%async_computation | async-start | bytes 4980736 | tf_op jit(solution)/shard_map/all_to_all | solution.py:509
  13.5 6.1 %pack_rest.1 = bf16[8,288,512]{2,1,0:T(8,128)(2,1)} custom-call(bf16[768,512]{1,0:T(8,128)(2,1)} %get-tuple-element.36.unit_ref, s32[768]{0:T(1024)} %lab_ref.5, s32[1,768]{1,0:T(1,128)} %get-tuple-element.37.rank_ref), custom_call_target="tpu_custom_call" | custom-call | flops 1811939328 | bytes 2359296 | tf_op jit(solution)/shard_map/pack_rest/pallas_call | solution.py:128
  19.6 25.3 %all-to-all-done.got_ref = bf16[8,304,512]{2,1,0:T(8,128)(2,1)S(1)} async-done(((bf16[8,304,512]{2,1,0:T(8,128)(2,1)}), bf16[8,304,512]{2,1,0:T(8,128)(2,1)S(1)}, u32[]{:S(2)}, u32[]{:S(2)}) %all-to-all-start) | async-done | bytes 2490400 | tf_op jit(solution)/shard_map/all_to_all | solution.py:509
  44.9 4.4 %all-to-all-start.1 = ((bf16[8,288,512]{2,1,0:T(8,128)(2,1)}), bf16[8,288,512]{2,1,0:T(8,128)(2,1)}, u32[]{:S(2)}, u32[]{:S(2)}) async-start(bf16[8,288,512]{2,1,0:T(8,128)(2,1)} %pack_rest.1), calls=%async_computation.1 | async-start | bytes 4718592 | tf_op jit(solution)/shard_map/all_to_all | solution.py:509
  49.3 1.6 %compact_first.1 = (bf16[784,512]{1,0:T(8,128)(2,1)S(1)}, s32[16]{0:T(128)S(1)}) custom-call(bf16[8,304,512]{2,1,0:T(8,128)(2,1)S(1)} %all-to-all-done.got_ref), custom_call_target="tpu_custom_call" | custom-call | tf_op jit(solution)/shard_map/compact_first/pallas_call | solution.py:179
  51.0 0.6 collective-permute-start.2
  51.6 1.6 %collective-permute-start = (bf16[784,512]{1,0:T(8,128)(2,1)S(1)}, bf16[784,512]{1,0:T(8,128)(2,1)}, u32[]{:S(2)}, u32[]{:S(2)}) collective-permute-start(bf16[784,512]{1,0:T(8,128)(2,1)S(1)} %get-tuple-element.42.block.refs_0_), channel_id=1, source_target_pairs={{0,1},{1,2},{2,3},{3,0},{4,5},{5,6},{6,7},{7,4},{8,9},{9,10},{10,1... | collective-permute-start | bytes 2408456 | tf_op jit(solution)/shard_map/ppermute | solution.py:493
  53.1 1.7 %collective-permute-start.1 = (bf16[784,512]{1,0:T(8,128)(2,1)S(1)}, bf16[784,512]{1,0:T(8,128)(2,1)S(1)}, u32[]{:S(2)}, u32[]{:S(2)}) collective-permute-start(bf16[784,512]{1,0:T(8,128)(2,1)S(1)} %get-tuple-element.42.block.refs_0_), channel_id=1, source_target_pairs={{0,3},{1,0},{2,1},{3,2},{4,7},{5,4},{6,5},{7,6},{8,11},{9,8},{10,9... | collective-permute-start | bytes 2408456 | tf_op jit(solution)/shard_map/ppermute | solution.py:493
  54.8 8.4 %collective-permute-done.2.refs_1_.refs_0_ = bf16[784,512]{1,0:T(8,128)(2,1)S(1)} collective-permute-done((bf16[784,512]{1,0:T(8,128)(2,1)S(1)}, bf16[784,512]{1,0:T(8,128)(2,1)S(1)}, u32[]{:S(2)}, u32[]{:S(2)}) %collective-permute-start.2) | collective-permute-done | bytes 802848 | tf_op jit(solution)/shard_map/ppermute | solution.py:493
  63.2 0.8 collective-permute-start.3
  64.0 6.7 %collective-permute-done.refs_3_ = bf16[784,512]{1,0:T(8,128)(2,1)} collective-permute-done((bf16[784,512]{1,0:T(8,128)(2,1)S(1)}, bf16[784,512]{1,0:T(8,128)(2,1)}, u32[]{:S(2)}, u32[]{:S(2)}) %collective-permute-start) | collective-permute-done | bytes 802848 | tf_op jit(solution)/shard_map/ppermute | solution.py:493
  70.8 2.0 %collective-permute-start.5 = (bf16[784,512]{1,0:T(8,128)(2,1)}, bf16[784,512]{1,0:T(8,128)(2,1)}, u32[]{:S(2)}, u32[]{:S(2)}) collective-permute-start(bf16[784,512]{1,0:T(8,128)(2,1)} %collective-permute-done.refs_3_), channel_id=1, source_target_pairs={{0,1},{1,2},{2,3},{3,0},{4,5},{5,6},{6,7},{7,4},{8,9},{9,10},{10,1... | collective-permute-start | bytes 2408456 | tf_op jit(solution)/shard_map/ppermute | solution.py:493
  72.7 0.2 collective-permute-done.1.refs_2_.refs_1_
  72.9 0.0 copy-start.2
  72.9 0.9 copy-done.2
  73.8 1.5 %collective-permute-done.3.refs_2_.refs_1_ = bf16[784,512]{1,0:T(8,128)(2,1)S(1)} collective-permute-done((bf16[784,512]{1,0:T(8,128)(2,1)S(1)}, bf16[784,512]{1,0:T(8,128)(2,1)S(1)}, u32[]{:S(2)}, u32[]{:S(2)}) %collective-permute-start.3) | collective-permute-done | bytes 802848 | tf_op jit(solution)/shard_map/ppermute | solution.py:493
  75.4 4.0 %all-to-all-done.1.got_ref = bf16[8,288,512]{2,1,0:T(8,128)(2,1)} async-done(((bf16[8,288,512]{2,1,0:T(8,128)(2,1)}), bf16[8,288,512]{2,1,0:T(8,128)(2,1)}, u32[]{:S(2)}, u32[]{:S(2)}) %all-to-all-start.1) | async-done | bytes 2359328 | tf_op jit(solution)/shard_map/all_to_all | solution.py:509
  79.3 3.2 %compact_rest.1.refs_0_.refs_2_.refs_4_.refs_3_ = bf16[768,512]{1,0:T(8,128)(2,1)S(1)} custom-call(s32[16]{0:T(128)S(1)} %get-tuple-element.40.place_ref.offset_ref, bf16[8,288,512]{2,1,0:T(8,128)(2,1)} %all-to-all-done.1.got_ref), custom_call_target="tpu_custom_call" | custom-call | tf_op jit(solution)/shard_map/compact_rest/pallas_call | solution.py:201
  82.5 0.6 collective-permute-start.4
  83.1 1.6 %collective-permute-start.8 = (bf16[768,512]{1,0:T(8,128)(2,1)S(1)}, bf16[768,512]{1,0:T(8,128)(2,1)}, u32[]{:S(2)}, u32[]{:S(2)}) collective-permute-start(bf16[768,512]{1,0:T(8,128)(2,1)S(1)} %compact_rest.1.refs_0_.refs_2_.refs_4_.refs_3_), channel_id=1, source_target_pairs={{0,1},{1,2},{2,3},{3,0},{4,5},{5,6},{6,7},{7,4},{8,9},{9,10},{10,1... | collective-permute-start | bytes 2359304 | tf_op jit(solution)/shard_map/ppermute | solution.py:493
  84.7 1.7 %collective-permute-start.6 = (bf16[768,512]{1,0:T(8,128)(2,1)S(1)}, bf16[768,512]{1,0:T(8,128)(2,1)}, u32[]{:S(2)}, u32[]{:S(2)}) collective-permute-start(bf16[768,512]{1,0:T(8,128)(2,1)S(1)} %compact_rest.1.refs_0_.refs_2_.refs_4_.refs_3_), channel_id=1, source_target_pairs={{0,3},{1,0},{2,1},{3,2},{4,7},{5,4},{6,5},{7,6},{8,11},{9,8},{10,9... | collective-permute-start | bytes 2359304 | tf_op jit(solution)/shard_map/ppermute | solution.py:493
  86.4 0.1 pad_add_fusion.half_ref
  86.4 0.0 collective-permute-done.5.refs_2_
  86.4 2.0 %own.1.refs_4_ = f32[8,768]{1,0:T(8,128)S(1)} custom-call(bf16[784,512]{1,0:T(8,128)(2,1)S(1)} %get-tuple-element.42.block.refs_0_, bf16[768,512]{1,0:T(8,128)(2,1)S(1)} %compact_rest.1.refs_0_.refs_2_.refs_4_.refs_3_), custom_call_target="tpu_custom_call" | custom-call | flops 1207959552 | bytes 1605632 | tf_op jit(solution)/shard_map/own/pallas_call | solution.py:279
  88.4 0.0 copy-start.3
  88.4 6.2 %collective-permute-done.4.refs_3_.refs_5_ = bf16[768,512]{1,0:T(8,128)(2,1)} collective-permute-done((bf16[768,512]{1,0:T(8,128)(2,1)S(1)}, bf16[768,512]{1,0:T(8,128)(2,1)}, u32[]{:S(2)}, u32[]{:S(2)}) %collective-permute-start.4) | collective-permute-done | bytes 786464 | tf_op jit(solution)/shard_map/ppermute | solution.py:493
  94.7 0.7 collective-permute-start.7
  95.4 3.4 %pairs.4 = (f32[8,768]{1,0:T(8,128)S(1)}, f32[8,768]{1,0:T(8,128)S(1)}) custom-call(s32[2]{0:T(128)S(1)} %pad_add_fusion.half_ref, bf16[784,512]{1,0:T(8,128)(2,1)S(1)} %get-tuple-element.42.block.refs_0_, bf16[784,512]{1,0:T(8,128)(2,1)S(1)} %collective-permute-done.2.refs_1_.refs_0_, bf16[768,512]{1,0:T(8,128)(2,1)S(1)} %compact_rest.1.refs_0_.refs_2_.refs_4_.refs_3_, ...), custom_call_target="tpu_custom_call" | custom-call | flops 1207959552 | bytes 3211264 | tf_op jit(solution)/shard_map/pairs/pallas_call | solution.py:401
  98.8 3.9 %collective-permute-done.8.refs_7_ = bf16[768,512]{1,0:T(8,128)(2,1)} collective-permute-done((bf16[768,512]{1,0:T(8,128)(2,1)S(1)}, bf16[768,512]{1,0:T(8,128)(2,1)}, u32[]{:S(2)}, u32[]{:S(2)}) %collective-permute-start.8) | collective-permute-done | bytes 786464 | tf_op jit(solution)/shard_map/ppermute | solution.py:493
  102.7 1.8 %collective-permute-start.9 = (bf16[768,512]{1,0:T(8,128)(2,1)}, bf16[768,512]{1,0:T(8,128)(2,1)S(1)}, u32[]{:S(2)}, u32[]{:S(2)}) collective-permute-start(bf16[768,512]{1,0:T(8,128)(2,1)} %collective-permute-done.8.refs_7_), channel_id=1, source_target_pairs={{0,1},{1,2},{2,3},{3,0},{4,5},{5,6},{6,7},{7,4},{8,9},{9,10},{10,1... | collective-permute-start | bytes 2359304 | tf_op jit(solution)/shard_map/ppermute | solution.py:493
  104.5 0.0 collective-permute-done.6.refs_6_.refs_4_
  104.5 0.0 copy-done.3
  104.5 8.8 %pairs.5 = (f32[8,768]{1,0:T(8,128)S(1)}, f32[8,768]{1,0:T(8,128)S(1)}, f32[8,768]{1,0:T(8,128)S(1)}, f32[8,768]{1,0:T(8,128)S(1)}) custom-call(s32[2]{0:T(128)S(1)} %pad_add_fusion.half_ref, bf16[784,512]{1,0:T(8,128)(2,1)S(1)} %get-tuple-element.42.block.refs_0_, bf16[784,512]{1,0:T(8,128)(2,1)S(1)} %collective-permute-done.2.refs_1_.refs_0_, ...), custom_call_target="tpu_custom_call" | custom-call | flops 4227858432 | bytes 6422528 | tf_op jit(solution)/shard_map/pairs/pallas_call | solution.py:401
  113.3 0.0 collective-permute-done.7.refs_5_.refs_4_
  113.3 4.5 %pairs.6 = (f32[8,768]{1,0:T(8,128)S(1)}, f32[8,768]{1,0:T(8,128)S(1)}, f32[8,768]{1,0:T(8,128)S(1)}) custom-call(s32[2]{0:T(128)S(1)} %pad_add_fusion.half_ref, bf16[784,512]{1,0:T(8,128)(2,1)S(1)} %get-tuple-element.42.block.refs_0_, bf16[784,512]{1,0:T(8,128)(2,1)S(1)} %copy-done.3, bf16[784,512]{1,0:T(8,128)(2,1)S(1)} %collective-permute-done.3.refs_2_.refs_1_, ...), custom_call_target="tpu_custom_call" | custom-call | flops 1811939328 | bytes 4816896 | tf_op jit(solution)/shard_map/pairs/pallas_call | solution.py:401
  117.7 0.0 collective-permute-done.9.refs_5_
  117.8 0.0 copy-start
  117.8 0.0 copy-start.1
  117.8 5.0 %pairs.7 = (f32[8,768]{1,0:T(8,128)S(1)}, f32[8,768]{1,0:T(8,128)S(1)}, f32[8,768]{1,0:T(8,128)S(1)}) custom-call(s32[2]{0:T(128)S(1)} %pad_add_fusion.half_ref, bf16[784,512]{1,0:T(8,128)(2,1)S(1)} %collective-permute-done.2.refs_1_.refs_0_, bf16[784,512]{1,0:T(8,128)(2,1)S(1)} %collective-permute-done.3.refs_2_.refs_1_, ...), custom_call_target="tpu_custom_call" | custom-call | flops 1811939328 | bytes 4816896 | tf_op jit(solution)/shard_map/pairs/pallas_call | solution.py:401
  122.8 2.7 %collective-permute-start.11 = (f32[8,768]{1,0:T(8,128)S(1)}, f32[8,768]{1,0:T(8,128)S(1)}, u32[]{:S(2)}, u32[]{:S(2)}) collective-permute-start(f32[8,768]{1,0:T(8,128)S(1)} %get-tuple-element.65), channel_id=1, source_target_pairs={{0,8},{1,9},{2,10},{3,11},{4,12},{5,13},{6,14},{7,15},{8,0},{9,1},... | collective-permute-start | bytes 73736 | tf_op jit(solution)/shard_map/ppermute | solution.py:493
  125.5 2.7 %collective-permute-start.13 = (f32[8,768]{1,0:T(8,128)S(1)}, f32[8,768]{1,0:T(8,128)S(1)}, u32[]{:S(2)}, u32[]{:S(2)}) collective-permute-start(f32[8,768]{1,0:T(8,128)S(1)} %get-tuple-element.67), channel_id=1, source_target_pairs={{0,3},{1,0},{2,1},{3,2},{4,7},{5,4},{6,5},{7,6},{8,11},{9,8},{10,9... | collective-permute-start | bytes 73736 | tf_op jit(solution)/shard_map/ppermute | solution.py:493
  128.2 2.4 %collective-permute-start.10 = (f32[8,768]{1,0:T(8,128)S(1)}, f32[8,768]{1,0:T(8,128)S(1)}, u32[]{:S(2)}, u32[]{:S(2)}) collective-permute-start(f32[8,768]{1,0:T(8,128)S(1)} %get-tuple-element.62), channel_id=1, source_target_pairs={{0,4},{1,5},{2,6},{3,7},{4,8},{5,9},{6,10},{7,11},{8,12},{9,13},{1... | collective-permute-start | bytes 73736 | tf_op jit(solution)/shard_map/ppermute | solution.py:493
  130.6 0.0 collective-permute-start.14
  130.6 0.9 collective-permute-start.12
  131.4 0.0 collective-permute-done.11.refs_2_
  131.4 0.0 collective-permute-done.13.refs_4_
  131.4 0.7 collective-permute-done.10.refs_1_
  132.1 3.8 %collective-permute-done.14.refs_5_ = f32[8,768]{1,0:T(8,128)S(1)} collective-permute-done((f32[8,768]{1,0:T(8,128)S(1)}, f32[8,768]{1,0:T(8,128)S(1)}, u32[]{:S(2)}, u32[]{:S(2)}) %collective-permute-start.14) | collective-permute-done | bytes 24608 | tf_op jit(solution)/shard_map/ppermute | solution.py:493
  135.9 0.0 collective-permute-done.12.refs_3_
  135.9 0.7 spread.1
  136.6 9.1 %all_to_all.15.back_ref = f32[8,8,128]{2,1,0:T(8,128)S(1)} all-to-all(f32[8,8,128]{2,1,0:T(8,128)S(1)} %spread.1), channel_id=1, replica_groups=mesh['tr'=8,'tc'=16] {'tr'}, dimensions={0} | all-to-all | bytes 65536 | tf_op jit(solution)/shard_map/all_to_all | solution.py:509
  145.8 0.0 copy-done
  145.8 0.0 copy-done.1
  145.8 1.5 unpack.1
Async XLA Ops:
  8.2 36.7 %all-to-all-start = ((bf16[8,304,512]{2,1,0:T(8,128)(2,1)}), bf16[8,304,512]{2,1,0:T(8,128)(2,1)S(1)}, u32[]{:S(2)}, u32[]{:S(2)}) async-start(bf16[8,304,512]{2,1,0:T(8,128)(2,1)} %get-tuple-element.38), calls=%async_computation | async-start | bytes 4980736 | tf_op jit(solution)/shard_map/all_to_all | solution.py:509
  44.9 34.4 %all-to-all-start.1 = ((bf16[8,288,512]{2,1,0:T(8,128)(2,1)}), bf16[8,288,512]{2,1,0:T(8,128)(2,1)}, u32[]{:S(2)}, u32[]{:S(2)}) async-start(bf16[8,288,512]{2,1,0:T(8,128)(2,1)} %pack_rest.1), calls=%async_computation.1 | async-start | bytes 4718592 | tf_op jit(solution)/shard_map/all_to_all | solution.py:509
  51.0 12.2 %collective-permute-start.2 = (bf16[784,512]{1,0:T(8,128)(2,1)S(1)}, bf16[784,512]{1,0:T(8,128)(2,1)S(1)}, u32[]{:S(2)}, u32[]{:S(2)}) collective-permute-start(bf16[784,512]{1,0:T(8,128)(2,1)S(1)} %get-tuple-element.42.block.refs_0_), channel_id=1, source_target_pairs={{0,12},{1,13},{2,14},{3,15},{4,0},{5,1},{6,2},{7,3},{8,4},{9,5},{1... | collective-permute-start | bytes 2408456 | tf_op jit(solution)/shard_map/ppermute | solution.py:493
  51.6 19.2 %collective-permute-start = (bf16[784,512]{1,0:T(8,128)(2,1)S(1)}, bf16[784,512]{1,0:T(8,128)(2,1)}, u32[]{:S(2)}, u32[]{:S(2)}) collective-permute-start(bf16[784,512]{1,0:T(8,128)(2,1)S(1)} %get-tuple-element.42.block.refs_0_), channel_id=1, source_target_pairs={{0,1},{1,2},{2,3},{3,0},{4,5},{5,6},{6,7},{7,4},{8,9},{9,10},{10,1... | collective-permute-start | bytes 2408456 | tf_op jit(solution)/shard_map/ppermute | solution.py:493
  53.1 19.8 %collective-permute-start.1 = (bf16[784,512]{1,0:T(8,128)(2,1)S(1)}, bf16[784,512]{1,0:T(8,128)(2,1)S(1)}, u32[]{:S(2)}, u32[]{:S(2)}) collective-permute-start(bf16[784,512]{1,0:T(8,128)(2,1)S(1)} %get-tuple-element.42.block.refs_0_), channel_id=1, source_target_pairs={{0,3},{1,0},{2,1},{3,2},{4,7},{5,4},{6,5},{7,6},{8,11},{9,8},{10,9... | collective-permute-start | bytes 2408456 | tf_op jit(solution)/shard_map/ppermute | solution.py:493
  63.2 12.2 %collective-permute-start.3 = (bf16[784,512]{1,0:T(8,128)(2,1)S(1)}, bf16[784,512]{1,0:T(8,128)(2,1)S(1)}, u32[]{:S(2)}, u32[]{:S(2)}) collective-permute-start(bf16[784,512]{1,0:T(8,128)(2,1)S(1)} %collective-permute-done.2.refs_1_.refs_0_), channel_id=1, source_target_pairs={{0,12},{1,13},{2,14},{3,15},{4,0},{5,1},{6,2},{7,3},{8,4},{9,5},{1... | collective-permute-start | bytes 2408456 | tf_op jit(solution)/shard_map/ppermute | solution.py:493
  70.8 15.7 %collective-permute-start.5 = (bf16[784,512]{1,0:T(8,128)(2,1)}, bf16[784,512]{1,0:T(8,128)(2,1)}, u32[]{:S(2)}, u32[]{:S(2)}) collective-permute-start(bf16[784,512]{1,0:T(8,128)(2,1)} %collective-permute-done.refs_3_), channel_id=1, source_target_pairs={{0,1},{1,2},{2,3},{3,0},{4,5},{5,6},{6,7},{7,4},{8,9},{9,10},{10,1... | collective-permute-start | bytes 2408456 | tf_op jit(solution)/shard_map/ppermute | solution.py:493
  72.9 0.9 copy-start.2
  82.5 12.2 %collective-permute-start.4 = (bf16[768,512]{1,0:T(8,128)(2,1)S(1)}, bf16[768,512]{1,0:T(8,128)(2,1)}, u32[]{:S(2)}, u32[]{:S(2)}) collective-permute-start(bf16[768,512]{1,0:T(8,128)(2,1)S(1)} %compact_rest.1.refs_0_.refs_2_.refs_4_.refs_3_), channel_id=1, source_target_pairs={{0,12},{1,13},{2,14},{3,15},{4,0},{5,1},{6,2},{7,3},{8,4},{9,5},{1... | collective-permute-start | bytes 2359304 | tf_op jit(solution)/shard_map/ppermute | solution.py:493
  83.1 19.6 %collective-permute-start.8 = (bf16[768,512]{1,0:T(8,128)(2,1)S(1)}, bf16[768,512]{1,0:T(8,128)(2,1)}, u32[]{:S(2)}, u32[]{:S(2)}) collective-permute-start(bf16[768,512]{1,0:T(8,128)(2,1)S(1)} %compact_rest.1.refs_0_.refs_2_.refs_4_.refs_3_), channel_id=1, source_target_pairs={{0,1},{1,2},{2,3},{3,0},{4,5},{5,6},{6,7},{7,4},{8,9},{9,10},{10,1... | collective-permute-start | bytes 2359304 | tf_op jit(solution)/shard_map/ppermute | solution.py:493
  84.7 19.8 %collective-permute-start.6 = (bf16[768,512]{1,0:T(8,128)(2,1)S(1)}, bf16[768,512]{1,0:T(8,128)(2,1)}, u32[]{:S(2)}, u32[]{:S(2)}) collective-permute-start(bf16[768,512]{1,0:T(8,128)(2,1)S(1)} %compact_rest.1.refs_0_.refs_2_.refs_4_.refs_3_), channel_id=1, source_target_pairs={{0,3},{1,0},{2,1},{3,2},{4,7},{5,4},{6,5},{7,6},{8,11},{9,8},{10,9... | collective-permute-start | bytes 2359304 | tf_op jit(solution)/shard_map/ppermute | solution.py:493
  88.4 16.0 %copy-start.3 = (bf16[784,512]{1,0:T(8,128)(2,1)S(1)}, bf16[784,512]{1,0:T(8,128)(2,1)}, u32[]{:S(2)}) copy-start(bf16[784,512]{1,0:T(8,128)(2,1)} %copy-done.2) | copy-start | bytes 2408452
  94.7 18.6 %collective-permute-start.7 = (bf16[768,512]{1,0:T(8,128)(2,1)}, bf16[768,512]{1,0:T(8,128)(2,1)S(1)}, u32[]{:S(2)}, u32[]{:S(2)}) collective-permute-start(bf16[768,512]{1,0:T(8,128)(2,1)} %collective-permute-done.4.refs_3_.refs_5_), channel_id=1, source_target_pairs={{0,12},{1,13},{2,14},{3,15},{4,0},{5,1},{6,2},{7,3},{8,4},{9,5},{1... | collective-permute-start | bytes 2359304 | tf_op jit(solution)/shard_map/ppermute | solution.py:493
  102.7 15.0 %collective-permute-start.9 = (bf16[768,512]{1,0:T(8,128)(2,1)}, bf16[768,512]{1,0:T(8,128)(2,1)S(1)}, u32[]{:S(2)}, u32[]{:S(2)}) collective-permute-start(bf16[768,512]{1,0:T(8,128)(2,1)} %collective-permute-done.8.refs_7_), channel_id=1, source_target_pairs={{0,1},{1,2},{2,3},{3,0},{4,5},{5,6},{6,7},{7,4},{8,9},{9,10},{10,1... | collective-permute-start | bytes 2359304 | tf_op jit(solution)/shard_map/ppermute | solution.py:493
  117.8 28.0 %copy-start = (s32[768]{0:T(1024)S(1)}, s32[768]{0:T(1024)}, u32[]{:S(2)}) copy-start(s32[768]{0:T(1024)} %lab_ref.5) | copy-start | bytes 9220
  117.8 28.0 %copy-start.1 = (s32[1,768]{1,0:T(1,128)S(1)}, s32[1,768]{1,0:T(1,128)}, u32[]{:S(2)}) copy-start(s32[1,768]{1,0:T(1,128)} %get-tuple-element.37.rank_ref) | copy-start | bytes 9220
  122.8 8.6 %collective-permute-start.11 = (f32[8,768]{1,0:T(8,128)S(1)}, f32[8,768]{1,0:T(8,128)S(1)}, u32[]{:S(2)}, u32[]{:S(2)}) collective-permute-start(f32[8,768]{1,0:T(8,128)S(1)} %get-tuple-element.65), channel_id=1, source_target_pairs={{0,8},{1,9},{2,10},{3,11},{4,12},{5,13},{6,14},{7,15},{8,0},{9,1},... | collective-permute-start | bytes 73736 | tf_op jit(solution)/shard_map/ppermute | solution.py:493
  125.5 5.9 %collective-permute-start.13 = (f32[8,768]{1,0:T(8,128)S(1)}, f32[8,768]{1,0:T(8,128)S(1)}, u32[]{:S(2)}, u32[]{:S(2)}) collective-permute-start(f32[8,768]{1,0:T(8,128)S(1)} %get-tuple-element.67), channel_id=1, source_target_pairs={{0,3},{1,0},{2,1},{3,2},{4,7},{5,4},{6,5},{7,6},{8,11},{9,8},{10,9... | collective-permute-start | bytes 73736 | tf_op jit(solution)/shard_map/ppermute | solution.py:493
  128.2 3.9 %collective-permute-start.10 = (f32[8,768]{1,0:T(8,128)S(1)}, f32[8,768]{1,0:T(8,128)S(1)}, u32[]{:S(2)}, u32[]{:S(2)}) collective-permute-start(f32[8,768]{1,0:T(8,128)S(1)} %get-tuple-element.62), channel_id=1, source_target_pairs={{0,4},{1,5},{2,6},{3,7},{4,8},{5,9},{6,10},{7,11},{8,12},{9,13},{1... | collective-permute-start | bytes 73736 | tf_op jit(solution)/shard_map/ppermute | solution.py:493
  130.6 5.3 %collective-permute-start.14 = (f32[8,768]{1,0:T(8,128)S(1)}, f32[8,768]{1,0:T(8,128)S(1)}, u32[]{:S(2)}, u32[]{:S(2)}) collective-permute-start(f32[8,768]{1,0:T(8,128)S(1)} %get-tuple-element.68), channel_id=1, source_target_pairs={{0,2},{1,3},{2,0},{3,1},{4,6},{5,7},{6,4},{7,5},{8,10},{9,11},{10,... | collective-permute-start | bytes 73736 | tf_op jit(solution)/shard_map/ppermute | solution.py:493
  130.6 5.3 %collective-permute-start.12 = (f32[8,768]{1,0:T(8,128)S(1)}, f32[8,768]{1,0:T(8,128)S(1)}, u32[]{:S(2)}, u32[]{:S(2)}) collective-permute-start(f32[8,768]{1,0:T(8,128)S(1)} %get-tuple-element.66), channel_id=1, source_target_pairs={{0,1},{1,2},{2,3},{3,0},{4,5},{5,6},{6,7},{7,4},{8,9},{9,10},{10,1... | collective-permute-start | bytes 73736 | tf_op jit(solution)/shard_map/ppermute | solution.py:493

commit v9 on v8

--- a/solution.py
+++ b/solution.py
@@ -28,6 +28,7 @@
 FLOOR = -5e29
 CHUNK = 256
 HALF = 384
+AT_ONCE = 2
 STRIP = 32
 VMEM = 24 * 1024 * 1024
 PACK_VMEM = 56 * 1024 * 1024
@@ -90,20 +91,21 @@
         seen = dot(onehot.astype(BF), before)
         rank_ref[...] = jnp.sum(onehot * seen, axis=0, keepdims=True).astype(jnp.int32)
 
-    chosen = pick(lab_ref, rank_ref, g, LANES)
-    out_ref[0] = dot(chosen[:PAIR], unit[...]).astype(BF)
     marks = jnp.broadcast_to(lab.astype(F32) + 1.0, (TAIL, ROWS)).astype(BF)
-    out_ref[0, CAP:, :LANES] = (dot_nt(marks, chosen) - 1.0).astype(BF)
-    out_ref[0, CAP:, LANES:] = jnp.zeros((TAIL, PIECE - LANES), BF)
+    for k in range(AT_ONCE):
+        chosen = pick(lab_ref, rank_ref, g * AT_ONCE + k, LANES)
+        out_ref[k] = dot(chosen[:PAIR], unit[...]).astype(BF)
+        out_ref[k, CAP:, :LANES] = (dot_nt(marks, chosen) - 1.0).astype(BF)
+        out_ref[k, CAP:, LANES:] = jnp.zeros((TAIL, PIECE - LANES), BF)
 
 
 def pack_first(embeddings, labels):
     return pl.pallas_call(
         pack_first_kernel,
-        grid=(TILE_ROWS,),
+        grid=(TILE_ROWS // AT_ONCE,),
         in_specs=[whole((ROWS, WIDTH)), whole((ROWS,))],
         out_specs=[
-            pl.BlockSpec((1, PAIR, PIECE), lambda g: (g, 0, 0)),
+            pl.BlockSpec((AT_ONCE, PAIR, PIECE), lambda g: (g, 0, 0)),
             whole((1, ROWS)),
         ]
         + [whole((ROWS, w)) for w in PIECES[1:]],

time: 148 us -> 147 us (level)
  no operation moved by 1% of the time
where the time goes in v9:
time: 147 us; the launch traced here: 146 us
  waiting for transfers between devices  60.8 us (41%)
  Pallas kernels  43.2 us (29%)
  starting transfers between devices  31.3 us (21%)
  blocking collectives  9.16 us (6%)
    ppermute x15, waiting for transfers between devices, shift(): return lax.ppermute(array, ('tr', 'tc'), moves)  31.5 us
    all_to_all x2, waiting for transfers between devices, exchange(): return lax.all_to_all(packed, 'tr', split_axis=0, concat_axis=0, tiled=True)  29.3 us
    pallas_call x4, Pallas kernels, pairs(): pl.pallas_call(functools.partial(pair_kernel, plan, names, list(old)), ou...  21.7 us
    ppermute x15, starting transfers between devices, shift(): return lax.ppermute(array, ('tr', 'tc'), moves)  21.6 us
    all_to_all x2, starting transfers between devices, exchange(): return lax.all_to_all(packed, 'tr', split_axis=0, concat_axis=0, tiled=True)  9.7 us
    all_to_all x1, blocking collectives, exchange(): return lax.all_to_all(packed, 'tr', split_axis=0, concat_axis=0, tiled=True)  9.16 us
    pallas_call x1, Pallas kernels, pack_first(): pl.pallas_call(pack_first_kernel, grid=(TILE_ROWS // AT_ONCE,), in_specs=...  6.44 us
    pallas_call x1, Pallas kernels, pack_rest(): pl.pallas_call(pack_rest_kernel, grid=(TILE_ROWS,), in_specs=[whole((ROWS...  6.09 us
  transfers between devices with their start and end apart: 17, of which 10 were waited for; matrix products, arithmetic and copies ran while one was open for 0% of the time, Pallas kernels for 20%

profile of v9, /device:TPU:2, one launch (start us, length us, event | category | flops | bytes accessed | tf_op | source)
XLA Modules:
  0.0 146.1 jit_solution(16247030607201816650)
XLA Ops:
  0.6 6.4 %pack_first.1 = (bf16[8,304,512]{2,1,0:T(8,128)(2,1)}, s32[1,768]{1,0:T(1,128)}, bf16[768,512]{1,0:T(8,128)(2,1)}) custom-call(bf16[768,1024]{1,0:T(8,128)(2,1)} %emb_ref.1, s32[768]{0:T(1024)} %lab_ref.5), custom_call_target="tpu_custom_call" | custom-call | tf_op jit(solution)/shard_map/pack_first/pallas_call | solution.py:103
  7.1 5.3 %all-to-all-start = ((bf16[8,304,512]{2,1,0:T(8,128)(2,1)}), bf16[8,304,512]{2,1,0:T(8,128)(2,1)S(1)}, u32[]{:S(2)}, u32[]{:S(2)}) async-start(bf16[8,304,512]{2,1,0:T(8,128)(2,1)} %get-tuple-element.38), calls=%async_computation | async-start | bytes 4980736 | tf_op jit(solution)/shard_map/all_to_all | solution.py:511
  12.4 6.1 %pack_rest.1 = bf16[8,288,512]{2,1,0:T(8,128)(2,1)} custom-call(bf16[768,512]{1,0:T(8,128)(2,1)} %get-tuple-element.36.unit_ref, s32[768]{0:T(1024)} %lab_ref.5, s32[1,768]{1,0:T(1,128)} %get-tuple-element.37.rank_ref), custom_call_target="tpu_custom_call" | custom-call | flops 1811939328 | bytes 2359296 | tf_op jit(solution)/shard_map/pack_rest/pallas_call | solution.py:130
  18.5 25.3 %all-to-all-done.got_ref = bf16[8,304,512]{2,1,0:T(8,128)(2,1)S(1)} async-done(((bf16[8,304,512]{2,1,0:T(8,128)(2,1)}), bf16[8,304,512]{2,1,0:T(8,128)(2,1)S(1)}, u32[]{:S(2)}, u32[]{:S(2)}) %all-to-all-start) | async-done | bytes 2490400 | tf_op jit(solution)/shard_map/all_to_all | solution.py:511
  43.8 4.4 %all-to-all-start.1 = ((bf16[8,288,512]{2,1,0:T(8,128)(2,1)}), bf16[8,288,512]{2,1,0:T(8,128)(2,1)}, u32[]{:S(2)}, u32[]{:S(2)}) async-start(bf16[8,288,512]{2,1,0:T(8,128)(2,1)} %pack_rest.1), calls=%async_computation.1 | async-start | bytes 4718592 | tf_op jit(solution)/shard_map/all_to_all | solution.py:511
  48.2 1.6 %compact_first.1 = (bf16[784,512]{1,0:T(8,128)(2,1)S(1)}, s32[16]{0:T(128)S(1)}) custom-call(bf16[8,304,512]{2,1,0:T(8,128)(2,1)S(1)} %all-to-all-done.got_ref), custom_call_target="tpu_custom_call" | custom-call | tf_op jit(solution)/shard_map/compact_first/pallas_call | solution.py:181
  49.8 0.6 collective-permute-start.2
  50.4 1.6 %collective-permute-start = (bf16[784,512]{1,0:T(8,128)(2,1)S(1)}, bf16[784,512]{1,0:T(8,128)(2,1)}, u32[]{:S(2)}, u32[]{:S(2)}) collective-permute-start(bf16[784,512]{1,0:T(8,128)(2,1)S(1)} %get-tuple-element.42.block.refs_0_), channel_id=1, source_target_pairs={{0,1},{1,2},{2,3},{3,0},{4,5},{5,6},{6,7},{7,4},{8,9},{9,10},{10,1... | collective-permute-start | bytes 2408456 | tf_op jit(solution)/shard_map/ppermute | solution.py:495
  52.0 1.7 %collective-permute-start.1 = (bf16[784,512]{1,0:T(8,128)(2,1)S(1)}, bf16[784,512]{1,0:T(8,128)(2,1)S(1)}, u32[]{:S(2)}, u32[]{:S(2)}) collective-permute-start(bf16[784,512]{1,0:T(8,128)(2,1)S(1)} %get-tuple-element.42.block.refs_0_), channel_id=1, source_target_pairs={{0,3},{1,0},{2,1},{3,2},{4,7},{5,4},{6,5},{7,6},{8,11},{9,8},{10,9... | collective-permute-start | bytes 2408456 | tf_op jit(solution)/shard_map/ppermute | solution.py:495
  53.7 8.4 %collective-permute-done.2.refs_1_.refs_0_ = bf16[784,512]{1,0:T(8,128)(2,1)S(1)} collective-permute-done((bf16[784,512]{1,0:T(8,128)(2,1)S(1)}, bf16[784,512]{1,0:T(8,128)(2,1)S(1)}, u32[]{:S(2)}, u32[]{:S(2)}) %collective-permute-start.2) | collective-permute-done | bytes 802848 | tf_op jit(solution)/shard_map/ppermute | solution.py:495
  62.0 0.8 collective-permute-start.3
  62.9 6.8 %collective-permute-done.refs_3_ = bf16[784,512]{1,0:T(8,128)(2,1)} collective-permute-done((bf16[784,512]{1,0:T(8,128)(2,1)S(1)}, bf16[784,512]{1,0:T(8,128)(2,1)}, u32[]{:S(2)}, u32[]{:S(2)}) %collective-permute-start) | collective-permute-done | bytes 802848 | tf_op jit(solution)/shard_map/ppermute | solution.py:495
  69.6 2.0 %collective-permute-start.5 = (bf16[784,512]{1,0:T(8,128)(2,1)}, bf16[784,512]{1,0:T(8,128)(2,1)}, u32[]{:S(2)}, u32[]{:S(2)}) collective-permute-start(bf16[784,512]{1,0:T(8,128)(2,1)} %collective-permute-done.refs_3_), channel_id=1, source_target_pairs={{0,1},{1,2},{2,3},{3,0},{4,5},{5,6},{6,7},{7,4},{8,9},{9,10},{10,1... | collective-permute-start | bytes 2408456 | tf_op jit(solution)/shard_map/ppermute | solution.py:495
  71.6 0.2 collective-permute-done.1.refs_2_.refs_1_
  71.8 0.0 copy-start.2
  71.8 0.9 copy-done.2
  72.7 1.5 %collective-permute-done.3.refs_2_.refs_1_ = bf16[784,512]{1,0:T(8,128)(2,1)S(1)} collective-permute-done((bf16[784,512]{1,0:T(8,128)(2,1)S(1)}, bf16[784,512]{1,0:T(8,128)(2,1)S(1)}, u32[]{:S(2)}, u32[]{:S(2)}) %collective-permute-start.3) | collective-permute-done | bytes 802848 | tf_op jit(solution)/shard_map/ppermute | solution.py:495
  74.2 4.0 %all-to-all-done.1.got_ref = bf16[8,288,512]{2,1,0:T(8,128)(2,1)} async-done(((bf16[8,288,512]{2,1,0:T(8,128)(2,1)}), bf16[8,288,512]{2,1,0:T(8,128)(2,1)}, u32[]{:S(2)}, u32[]{:S(2)}) %all-to-all-start.1) | async-done | bytes 2359328 | tf_op jit(solution)/shard_map/all_to_all | solution.py:511
  78.2 3.2 %compact_rest.1.refs_0_.refs_2_.refs_4_.refs_3_ = bf16[768,512]{1,0:T(8,128)(2,1)S(1)} custom-call(s32[16]{0:T(128)S(1)} %get-tuple-element.40.place_ref.offset_ref, bf16[8,288,512]{2,1,0:T(8,128)(2,1)} %all-to-all-done.1.got_ref), custom_call_target="tpu_custom_call" | custom-call | tf_op jit(solution)/shard_map/compact_rest/pallas_call | solution.py:203
  81.4 0.6 collective-permute-start.4
  82.0 1.6 %collective-permute-start.8 = (bf16[768,512]{1,0:T(8,128)(2,1)S(1)}, bf16[768,512]{1,0:T(8,128)(2,1)}, u32[]{:S(2)}, u32[]{:S(2)}) collective-permute-start(bf16[768,512]{1,0:T(8,128)(2,1)S(1)} %compact_rest.1.refs_0_.refs_2_.refs_4_.refs_3_), channel_id=1, source_target_pairs={{0,1},{1,2},{2,3},{3,0},{4,5},{5,6},{6,7},{7,4},{8,9},{9,10},{10,1... | collective-permute-start | bytes 2359304 | tf_op jit(solution)/shard_map/ppermute | solution.py:495
  83.6 1.7 %collective-permute-start.6 = (bf16[768,512]{1,0:T(8,128)(2,1)S(1)}, bf16[768,512]{1,0:T(8,128)(2,1)}, u32[]{:S(2)}, u32[]{:S(2)}) collective-permute-start(bf16[768,512]{1,0:T(8,128)(2,1)S(1)} %compact_rest.1.refs_0_.refs_2_.refs_4_.refs_3_), channel_id=1, source_target_pairs={{0,3},{1,0},{2,1},{3,2},{4,7},{5,4},{6,5},{7,6},{8,11},{9,8},{10,9... | collective-permute-start | bytes 2359304 | tf_op jit(solution)/shard_map/ppermute | solution.py:495
  85.2 0.1 pad_add_fusion.half_ref
  85.3 0.0 collective-permute-done.5.refs_2_
  85.3 2.0 %own.1.refs_4_ = f32[8,768]{1,0:T(8,128)S(1)} custom-call(bf16[784,512]{1,0:T(8,128)(2,1)S(1)} %get-tuple-element.42.block.refs_0_, bf16[768,512]{1,0:T(8,128)(2,1)S(1)} %compact_rest.1.refs_0_.refs_2_.refs_4_.refs_3_), custom_call_target="tpu_custom_call" | custom-call | flops 1207959552 | bytes 1605632 | tf_op jit(solution)/shard_map/own/pallas_call | solution.py:281
  87.3 0.0 copy-start.3
  87.3 6.2 %collective-permute-done.4.refs_3_.refs_5_ = bf16[768,512]{1,0:T(8,128)(2,1)} collective-permute-done((bf16[768,512]{1,0:T(8,128)(2,1)S(1)}, bf16[768,512]{1,0:T(8,128)(2,1)}, u32[]{:S(2)}, u32[]{:S(2)}) %collective-permute-start.4) | collective-permute-done | bytes 786464 | tf_op jit(solution)/shard_map/ppermute | solution.py:495
  93.5 0.7 collective-permute-start.7
  94.3 3.4 %pairs.4 = (f32[8,768]{1,0:T(8,128)S(1)}, f32[8,768]{1,0:T(8,128)S(1)}) custom-call(s32[2]{0:T(128)S(1)} %pad_add_fusion.half_ref, bf16[784,512]{1,0:T(8,128)(2,1)S(1)} %get-tuple-element.42.block.refs_0_, bf16[784,512]{1,0:T(8,128)(2,1)S(1)} %collective-permute-done.2.refs_1_.refs_0_, bf16[768,512]{1,0:T(8,128)(2,1)S(1)} %compact_rest.1.refs_0_.refs_2_.refs_4_.refs_3_, ...), custom_call_target="tpu_custom_call" | custom-call | flops 1207959552 | bytes 3211264 | tf_op jit(solution)/shard_map/pairs/pallas_call | solution.py:403
  97.7 3.9 %collective-permute-done.8.refs_7_ = bf16[768,512]{1,0:T(8,128)(2,1)} collective-permute-done((bf16[768,512]{1,0:T(8,128)(2,1)S(1)}, bf16[768,512]{1,0:T(8,128)(2,1)}, u32[]{:S(2)}, u32[]{:S(2)}) %collective-permute-start.8) | collective-permute-done | bytes 786464 | tf_op jit(solution)/shard_map/ppermute | solution.py:495
  101.6 1.8 %collective-permute-start.9 = (bf16[768,512]{1,0:T(8,128)(2,1)}, bf16[768,512]{1,0:T(8,128)(2,1)S(1)}, u32[]{:S(2)}, u32[]{:S(2)}) collective-permute-start(bf16[768,512]{1,0:T(8,128)(2,1)} %collective-permute-done.8.refs_7_), channel_id=1, source_target_pairs={{0,1},{1,2},{2,3},{3,0},{4,5},{5,6},{6,7},{7,4},{8,9},{9,10},{10,1... | collective-permute-start | bytes 2359304 | tf_op jit(solution)/shard_map/ppermute | solution.py:495
  103.3 0.0 collective-permute-done.6.refs_6_.refs_4_
  103.3 0.0 copy-done.3
  103.3 8.8 %pairs.5 = (f32[8,768]{1,0:T(8,128)S(1)}, f32[8,768]{1,0:T(8,128)S(1)}, f32[8,768]{1,0:T(8,128)S(1)}, f32[8,768]{1,0:T(8,128)S(1)}) custom-call(s32[2]{0:T(128)S(1)} %pad_add_fusion.half_ref, bf16[784,512]{1,0:T(8,128)(2,1)S(1)} %get-tuple-element.42.block.refs_0_, bf16[784,512]{1,0:T(8,128)(2,1)S(1)} %collective-permute-done.2.refs_1_.refs_0_, ...), custom_call_target="tpu_custom_call" | custom-call | flops 4227858432 | bytes 6422528 | tf_op jit(solution)/shard_map/pairs/pallas_call | solution.py:403
  112.1 0.0 collective-permute-done.7.refs_5_.refs_4_
  112.1 4.5 %pairs.6 = (f32[8,768]{1,0:T(8,128)S(1)}, f32[8,768]{1,0:T(8,128)S(1)}, f32[8,768]{1,0:T(8,128)S(1)}) custom-call(s32[2]{0:T(128)S(1)} %pad_add_fusion.half_ref, bf16[784,512]{1,0:T(8,128)(2,1)S(1)} %get-tuple-element.42.block.refs_0_, bf16[784,512]{1,0:T(8,128)(2,1)S(1)} %copy-done.3, bf16[784,512]{1,0:T(8,128)(2,1)S(1)} %collective-permute-done.3.refs_2_.refs_1_, ...), custom_call_target="tpu_custom_call" | custom-call | flops 1811939328 | bytes 4816896 | tf_op jit(solution)/shard_map/pairs/pallas_call | solution.py:403
  116.6 0.0 collective-permute-done.9.refs_5_
  116.6 0.0 copy-start
  116.6 0.0 copy-start.1
  116.6 5.0 %pairs.7 = (f32[8,768]{1,0:T(8,128)S(1)}, f32[8,768]{1,0:T(8,128)S(1)}, f32[8,768]{1,0:T(8,128)S(1)}) custom-call(s32[2]{0:T(128)S(1)} %pad_add_fusion.half_ref, bf16[784,512]{1,0:T(8,128)(2,1)S(1)} %collective-permute-done.2.refs_1_.refs_0_, bf16[784,512]{1,0:T(8,128)(2,1)S(1)} %collective-permute-done.3.refs_2_.refs_1_, ...), custom_call_target="tpu_custom_call" | custom-call | flops 1811939328 | bytes 4816896 | tf_op jit(solution)/shard_map/pairs/pallas_call | solution.py:403
  121.7 2.7 %collective-permute-start.11 = (f32[8,768]{1,0:T(8,128)S(1)}, f32[8,768]{1,0:T(8,128)S(1)}, u32[]{:S(2)}, u32[]{:S(2)}) collective-permute-start(f32[8,768]{1,0:T(8,128)S(1)} %get-tuple-element.65), channel_id=1, source_target_pairs={{0,8},{1,9},{2,10},{3,11},{4,12},{5,13},{6,14},{7,15},{8,0},{9,1},... | collective-permute-start | bytes 73736 | tf_op jit(solution)/shard_map/ppermute | solution.py:495
  124.4 2.7 %collective-permute-start.13 = (f32[8,768]{1,0:T(8,128)S(1)}, f32[8,768]{1,0:T(8,128)S(1)}, u32[]{:S(2)}, u32[]{:S(2)}) collective-permute-start(f32[8,768]{1,0:T(8,128)S(1)} %get-tuple-element.67), channel_id=1, source_target_pairs={{0,3},{1,0},{2,1},{3,2},{4,7},{5,4},{6,5},{7,6},{8,11},{9,8},{10,9... | collective-permute-start | bytes 73736 | tf_op jit(solution)/shard_map/ppermute | solution.py:495
  127.1 2.4 %collective-permute-start.10 = (f32[8,768]{1,0:T(8,128)S(1)}, f32[8,768]{1,0:T(8,128)S(1)}, u32[]{:S(2)}, u32[]{:S(2)}) collective-permute-start(f32[8,768]{1,0:T(8,128)S(1)} %get-tuple-element.62), channel_id=1, source_target_pairs={{0,4},{1,5},{2,6},{3,7},{4,8},{5,9},{6,10},{7,11},{8,12},{9,13},{1... | collective-permute-start | bytes 73736 | tf_op jit(solution)/shard_map/ppermute | solution.py:495
  129.4 0.0 collective-permute-start.14
  129.4 0.9 collective-permute-start.12
  130.3 0.0 collective-permute-done.11.refs_2_
  130.3 0.0 collective-permute-done.13.refs_4_
  130.3 0.7 collective-permute-done.10.refs_1_
  131.0 3.8 %collective-permute-done.14.refs_5_ = f32[8,768]{1,0:T(8,128)S(1)} collective-permute-done((f32[8,768]{1,0:T(8,128)S(1)}, f32[8,768]{1,0:T(8,128)S(1)}, u32[]{:S(2)}, u32[]{:S(2)}) %collective-permute-start.14) | collective-permute-done | bytes 24608 | tf_op jit(solution)/shard_map/ppermute | solution.py:495
  134.8 0.0 collective-permute-done.12.refs_3_
  134.8 0.7 spread.1
  135.5 9.2 %all_to_all.15.back_ref = f32[8,8,128]{2,1,0:T(8,128)S(1)} all-to-all(f32[8,8,128]{2,1,0:T(8,128)S(1)} %spread.1), channel_id=1, replica_groups=mesh['tr'=8,'tc'=16] {'tr'}, dimensions={0} | all-to-all | bytes 65536 | tf_op jit(solution)/shard_map/all_to_all | solution.py:511
  144.7 0.0 copy-done
  144.7 0.0 copy-done.1
  144.7 1.5 %unpack.1 = (f32[768]{0:T(1024)}, f32[768]{0:T(1024)}, f32[768]{0:T(1024)}) custom-call(f32[8,8,128]{2,1,0:T(8,128)S(1)} %all_to_all.15.back_ref, s32[768]{0:T(1024)S(1)} %copy-done, s32[1,768]{1,0:T(1,128)S(1)} %copy-done.1), custom_call_target="tpu_custom_call" | custom-call | tf_op jit(solution)/shard_map/unpack/pallas_call | solution.py:476
Async XLA Ops:
  7.1 36.7 %all-to-all-start = ((bf16[8,304,512]{2,1,0:T(8,128)(2,1)}), bf16[8,304,512]{2,1,0:T(8,128)(2,1)S(1)}, u32[]{:S(2)}, u32[]{:S(2)}) async-start(bf16[8,304,512]{2,1,0:T(8,128)(2,1)} %get-tuple-element.38), calls=%async_computation | async-start | bytes 4980736 | tf_op jit(solution)/shard_map/all_to_all | solution.py:511
  43.8 34.4 %all-to-all-start.1 = ((bf16[8,288,512]{2,1,0:T(8,128)(2,1)}), bf16[8,288,512]{2,1,0:T(8,128)(2,1)}, u32[]{:S(2)}, u32[]{:S(2)}) async-start(bf16[8,288,512]{2,1,0:T(8,128)(2,1)} %pack_rest.1), calls=%async_computation.1 | async-start | bytes 4718592 | tf_op jit(solution)/shard_map/all_to_all | solution.py:511
  49.8 12.2 %collective-permute-start.2 = (bf16[784,512]{1,0:T(8,128)(2,1)S(1)}, bf16[784,512]{1,0:T(8,128)(2,1)S(1)}, u32[]{:S(2)}, u32[]{:S(2)}) collective-permute-start(bf16[784,512]{1,0:T(8,128)(2,1)S(1)} %get-tuple-element.42.block.refs_0_), channel_id=1, source_target_pairs={{0,12},{1,13},{2,14},{3,15},{4,0},{5,1},{6,2},{7,3},{8,4},{9,5},{1... | collective-permute-start | bytes 2408456 | tf_op jit(solution)/shard_map/ppermute | solution.py:495
  50.4 19.2 %collective-permute-start = (bf16[784,512]{1,0:T(8,128)(2,1)S(1)}, bf16[784,512]{1,0:T(8,128)(2,1)}, u32[]{:S(2)}, u32[]{:S(2)}) collective-permute-start(bf16[784,512]{1,0:T(8,128)(2,1)S(1)} %get-tuple-element.42.block.refs_0_), channel_id=1, source_target_pairs={{0,1},{1,2},{2,3},{3,0},{4,5},{5,6},{6,7},{7,4},{8,9},{9,10},{10,1... | collective-permute-start | bytes 2408456 | tf_op jit(solution)/shard_map/ppermute | solution.py:495
  52.0 19.8 %collective-permute-start.1 = (bf16[784,512]{1,0:T(8,128)(2,1)S(1)}, bf16[784,512]{1,0:T(8,128)(2,1)S(1)}, u32[]{:S(2)}, u32[]{:S(2)}) collective-permute-start(bf16[784,512]{1,0:T(8,128)(2,1)S(1)} %get-tuple-element.42.block.refs_0_), channel_id=1, source_target_pairs={{0,3},{1,0},{2,1},{3,2},{4,7},{5,4},{6,5},{7,6},{8,11},{9,8},{10,9... | collective-permute-start | bytes 2408456 | tf_op jit(solution)/shard_map/ppermute | solution.py:495
  62.0 12.2 %collective-permute-start.3 = (bf16[784,512]{1,0:T(8,128)(2,1)S(1)}, bf16[784,512]{1,0:T(8,128)(2,1)S(1)}, u32[]{:S(2)}, u32[]{:S(2)}) collective-permute-start(bf16[784,512]{1,0:T(8,128)(2,1)S(1)} %collective-permute-done.2.refs_1_.refs_0_), channel_id=1, source_target_pairs={{0,12},{1,13},{2,14},{3,15},{4,0},{5,1},{6,2},{7,3},{8,4},{9,5},{1... | collective-permute-start | bytes 2408456 | tf_op jit(solution)/shard_map/ppermute | solution.py:495
  69.6 15.7 %collective-permute-start.5 = (bf16[784,512]{1,0:T(8,128)(2,1)}, bf16[784,512]{1,0:T(8,128)(2,1)}, u32[]{:S(2)}, u32[]{:S(2)}) collective-permute-start(bf16[784,512]{1,0:T(8,128)(2,1)} %collective-permute-done.refs_3_), channel_id=1, source_target_pairs={{0,1},{1,2},{2,3},{3,0},{4,5},{5,6},{6,7},{7,4},{8,9},{9,10},{10,1... | collective-permute-start | bytes 2408456 | tf_op jit(solution)/shard_map/ppermute | solution.py:495
  71.8 0.9 copy-start.2
  81.4 12.2 %collective-permute-start.4 = (bf16[768,512]{1,0:T(8,128)(2,1)S(1)}, bf16[768,512]{1,0:T(8,128)(2,1)}, u32[]{:S(2)}, u32[]{:S(2)}) collective-permute-start(bf16[768,512]{1,0:T(8,128)(2,1)S(1)} %compact_rest.1.refs_0_.refs_2_.refs_4_.refs_3_), channel_id=1, source_target_pairs={{0,12},{1,13},{2,14},{3,15},{4,0},{5,1},{6,2},{7,3},{8,4},{9,5},{1... | collective-permute-start | bytes 2359304 | tf_op jit(solution)/shard_map/ppermute | solution.py:495
  82.0 19.6 %collective-permute-start.8 = (bf16[768,512]{1,0:T(8,128)(2,1)S(1)}, bf16[768,512]{1,0:T(8,128)(2,1)}, u32[]{:S(2)}, u32[]{:S(2)}) collective-permute-start(bf16[768,512]{1,0:T(8,128)(2,1)S(1)} %compact_rest.1.refs_0_.refs_2_.refs_4_.refs_3_), channel_id=1, source_target_pairs={{0,1},{1,2},{2,3},{3,0},{4,5},{5,6},{6,7},{7,4},{8,9},{9,10},{10,1... | collective-permute-start | bytes 2359304 | tf_op jit(solution)/shard_map/ppermute | solution.py:495
  83.6 19.8 %collective-permute-start.6 = (bf16[768,512]{1,0:T(8,128)(2,1)S(1)}, bf16[768,512]{1,0:T(8,128)(2,1)}, u32[]{:S(2)}, u32[]{:S(2)}) collective-permute-start(bf16[768,512]{1,0:T(8,128)(2,1)S(1)} %compact_rest.1.refs_0_.refs_2_.refs_4_.refs_3_), channel_id=1, source_target_pairs={{0,3},{1,0},{2,1},{3,2},{4,7},{5,4},{6,5},{7,6},{8,11},{9,8},{10,9... | collective-permute-start | bytes 2359304 | tf_op jit(solution)/shard_map/ppermute | solution.py:495
  87.3 16.0 %copy-start.3 = (bf16[784,512]{1,0:T(8,128)(2,1)S(1)}, bf16[784,512]{1,0:T(8,128)(2,1)}, u32[]{:S(2)}) copy-start(bf16[784,512]{1,0:T(8,128)(2,1)} %copy-done.2) | copy-start | bytes 2408452
  93.5 18.6 %collective-permute-start.7 = (bf16[768,512]{1,0:T(8,128)(2,1)}, bf16[768,512]{1,0:T(8,128)(2,1)S(1)}, u32[]{:S(2)}, u32[]{:S(2)}) collective-permute-start(bf16[768,512]{1,0:T(8,128)(2,1)} %collective-permute-done.4.refs_3_.refs_5_), channel_id=1, source_target_pairs={{0,12},{1,13},{2,14},{3,15},{4,0},{5,1},{6,2},{7,3},{8,4},{9,5},{1... | collective-permute-start | bytes 2359304 | tf_op jit(solution)/shard_map/ppermute | solution.py:495
  101.6 15.0 %collective-permute-start.9 = (bf16[768,512]{1,0:T(8,128)(2,1)}, bf16[768,512]{1,0:T(8,128)(2,1)S(1)}, u32[]{:S(2)}, u32[]{:S(2)}) collective-permute-start(bf16[768,512]{1,0:T(8,128)(2,1)} %collective-permute-done.8.refs_7_), channel_id=1, source_target_pairs={{0,1},{1,2},{2,3},{3,0},{4,5},{5,6},{6,7},{7,4},{8,9},{9,10},{10,1... | collective-permute-start | bytes 2359304 | tf_op jit(solution)/shard_map/ppermute | solution.py:495
  116.6 28.0 %copy-start = (s32[768]{0:T(1024)S(1)}, s32[768]{0:T(1024)}, u32[]{:S(2)}) copy-start(s32[768]{0:T(1024)} %lab_ref.5) | copy-start | bytes 9220
  116.6 28.0 %copy-start.1 = (s32[1,768]{1,0:T(1,128)S(1)}, s32[1,768]{1,0:T(1,128)}, u32[]{:S(2)}) copy-start(s32[1,768]{1,0:T(1,128)} %get-tuple-element.37.rank_ref) | copy-start | bytes 9220
  121.7 8.6 %collective-permute-start.11 = (f32[8,768]{1,0:T(8,128)S(1)}, f32[8,768]{1,0:T(8,128)S(1)}, u32[]{:S(2)}, u32[]{:S(2)}) collective-permute-start(f32[8,768]{1,0:T(8,128)S(1)} %get-tuple-element.65), channel_id=1, source_target_pairs={{0,8},{1,9},{2,10},{3,11},{4,12},{5,13},{6,14},{7,15},{8,0},{9,1},... | collective-permute-start | bytes 73736 | tf_op jit(solution)/shard_map/ppermute | solution.py:495
  124.4 5.9 %collective-permute-start.13 = (f32[8,768]{1,0:T(8,128)S(1)}, f32[8,768]{1,0:T(8,128)S(1)}, u32[]{:S(2)}, u32[]{:S(2)}) collective-permute-start(f32[8,768]{1,0:T(8,128)S(1)} %get-tuple-element.67), channel_id=1, source_target_pairs={{0,3},{1,0},{2,1},{3,2},{4,7},{5,4},{6,5},{7,6},{8,11},{9,8},{10,9... | collective-permute-start | bytes 73736 | tf_op jit(solution)/shard_map/ppermute | solution.py:495
  127.1 3.9 %collective-permute-start.10 = (f32[8,768]{1,0:T(8,128)S(1)}, f32[8,768]{1,0:T(8,128)S(1)}, u32[]{:S(2)}, u32[]{:S(2)}) collective-permute-start(f32[8,768]{1,0:T(8,128)S(1)} %get-tuple-element.62), channel_id=1, source_target_pairs={{0,4},{1,5},{2,6},{3,7},{4,8},{5,9},{6,10},{7,11},{8,12},{9,13},{1... | collective-permute-start | bytes 73736 | tf_op jit(solution)/shard_map/ppermute | solution.py:495
  129.4 5.3 %collective-permute-start.14 = (f32[8,768]{1,0:T(8,128)S(1)}, f32[8,768]{1,0:T(8,128)S(1)}, u32[]{:S(2)}, u32[]{:S(2)}) collective-permute-start(f32[8,768]{1,0:T(8,128)S(1)} %get-tuple-element.68), channel_id=1, source_target_pairs={{0,2},{1,3},{2,0},{3,1},{4,6},{5,7},{6,4},{7,5},{8,10},{9,11},{10,... | collective-permute-start | bytes 73736 | tf_op jit(solution)/shard_map/ppermute | solution.py:495
  129.4 5.3 %collective-permute-start.12 = (f32[8,768]{1,0:T(8,128)S(1)}, f32[8,768]{1,0:T(8,128)S(1)}, u32[]{:S(2)}, u32[]{:S(2)}) collective-permute-start(f32[8,768]{1,0:T(8,128)S(1)} %get-tuple-element.66), channel_id=1, source_target_pairs={{0,1},{1,2},{2,3},{3,0},{4,5},{5,6},{6,7},{7,4},{8,9},{9,10},{10,1... | collective-permute-start | bytes 73736 | tf_op jit(solution)/shard_map/ppermute | solution.py:495

commit v10 on v9

--- a/solution.py
+++ b/solution.py
@@ -305,7 +305,8 @@
     place = {b: i for i, b in enumerate(blocks)}
     lane = iota((1, 128), 1)
     empty = jnp.where(lane % 4 == 0, NEGATIVE, 0.0)
-    for i in range(n):
+    lefts = {place[l] for l, _, _ in plan} | {place[r] for _, r, axis in plan if axis is not None}
+    for i in lefts:
         rows[i] = jnp.broadcast_to(empty, (ROWS, 128))
     tops[...] = jnp.full((n, 8, ROWS), FLOOR, F32)
     totals[...] = jnp.zeros((n, 8, ROWS), F32)
@@ -317,7 +318,8 @@
             ready.add(i)
             one, many = spread_names(ins[i])
             names[i] = jnp.broadcast_to(one, (8, ROWS))
-            marks[i] = many
+            if i in lefts:
+                marks[i] = many
 
     steps = []
     for k, (left, right, axis) in enumerate(plan):

time: 147 us -> 147 us (level)
  no operation moved by 1% of the time
where the time goes in v10:
time: 147 us; the launch traced here: 146 us
  waiting for transfers between devices  60.8 us (41%)
  Pallas kernels  43.1 us (29%)
  starting transfers between devices  31.3 us (21%)
  blocking collectives  9.16 us (6%)
    ppermute x15, waiting for transfers between devices, shift(): return lax.ppermute(array, ('tr', 'tc'), moves)  31.5 us
    all_to_all x2, waiting for transfers between devices, exchange(): return lax.all_to_all(packed, 'tr', split_axis=0, concat_axis=0, tiled=True)  29.3 us
    ppermute x15, starting transfers between devices, shift(): return lax.ppermute(array, ('tr', 'tc'), moves)  21.6 us
    pallas_call x4, Pallas kernels, pairs(): pl.pallas_call(functools.partial(pair_kernel, plan, names, list(old)), ou...  21.6 us
    all_to_all x2, starting transfers between devices, exchange(): return lax.all_to_all(packed, 'tr', split_axis=0, concat_axis=0, tiled=True)  9.7 us
    all_to_all x1, blocking collectives, exchange(): return lax.all_to_all(packed, 'tr', split_axis=0, concat_axis=0, tiled=True)  9.16 us
    pallas_call x1, Pallas kernels, pack_first(): pl.pallas_call(pack_first_kernel, grid=(TILE_ROWS // AT_ONCE,), in_specs=...  6.44 us
    pallas_call x1, Pallas kernels, pack_rest(): pl.pallas_call(pack_rest_kernel, grid=(TILE_ROWS,), in_specs=[whole((ROWS...  6.09 us
  transfers between devices with their start and end apart: 17, of which 10 were waited for; matrix products, arithmetic and copies ran while one was open for 0% of the time, Pallas kernels for 20%

profile of v10, /device:TPU:2, one launch (start us, length us, event | category | flops | bytes accessed | tf_op | source)
XLA Modules:
  0.0 146.0 jit_solution(10400850550112887596)
XLA Ops:
  0.6 6.4 %pack_first.1 = (bf16[8,304,512]{2,1,0:T(8,128)(2,1)}, s32[1,768]{1,0:T(1,128)}, bf16[768,512]{1,0:T(8,128)(2,1)}) custom-call(bf16[768,1024]{1,0:T(8,128)(2,1)} %emb_ref.1, s32[768]{0:T(1024)} %lab_ref.5), custom_call_target="tpu_custom_call" | custom-call | tf_op jit(solution)/shard_map/pack_first/pallas_call | solution.py:103
  7.1 5.3 %all-to-all-start = ((bf16[8,304,512]{2,1,0:T(8,128)(2,1)}), bf16[8,304,512]{2,1,0:T(8,128)(2,1)S(1)}, u32[]{:S(2)}, u32[]{:S(2)}) async-start(bf16[8,304,512]{2,1,0:T(8,128)(2,1)} %get-tuple-element.38), calls=%async_computation | async-start | bytes 4980736 | tf_op jit(solution)/shard_map/all_to_all | solution.py:513
  12.4 6.1 %pack_rest.1 = bf16[8,288,512]{2,1,0:T(8,128)(2,1)} custom-call(bf16[768,512]{1,0:T(8,128)(2,1)} %get-tuple-element.36.unit_ref, s32[768]{0:T(1024)} %lab_ref.5, s32[1,768]{1,0:T(1,128)} %get-tuple-element.37.rank_ref), custom_call_target="tpu_custom_call" | custom-call | flops 1811939328 | bytes 2359296 | tf_op jit(solution)/shard_map/pack_rest/pallas_call | solution.py:130
  18.5 25.3 %all-to-all-done.got_ref = bf16[8,304,512]{2,1,0:T(8,128)(2,1)S(1)} async-done(((bf16[8,304,512]{2,1,0:T(8,128)(2,1)}), bf16[8,304,512]{2,1,0:T(8,128)(2,1)S(1)}, u32[]{:S(2)}, u32[]{:S(2)}) %all-to-all-start) | async-done | bytes 2490400 | tf_op jit(solution)/shard_map/all_to_all | solution.py:513
  43.8 4.4 %all-to-all-start.1 = ((bf16[8,288,512]{2,1,0:T(8,128)(2,1)}), bf16[8,288,512]{2,1,0:T(8,128)(2,1)}, u32[]{:S(2)}, u32[]{:S(2)}) async-start(bf16[8,288,512]{2,1,0:T(8,128)(2,1)} %pack_rest.1), calls=%async_computation.1 | async-start | bytes 4718592 | tf_op jit(solution)/shard_map/all_to_all | solution.py:513
  48.2 1.6 %compact_first.1 = (bf16[784,512]{1,0:T(8,128)(2,1)S(1)}, s32[16]{0:T(128)S(1)}) custom-call(bf16[8,304,512]{2,1,0:T(8,128)(2,1)S(1)} %all-to-all-done.got_ref), custom_call_target="tpu_custom_call" | custom-call | tf_op jit(solution)/shard_map/compact_first/pallas_call | solution.py:181
  49.8 0.6 collective-permute-start.2
  50.4 1.6 %collective-permute-start = (bf16[784,512]{1,0:T(8,128)(2,1)S(1)}, bf16[784,512]{1,0:T(8,128)(2,1)}, u32[]{:S(2)}, u32[]{:S(2)}) collective-permute-start(bf16[784,512]{1,0:T(8,128)(2,1)S(1)} %get-tuple-element.42.block.refs_0_), channel_id=1, source_target_pairs={{0,1},{1,2},{2,3},{3,0},{4,5},{5,6},{6,7},{7,4},{8,9},{9,10},{10,1... | collective-permute-start | bytes 2408456 | tf_op jit(solution)/shard_map/ppermute | solution.py:497
  52.0 1.7 %collective-permute-start.1 = (bf16[784,512]{1,0:T(8,128)(2,1)S(1)}, bf16[784,512]{1,0:T(8,128)(2,1)S(1)}, u32[]{:S(2)}, u32[]{:S(2)}) collective-permute-start(bf16[784,512]{1,0:T(8,128)(2,1)S(1)} %get-tuple-element.42.block.refs_0_), channel_id=1, source_target_pairs={{0,3},{1,0},{2,1},{3,2},{4,7},{5,4},{6,5},{7,6},{8,11},{9,8},{10,9... | collective-permute-start | bytes 2408456 | tf_op jit(solution)/shard_map/ppermute | solution.py:497
  53.7 8.4 %collective-permute-done.2.refs_1_.refs_0_ = bf16[784,512]{1,0:T(8,128)(2,1)S(1)} collective-permute-done((bf16[784,512]{1,0:T(8,128)(2,1)S(1)}, bf16[784,512]{1,0:T(8,128)(2,1)S(1)}, u32[]{:S(2)}, u32[]{:S(2)}) %collective-permute-start.2) | collective-permute-done | bytes 802848 | tf_op jit(solution)/shard_map/ppermute | solution.py:497
  62.0 0.8 collective-permute-start.3
  62.9 6.8 %collective-permute-done.refs_3_ = bf16[784,512]{1,0:T(8,128)(2,1)} collective-permute-done((bf16[784,512]{1,0:T(8,128)(2,1)S(1)}, bf16[784,512]{1,0:T(8,128)(2,1)}, u32[]{:S(2)}, u32[]{:S(2)}) %collective-permute-start) | collective-permute-done | bytes 802848 | tf_op jit(solution)/shard_map/ppermute | solution.py:497
  69.6 2.0 %collective-permute-start.5 = (bf16[784,512]{1,0:T(8,128)(2,1)}, bf16[784,512]{1,0:T(8,128)(2,1)}, u32[]{:S(2)}, u32[]{:S(2)}) collective-permute-start(bf16[784,512]{1,0:T(8,128)(2,1)} %collective-permute-done.refs_3_), channel_id=1, source_target_pairs={{0,1},{1,2},{2,3},{3,0},{4,5},{5,6},{6,7},{7,4},{8,9},{9,10},{10,1... | collective-permute-start | bytes 2408456 | tf_op jit(solution)/shard_map/ppermute | solution.py:497
  71.6 0.2 collective-permute-done.1.refs_2_.refs_1_
  71.8 0.0 copy-start.2
  71.8 0.9 copy-done.2
  72.7 1.5 %collective-permute-done.3.refs_2_.refs_1_ = bf16[784,512]{1,0:T(8,128)(2,1)S(1)} collective-permute-done((bf16[784,512]{1,0:T(8,128)(2,1)S(1)}, bf16[784,512]{1,0:T(8,128)(2,1)S(1)}, u32[]{:S(2)}, u32[]{:S(2)}) %collective-permute-start.3) | collective-permute-done | bytes 802848 | tf_op jit(solution)/shard_map/ppermute | solution.py:497
  74.2 4.0 %all-to-all-done.1.got_ref = bf16[8,288,512]{2,1,0:T(8,128)(2,1)} async-done(((bf16[8,288,512]{2,1,0:T(8,128)(2,1)}), bf16[8,288,512]{2,1,0:T(8,128)(2,1)}, u32[]{:S(2)}, u32[]{:S(2)}) %all-to-all-start.1) | async-done | bytes 2359328 | tf_op jit(solution)/shard_map/all_to_all | solution.py:513
  78.2 3.2 %compact_rest.1.refs_0_.refs_2_.refs_4_.refs_3_ = bf16[768,512]{1,0:T(8,128)(2,1)S(1)} custom-call(s32[16]{0:T(128)S(1)} %get-tuple-element.40.place_ref.offset_ref, bf16[8,288,512]{2,1,0:T(8,128)(2,1)} %all-to-all-done.1.got_ref), custom_call_target="tpu_custom_call" | custom-call | tf_op jit(solution)/shard_map/compact_rest/pallas_call | solution.py:203
  81.4 0.6 collective-permute-start.4
  82.0 1.6 %collective-permute-start.8 = (bf16[768,512]{1,0:T(8,128)(2,1)S(1)}, bf16[768,512]{1,0:T(8,128)(2,1)}, u32[]{:S(2)}, u32[]{:S(2)}) collective-permute-start(bf16[768,512]{1,0:T(8,128)(2,1)S(1)} %compact_rest.1.refs_0_.refs_2_.refs_4_.refs_3_), channel_id=1, source_target_pairs={{0,1},{1,2},{2,3},{3,0},{4,5},{5,6},{6,7},{7,4},{8,9},{9,10},{10,1... | collective-permute-start | bytes 2359304 | tf_op jit(solution)/shard_map/ppermute | solution.py:497
  83.6 1.7 %collective-permute-start.6 = (bf16[768,512]{1,0:T(8,128)(2,1)S(1)}, bf16[768,512]{1,0:T(8,128)(2,1)}, u32[]{:S(2)}, u32[]{:S(2)}) collective-permute-start(bf16[768,512]{1,0:T(8,128)(2,1)S(1)} %compact_rest.1.refs_0_.refs_2_.refs_4_.refs_3_), channel_id=1, source_target_pairs={{0,3},{1,0},{2,1},{3,2},{4,7},{5,4},{6,5},{7,6},{8,11},{9,8},{10,9... | collective-permute-start | bytes 2359304 | tf_op jit(solution)/shard_map/ppermute | solution.py:497
  85.2 0.1 pad_add_fusion.half_ref
  85.3 0.0 collective-permute-done.5.refs_2_
  85.3 2.0 %own.1.refs_4_ = f32[8,768]{1,0:T(8,128)S(1)} custom-call(bf16[784,512]{1,0:T(8,128)(2,1)S(1)} %get-tuple-element.42.block.refs_0_, bf16[768,512]{1,0:T(8,128)(2,1)S(1)} %compact_rest.1.refs_0_.refs_2_.refs_4_.refs_3_), custom_call_target="tpu_custom_call" | custom-call | flops 1207959552 | bytes 1605632 | tf_op jit(solution)/shard_map/own/pallas_call | solution.py:281
  87.3 0.0 copy-start.3
  87.3 6.2 %collective-permute-done.4.refs_3_.refs_5_ = bf16[768,512]{1,0:T(8,128)(2,1)} collective-permute-done((bf16[768,512]{1,0:T(8,128)(2,1)S(1)}, bf16[768,512]{1,0:T(8,128)(2,1)}, u32[]{:S(2)}, u32[]{:S(2)}) %collective-permute-start.4) | collective-permute-done | bytes 786464 | tf_op jit(solution)/shard_map/ppermute | solution.py:497
  93.5 0.7 collective-permute-start.7
  94.3 3.4 %pairs.4 = (f32[8,768]{1,0:T(8,128)S(1)}, f32[8,768]{1,0:T(8,128)S(1)}) custom-call(s32[2]{0:T(128)S(1)} %pad_add_fusion.half_ref, bf16[784,512]{1,0:T(8,128)(2,1)S(1)} %get-tuple-element.42.block.refs_0_, bf16[784,512]{1,0:T(8,128)(2,1)S(1)} %collective-permute-done.2.refs_1_.refs_0_, bf16[768,512]{1,0:T(8,128)(2,1)S(1)} %compact_rest.1.refs_0_.refs_2_.refs_4_.refs_3_, ...), custom_call_target="tpu_custom_call" | custom-call | flops 1207959552 | bytes 3211264 | tf_op jit(solution)/shard_map/pairs/pallas_call | solution.py:405
  97.7 3.9 %collective-permute-done.8.refs_7_ = bf16[768,512]{1,0:T(8,128)(2,1)} collective-permute-done((bf16[768,512]{1,0:T(8,128)(2,1)S(1)}, bf16[768,512]{1,0:T(8,128)(2,1)}, u32[]{:S(2)}, u32[]{:S(2)}) %collective-permute-start.8) | collective-permute-done | bytes 786464 | tf_op jit(solution)/shard_map/ppermute | solution.py:497
  101.6 1.8 %collective-permute-start.9 = (bf16[768,512]{1,0:T(8,128)(2,1)}, bf16[768,512]{1,0:T(8,128)(2,1)S(1)}, u32[]{:S(2)}, u32[]{:S(2)}) collective-permute-start(bf16[768,512]{1,0:T(8,128)(2,1)} %collective-permute-done.8.refs_7_), channel_id=1, source_target_pairs={{0,1},{1,2},{2,3},{3,0},{4,5},{5,6},{6,7},{7,4},{8,9},{9,10},{10,1... | collective-permute-start | bytes 2359304 | tf_op jit(solution)/shard_map/ppermute | solution.py:497
  103.3 0.0 collective-permute-done.6.refs_6_.refs_4_
  103.3 0.0 copy-done.3
  103.3 8.8 %pairs.5 = (f32[8,768]{1,0:T(8,128)S(1)}, f32[8,768]{1,0:T(8,128)S(1)}, f32[8,768]{1,0:T(8,128)S(1)}, f32[8,768]{1,0:T(8,128)S(1)}) custom-call(s32[2]{0:T(128)S(1)} %pad_add_fusion.half_ref, bf16[784,512]{1,0:T(8,128)(2,1)S(1)} %get-tuple-element.42.block.refs_0_, bf16[784,512]{1,0:T(8,128)(2,1)S(1)} %collective-permute-done.2.refs_1_.refs_0_, ...), custom_call_target="tpu_custom_call" | custom-call | flops 4227858432 | bytes 6422528 | tf_op jit(solution)/shard_map/pairs/pallas_call | solution.py:405
  112.1 0.0 collective-permute-done.7.refs_5_.refs_4_
  112.1 4.4 %pairs.6 = (f32[8,768]{1,0:T(8,128)S(1)}, f32[8,768]{1,0:T(8,128)S(1)}, f32[8,768]{1,0:T(8,128)S(1)}) custom-call(s32[2]{0:T(128)S(1)} %pad_add_fusion.half_ref, bf16[784,512]{1,0:T(8,128)(2,1)S(1)} %get-tuple-element.42.block.refs_0_, bf16[784,512]{1,0:T(8,128)(2,1)S(1)} %copy-done.3, bf16[784,512]{1,0:T(8,128)(2,1)S(1)} %collective-permute-done.3.refs_2_.refs_1_, ...), custom_call_target="tpu_custom_call" | custom-call | flops 1811939328 | bytes 4816896 | tf_op jit(solution)/shard_map/pairs/pallas_call | solution.py:405
  116.6 0.0 collective-permute-done.9.refs_5_
  116.6 0.0 copy-start
  116.6 0.0 copy-start.1
  116.6 5.0 %pairs.7 = (f32[8,768]{1,0:T(8,128)S(1)}, f32[8,768]{1,0:T(8,128)S(1)}, f32[8,768]{1,0:T(8,128)S(1)}) custom-call(s32[2]{0:T(128)S(1)} %pad_add_fusion.half_ref, bf16[784,512]{1,0:T(8,128)(2,1)S(1)} %collective-permute-done.2.refs_1_.refs_0_, bf16[784,512]{1,0:T(8,128)(2,1)S(1)} %collective-permute-done.3.refs_2_.refs_1_, ...), custom_call_target="tpu_custom_call" | custom-call | flops 1811939328 | bytes 4816896 | tf_op jit(solution)/shard_map/pairs/pallas_call | solution.py:405
  121.6 2.7 %collective-permute-start.11 = (f32[8,768]{1,0:T(8,128)S(1)}, f32[8,768]{1,0:T(8,128)S(1)}, u32[]{:S(2)}, u32[]{:S(2)}) collective-permute-start(f32[8,768]{1,0:T(8,128)S(1)} %get-tuple-element.65), channel_id=1, source_target_pairs={{0,8},{1,9},{2,10},{3,11},{4,12},{5,13},{6,14},{7,15},{8,0},{9,1},... | collective-permute-start | bytes 73736 | tf_op jit(solution)/shard_map/ppermute | solution.py:497
  124.3 2.6 %collective-permute-start.13 = (f32[8,768]{1,0:T(8,128)S(1)}, f32[8,768]{1,0:T(8,128)S(1)}, u32[]{:S(2)}, u32[]{:S(2)}) collective-permute-start(f32[8,768]{1,0:T(8,128)S(1)} %get-tuple-element.67), channel_id=1, source_target_pairs={{0,3},{1,0},{2,1},{3,2},{4,7},{5,4},{6,5},{7,6},{8,11},{9,8},{10,9... | collective-permute-start | bytes 73736 | tf_op jit(solution)/shard_map/ppermute | solution.py:497
  126.9 2.4 %collective-permute-start.10 = (f32[8,768]{1,0:T(8,128)S(1)}, f32[8,768]{1,0:T(8,128)S(1)}, u32[]{:S(2)}, u32[]{:S(2)}) collective-permute-start(f32[8,768]{1,0:T(8,128)S(1)} %get-tuple-element.62), channel_id=1, source_target_pairs={{0,4},{1,5},{2,6},{3,7},{4,8},{5,9},{6,10},{7,11},{8,12},{9,13},{1... | collective-permute-start | bytes 73736 | tf_op jit(solution)/shard_map/ppermute | solution.py:497
  129.3 0.0 collective-permute-start.14
  129.3 0.9 collective-permute-start.12
  130.2 0.0 collective-permute-done.11.refs_2_
  130.2 0.0 collective-permute-done.13.refs_4_
  130.2 0.7 collective-permute-done.10.refs_1_
  130.9 3.8 %collective-permute-done.14.refs_5_ = f32[8,768]{1,0:T(8,128)S(1)} collective-permute-done((f32[8,768]{1,0:T(8,128)S(1)}, f32[8,768]{1,0:T(8,128)S(1)}, u32[]{:S(2)}, u32[]{:S(2)}) %collective-permute-start.14) | collective-permute-done | bytes 24608 | tf_op jit(solution)/shard_map/ppermute | solution.py:497
  134.7 0.0 collective-permute-done.12.refs_3_
  134.7 0.7 spread.1
  135.4 9.2 %all_to_all.15.back_ref = f32[8,8,128]{2,1,0:T(8,128)S(1)} all-to-all(f32[8,8,128]{2,1,0:T(8,128)S(1)} %spread.1), channel_id=1, replica_groups=mesh['tr'=8,'tc'=16] {'tr'}, dimensions={0} | all-to-all | bytes 65536 | tf_op jit(solution)/shard_map/all_to_all | solution.py:513
  144.5 0.0 copy-done
  144.5 0.0 copy-done.1
  144.5 1.5 %unpack.1 = (f32[768]{0:T(1024)}, f32[768]{0:T(1024)}, f32[768]{0:T(1024)}) custom-call(f32[8,8,128]{2,1,0:T(8,128)S(1)} %all_to_all.15.back_ref, s32[768]{0:T(1024)S(1)} %copy-done, s32[1,768]{1,0:T(1,128)S(1)} %copy-done.1), custom_call_target="tpu_custom_call" | custom-call | tf_op jit(solution)/shard_map/unpack/pallas_call | solution.py:478
Async XLA Ops:
  7.1 36.7 %all-to-all-start = ((bf16[8,304,512]{2,1,0:T(8,128)(2,1)}), bf16[8,304,512]{2,1,0:T(8,128)(2,1)S(1)}, u32[]{:S(2)}, u32[]{:S(2)}) async-start(bf16[8,304,512]{2,1,0:T(8,128)(2,1)} %get-tuple-element.38), calls=%async_computation | async-start | bytes 4980736 | tf_op jit(solution)/shard_map/all_to_all | solution.py:513
  43.8 34.4 %all-to-all-start.1 = ((bf16[8,288,512]{2,1,0:T(8,128)(2,1)}), bf16[8,288,512]{2,1,0:T(8,128)(2,1)}, u32[]{:S(2)}, u32[]{:S(2)}) async-start(bf16[8,288,512]{2,1,0:T(8,128)(2,1)} %pack_rest.1), calls=%async_computation.1 | async-start | bytes 4718592 | tf_op jit(solution)/shard_map/all_to_all | solution.py:513
  49.8 12.2 %collective-permute-start.2 = (bf16[784,512]{1,0:T(8,128)(2,1)S(1)}, bf16[784,512]{1,0:T(8,128)(2,1)S(1)}, u32[]{:S(2)}, u32[]{:S(2)}) collective-permute-start(bf16[784,512]{1,0:T(8,128)(2,1)S(1)} %get-tuple-element.42.block.refs_0_), channel_id=1, source_target_pairs={{0,12},{1,13},{2,14},{3,15},{4,0},{5,1},{6,2},{7,3},{8,4},{9,5},{1... | collective-permute-start | bytes 2408456 | tf_op jit(solution)/shard_map/ppermute | solution.py:497
  50.4 19.2 %collective-permute-start = (bf16[784,512]{1,0:T(8,128)(2,1)S(1)}, bf16[784,512]{1,0:T(8,128)(2,1)}, u32[]{:S(2)}, u32[]{:S(2)}) collective-permute-start(bf16[784,512]{1,0:T(8,128)(2,1)S(1)} %get-tuple-element.42.block.refs_0_), channel_id=1, source_target_pairs={{0,1},{1,2},{2,3},{3,0},{4,5},{5,6},{6,7},{7,4},{8,9},{9,10},{10,1... | collective-permute-start | bytes 2408456 | tf_op jit(solution)/shard_map/ppermute | solution.py:497
  52.0 19.8 %collective-permute-start.1 = (bf16[784,512]{1,0:T(8,128)(2,1)S(1)}, bf16[784,512]{1,0:T(8,128)(2,1)S(1)}, u32[]{:S(2)}, u32[]{:S(2)}) collective-permute-start(bf16[784,512]{1,0:T(8,128)(2,1)S(1)} %get-tuple-element.42.block.refs_0_), channel_id=1, source_target_pairs={{0,3},{1,0},{2,1},{3,2},{4,7},{5,4},{6,5},{7,6},{8,11},{9,8},{10,9... | collective-permute-start | bytes 2408456 | tf_op jit(solution)/shard_map/ppermute | solution.py:497
  62.0 12.2 %collective-permute-start.3 = (bf16[784,512]{1,0:T(8,128)(2,1)S(1)}, bf16[784,512]{1,0:T(8,128)(2,1)S(1)}, u32[]{:S(2)}, u32[]{:S(2)}) collective-permute-start(bf16[784,512]{1,0:T(8,128)(2,1)S(1)} %collective-permute-done.2.refs_1_.refs_0_), channel_id=1, source_target_pairs={{0,12},{1,13},{2,14},{3,15},{4,0},{5,1},{6,2},{7,3},{8,4},{9,5},{1... | collective-permute-start | bytes 2408456 | tf_op jit(solution)/shard_map/ppermute | solution.py:497
  69.6 15.7 %collective-permute-start.5 = (bf16[784,512]{1,0:T(8,128)(2,1)}, bf16[784,512]{1,0:T(8,128)(2,1)}, u32[]{:S(2)}, u32[]{:S(2)}) collective-permute-start(bf16[784,512]{1,0:T(8,128)(2,1)} %collective-permute-done.refs_3_), channel_id=1, source_target_pairs={{0,1},{1,2},{2,3},{3,0},{4,5},{5,6},{6,7},{7,4},{8,9},{9,10},{10,1... | collective-permute-start | bytes 2408456 | tf_op jit(solution)/shard_map/ppermute | solution.py:497
  71.8 0.9 copy-start.2
  81.4 12.2 %collective-permute-start.4 = (bf16[768,512]{1,0:T(8,128)(2,1)S(1)}, bf16[768,512]{1,0:T(8,128)(2,1)}, u32[]{:S(2)}, u32[]{:S(2)}) collective-permute-start(bf16[768,512]{1,0:T(8,128)(2,1)S(1)} %compact_rest.1.refs_0_.refs_2_.refs_4_.refs_3_), channel_id=1, source_target_pairs={{0,12},{1,13},{2,14},{3,15},{4,0},{5,1},{6,2},{7,3},{8,4},{9,5},{1... | collective-permute-start | bytes 2359304 | tf_op jit(solution)/shard_map/ppermute | solution.py:497
  82.0 19.6 %collective-permute-start.8 = (bf16[768,512]{1,0:T(8,128)(2,1)S(1)}, bf16[768,512]{1,0:T(8,128)(2,1)}, u32[]{:S(2)}, u32[]{:S(2)}) collective-permute-start(bf16[768,512]{1,0:T(8,128)(2,1)S(1)} %compact_rest.1.refs_0_.refs_2_.refs_4_.refs_3_), channel_id=1, source_target_pairs={{0,1},{1,2},{2,3},{3,0},{4,5},{5,6},{6,7},{7,4},{8,9},{9,10},{10,1... | collective-permute-start | bytes 2359304 | tf_op jit(solution)/shard_map/ppermute | solution.py:497
  83.6 19.8 %collective-permute-start.6 = (bf16[768,512]{1,0:T(8,128)(2,1)S(1)}, bf16[768,512]{1,0:T(8,128)(2,1)}, u32[]{:S(2)}, u32[]{:S(2)}) collective-permute-start(bf16[768,512]{1,0:T(8,128)(2,1)S(1)} %compact_rest.1.refs_0_.refs_2_.refs_4_.refs_3_), channel_id=1, source_target_pairs={{0,3},{1,0},{2,1},{3,2},{4,7},{5,4},{6,5},{7,6},{8,11},{9,8},{10,9... | collective-permute-start | bytes 2359304 | tf_op jit(solution)/shard_map/ppermute | solution.py:497
  87.3 16.0 %copy-start.3 = (bf16[784,512]{1,0:T(8,128)(2,1)S(1)}, bf16[784,512]{1,0:T(8,128)(2,1)}, u32[]{:S(2)}) copy-start(bf16[784,512]{1,0:T(8,128)(2,1)} %copy-done.2) | copy-start | bytes 2408452
  93.5 18.6 %collective-permute-start.7 = (bf16[768,512]{1,0:T(8,128)(2,1)}, bf16[768,512]{1,0:T(8,128)(2,1)S(1)}, u32[]{:S(2)}, u32[]{:S(2)}) collective-permute-start(bf16[768,512]{1,0:T(8,128)(2,1)} %collective-permute-done.4.refs_3_.refs_5_), channel_id=1, source_target_pairs={{0,12},{1,13},{2,14},{3,15},{4,0},{5,1},{6,2},{7,3},{8,4},{9,5},{1... | collective-permute-start | bytes 2359304 | tf_op jit(solution)/shard_map/ppermute | solution.py:497
  101.6 15.0 %collective-permute-start.9 = (bf16[768,512]{1,0:T(8,128)(2,1)}, bf16[768,512]{1,0:T(8,128)(2,1)S(1)}, u32[]{:S(2)}, u32[]{:S(2)}) collective-permute-start(bf16[768,512]{1,0:T(8,128)(2,1)} %collective-permute-done.8.refs_7_), channel_id=1, source_target_pairs={{0,1},{1,2},{2,3},{3,0},{4,5},{5,6},{6,7},{7,4},{8,9},{9,10},{10,1... | collective-permute-start | bytes 2359304 | tf_op jit(solution)/shard_map/ppermute | solution.py:497
  116.6 28.0 %copy-start = (s32[768]{0:T(1024)S(1)}, s32[768]{0:T(1024)}, u32[]{:S(2)}) copy-start(s32[768]{0:T(1024)} %lab_ref.5) | copy-start | bytes 9220
  116.6 28.0 %copy-start.1 = (s32[1,768]{1,0:T(1,128)S(1)}, s32[1,768]{1,0:T(1,128)}, u32[]{:S(2)}) copy-start(s32[1,768]{1,0:T(1,128)} %get-tuple-element.37.rank_ref) | copy-start | bytes 9220
  121.6 8.6 %collective-permute-start.11 = (f32[8,768]{1,0:T(8,128)S(1)}, f32[8,768]{1,0:T(8,128)S(1)}, u32[]{:S(2)}, u32[]{:S(2)}) collective-permute-start(f32[8,768]{1,0:T(8,128)S(1)} %get-tuple-element.65), channel_id=1, source_target_pairs={{0,8},{1,9},{2,10},{3,11},{4,12},{5,13},{6,14},{7,15},{8,0},{9,1},... | collective-permute-start | bytes 73736 | tf_op jit(solution)/shard_map/ppermute | solution.py:497
  124.3 5.9 %collective-permute-start.13 = (f32[8,768]{1,0:T(8,128)S(1)}, f32[8,768]{1,0:T(8,128)S(1)}, u32[]{:S(2)}, u32[]{:S(2)}) collective-permute-start(f32[8,768]{1,0:T(8,128)S(1)} %get-tuple-element.67), channel_id=1, source_target_pairs={{0,3},{1,0},{2,1},{3,2},{4,7},{5,4},{6,5},{7,6},{8,11},{9,8},{10,9... | collective-permute-start | bytes 73736 | tf_op jit(solution)/shard_map/ppermute | solution.py:497
  126.9 3.9 %collective-permute-start.10 = (f32[8,768]{1,0:T(8,128)S(1)}, f32[8,768]{1,0:T(8,128)S(1)}, u32[]{:S(2)}, u32[]{:S(2)}) collective-permute-start(f32[8,768]{1,0:T(8,128)S(1)} %get-tuple-element.62), channel_id=1, source_target_pairs={{0,4},{1,5},{2,6},{3,7},{4,8},{5,9},{6,10},{7,11},{8,12},{9,13},{1... | collective-permute-start | bytes 73736 | tf_op jit(solution)/shard_map/ppermute | solution.py:497
  129.3 5.3 %collective-permute-start.14 = (f32[8,768]{1,0:T(8,128)S(1)}, f32[8,768]{1,0:T(8,128)S(1)}, u32[]{:S(2)}, u32[]{:S(2)}) collective-permute-start(f32[8,768]{1,0:T(8,128)S(1)} %get-tuple-element.68), channel_id=1, source_target_pairs={{0,2},{1,3},{2,0},{3,1},{4,6},{5,7},{6,4},{7,5},{8,10},{9,11},{10,... | collective-permute-start | bytes 73736 | tf_op jit(solution)/shard_map/ppermute | solution.py:497
  129.3 5.3 %collective-permute-start.12 = (f32[8,768]{1,0:T(8,128)S(1)}, f32[8,768]{1,0:T(8,128)S(1)}, u32[]{:S(2)}, u32[]{:S(2)}) collective-permute-start(f32[8,768]{1,0:T(8,128)S(1)} %get-tuple-element.66), channel_id=1, source_target_pairs={{0,1},{1,2},{2,3},{3,0},{4,5},{5,6},{6,7},{7,4},{8,9},{9,10},{10,1... | collective-permute-start | bytes 73736 | tf_op jit(solution)/shard_map/ppermute | solution.py:497
